TPU v7x, 32 devices: a whole 2x2x4 slice. The times are simulated.
32 devices in a mesh: dom: 16 (over z, y, core), col: 2 (over x).
Axes of the slice: x: 2, y: 2, z: 4, core: 2. Of those that a mesh axis runs over, the one named last changes fastest.
Arguments:
- features: bfloat16 [128, 4096], P('col', 'dom'), may hold values from -6 to 6
- cached_embed: bfloat16 [128, 4096], P('col'), may hold values from -6 to 6
- staleness: int32 [16], replicated, may hold values from 0 to 15, as said below
- node_counts: int32 [16], replicated, may hold values from 64 to 256, as said below
- neighbours: int32 [16, 4096], P(None, 'dom'), may hold values from 0 to 4095, as said below
- degrees: int32 [4096], P('dom'), may hold values from 1 to 16
- w_self: bfloat16 [128, 256], P('col'), may hold values from -0.5 to 0.5
- w_nbr: bfloat16 [128, 256], P('col'), may hold values from -0.5 to 0.5
- sage_bias: float32 [256], P('col'), may hold values from -3 to 3
- cotangent: bfloat16 [256, 4096], P('col', 'dom'), may hold values from -6 to 6
Outputs:
- activation: bfloat16 [256, 4096], P('col', 'dom')
- grad_feat: bfloat16 [128, 4096], P('col', 'dom')
- grad_self: float32 [128, 256], P('col')
- grad_nbr: float32 [128, 256], P('col')
- grad_bias: float32 [256], P('col')
Inputs may be any that keep to these rules, and one draw needn't show every extreme that they name: Exactly 4 partitions have staleness of 8 or more. `node_counts`: some partition has all 256 node slots live. `neighbours`: every neighbour slot names a live node slot; about half lie in the node's own partition.
All inputs are finite; a program needn't handle non-finite values.
Results may differ from a plain program's by a relative error of at most 0.015.
Values may be sent and summed in bfloat16 or wider, within the bound.
No kernel may reach another device: no remote copies, remote signals or barrier semaphores. Data moves between devices by JAX's collectives and lax.ppermute only.
A program may use at most 64 MiB of HBM per device.

v0:
```python
import jax
import jax.numpy as jnp
from jax import lax
from jax.sharding import PartitionSpec as P

LIMIT = 8


def left_product(weight, data):
    return lax.dot_general(
        weight, data, (((0,), (0,)), ((), ())), preferred_element_type=jnp.float32
    )


def right_product(data, grads):
    return lax.dot_general(
        data, grads, (((1,), (1,)), ((), ())), preferred_element_type=jnp.float32
    )


def per_device(
    features,
    cached_embed,
    staleness,
    node_counts,
    neighbours,
    degrees,
    w_self,
    w_nbr,
    sage_bias,
    cotangent,
):
    col_width = features.shape[0]
    part_rows = features.shape[1]
    slot_count = neighbours.shape[0]
    my_index = lax.axis_index("dom")
    fresh_flag = (staleness >= LIMIT).astype(jnp.int32)
    my_fresh = fresh_flag[my_index]
    own_cache = lax.dynamic_slice_in_dim(cached_embed, my_index * part_rows, part_rows, 1)
    own_source = jnp.where(my_fresh == 1, features, own_cache)
    sources = lax.all_gather(own_source, "dom", axis=1, tiled=True)
    local_slot = jnp.arange(part_rows, dtype=jnp.int32)
    live_rows = (local_slot < node_counts[my_index]).astype(jnp.float32)
    slot_index = jnp.arange(slot_count, dtype=jnp.int32)
    used = (slot_index[:, None] < degrees[None, :]).astype(jnp.float32)
    weights = used * (live_rows / degrees.astype(jnp.float32))[None, :]
    gathered = sources[:, neighbours].astype(jnp.float32)
    aggregated = jnp.sum(weights[None, :, :] * gathered, axis=1).astype(jnp.bfloat16)
    partial_pre = left_product(w_self, features) + left_product(w_nbr, aggregated)
    pre_act = (
        lax.psum_scatter(
            partial_pre.astype(jnp.bfloat16), "col", scatter_dimension=0, tiled=True
        ).astype(jnp.float32)
        + sage_bias[:, None]
    )
    sigmoid = 1.0 / (1.0 + jnp.exp(-pre_act))
    activation = (live_rows[None, :] * pre_act * sigmoid).astype(jnp.bfloat16)
    grad_pre = (
        live_rows[None, :]
        * cotangent.astype(jnp.float32)
        * sigmoid
        * (1.0 + pre_act * (1.0 - sigmoid))
    ).astype(jnp.bfloat16)
    grad_full = lax.all_gather(grad_pre, "col", axis=0, tiled=True)
    self_part = right_product(features, grad_full)
    nbr_part = right_product(aggregated, grad_full)
    bias_part = jnp.sum(grad_pre.astype(jnp.float32), axis=1)
    grad_self, grad_nbr, grad_bias = lax.psum((self_part, nbr_part, bias_part), "dom")
    grad_agg = jnp.dot(w_nbr, grad_full, preferred_element_type=jnp.float32).astype(jnp.bfloat16)
    own_term = jnp.dot(w_self, grad_full, preferred_element_type=jnp.float32)
    spread = weights[None, :, :] * grad_agg.astype(jnp.float32)[:, None, :]
    total_rows = cached_embed.shape[1]
    contrib = (
        jnp.zeros((col_width, total_rows), jnp.float32)
        .at[:, neighbours.reshape(-1)]
        .add(spread.reshape(col_width, -1))
    )
    part_total = lax.axis_size("dom")
    listed_total = part_total // 4
    listed_order = jnp.argsort(1 - fresh_flag, stable=True)[:listed_total]
    blocks = contrib.reshape(col_width, part_total, part_rows)
    kept = jnp.take(blocks, listed_order, axis=1)
    summed = lax.psum(kept, "dom")
    part_ids = jnp.arange(part_total, dtype=jnp.int32)
    my_rank = jnp.sum(jnp.where(part_ids < my_index, fresh_flag, 0))
    my_rank = jnp.minimum(my_rank, listed_total - 1)
    back = lax.dynamic_index_in_dim(summed, my_rank, 1, keepdims=False)
    grad_feat = (own_term + my_fresh.astype(jnp.float32) * back).astype(jnp.bfloat16)
    return (activation, grad_feat, grad_self, grad_nbr, grad_bias)


def solution(mesh):
    placed = (
        P("col", "dom"),
        P("col", None),
        P(),
        P(),
        P(None, "dom"),
        P("dom"),
        P("col", None),
        P("col", None),
        P("col"),
        P("col", "dom"),
    )
    return jax.shard_map(
        per_device,
        mesh=mesh,
        in_specs=placed,
        out_specs=(P("col", "dom"), P("col", "dom"), P("col", None), P("col", None), P("col")),
        check_vma=False,
    )
```

profile of v0, /device:TPU:0, one launch (start us, length us, event | category | flops | bytes accessed | tf_op | source)
XLA Modules:
  0.0 202.1 jit_solution(14441748542579441865)
XLA Ops:
  7.2 0.0 copy-start
  7.2 0.0 reduce-scatter.2.cloned.1.call-start
  7.2 1.0 copy-done
  8.2 0.1 copy.25
  8.3 0.7 compare_convert_fusion
  9.0 0.9 copy.20
  9.9 0.6 dynamic_slice.14
  11.1 26.2 %all_gather.6 = bf16[64,4096]{0,1:T(8,128)(2,1)S(1)} all-gather(bf16[64,256]{0,1:T(8,128)(2,1)S(1)} %broadcast_select_fusion), channel_id=1, replica_groups=mesh['dom'=16,'col'=2] {'dom'}, dimensions={1}, use_global_device_ids=true | all-gather | bytes 557056 | tf_op jit(solution)/shard_map/all_gather | solution.py:41
  37.4 0.7 fusion.12
  38.1 1.2 dynamic_slice.13
  39.4 1.3 convert_divide_fusion
  40.7 0.7 fusion.14
  41.4 0.0 copy-start.3
  41.4 0.0 copy-start.1
  41.4 0.0 copy-start.2
  41.4 0.0 copy-start.7
  41.4 12.1 %gather_fusion = bf16[4096,64]{1,0:T(8,128)(2,1)S(1)} fusion(bf16[64,4096]{0,1:T(8,128)(2,1)S(1)} %all_gather.6, s32[4096]{0:T(1024)S(1)} %broadcast_clamp_fusion), kind=kCustom, calls=%fused_computation | custom fusion | bytes 1064960 | tf_op jit(solution)/shard_map/gather | solution.py:47
  53.6 0.0 copy-start.4
  53.6 0.0 copy-start.5
  53.6 0.0 copy-start.6
  53.6 0.7 fusion
  54.3 0.0 copy-done.3
  54.3 0.2 convolution_bitcast_fusion
  54.6 0.0 copy-done.1
  54.6 0.0 copy-done.2
  54.6 0.9 fusion.3
  55.4 0.0 reduce-scatter.2.cloned.1.call-update
  55.4 0.0 all-reduce.3.cloned.1.call-start
  55.5 0.0 copy-done.7
  55.5 0.6 fusion.15
  56.1 0.0 copy-done.4
  56.2 1.2 sort.17
  57.5 0.7 compare_convert_fusion.1
  58.1 5.0 %reduce-scatter.2.cloned.1.call-done = bf16[128,256]{1,0:T(8,128)(2,1)} async-done(((bf16[256,256]{1,0:T(8,128)(2,1)}), bf16[128,256]{1,0:T(8,128)(2,1)}) %reduce-scatter.2.cloned.1.call-update) | async-done | bytes 65552 | tf_op jit(solution)/shard_map/reduce_scatter | solution.py:51
  63.2 0.0 copy-done.5
  63.2 0.0 copy-done.6
  63.2 1.6 convert_reduce_fusion
  64.8 4.9 %all_gather.7 = bf16[256,256]{1,0:T(8,128)(2,1)S(1)} all-gather(bf16[128,256]{1,0:T(8,128)(2,1)S(1)} %get-tuple-element.11), channel_id=1, replica_groups=mesh['dom'=16,'col'=2] {'col'}, dimensions={0}, use_global_device_ids=true | all-gather | bytes 196608 | tf_op jit(solution)/shard_map/all_gather | solution.py:64
  69.7 0.8 fusion.16
  70.5 0.1 fusion.7
  70.7 0.8 convolution_bitcast_fusion.2
  71.5 0.1 copy.22
  71.6 0.6 bitcast_multiply_fusion
  72.2 23.8 %scatter_custom_fusion = f32[64,4096]{0,1:T(8,128)} fusion(s32[4096]{0:T(1024)S(1)} %bitcast.56, f32[64,4096]{0,1:T(8,128)S(1)} %bitcast_multiply_fusion, f32[]{:T(128)} %constant.19.clone.1), kind=kCustom, calls=%fused_computation.5 | custom fusion | flops 262144 | bytes 3145732 | tf_op jit(solution)/shard_map/scatter-add | solution.py:76
  96.0 2.2 %copy.23 = f32[64,16,256]{2,0,1:T(8,128)S(1)} copy(f32[64,16,256]{0,2,1:T(8,128)} %bitcast.50) | data formatting | bytes 2097152 | tf_op jit(solution)/shard_map/reshape | solution.py:81
  98.2 0.6 gather_fusion.1
  98.8 0.8 select_bitcast_fusion
  99.6 0.0 all-reduce.3.cloned.1.call-update
  100.9 32.5 %psum.31 = f32[128]{0:T(128)} all-reduce(f32[128]{0:T(128)S(1)} %get-tuple-element.10), channel_id=1, replica_groups=mesh['dom'=16,'col'=2] {'dom'}, use_global_device_ids=true, to_apply=%region_9.10 | all-reduce | flops 128 | bytes 1024 | tf_op jit(solution)/shard_map/psum | solution.py:68
  133.4 57.3 %all-reduce.3.cloned.1.call-done = (f32[64,4,256]{2,0,1:T(8,128)}, f32[64,256]{1,0:T(8,128)}, f32[64,256]{1,0:T(8,128)}) async-done(((f32[64,4,256]{2,0,1:T(8,128)}, f32[64,256]{1,0:T(8,128)}, f32[64,256]{1,0:T(8,128)}), (f32[64,4,256]{2,0,1:T(8,128)}, f32[64,256]{1,0:T(8,128)}, f32[64,256]{1,0:T(8,128)})) %all-reduce.3.cloned.1.call-update) | async-done | bytes 393232 | tf_op jit(solution)/shard_map/psum | solution.py:83
  190.7 1.6 fusion.5
  192.3 1.5 copy.32
  193.8 1.5 copy.33
  (10 shorter events, 0.1 us)
Async XLA Ops:
  7.2 1.0 copy-start
  7.2 56.0 %reduce-scatter.2.cloned.1.call-start = ((), (), s32[]{:S(2)}) async-start(), calls=%async_computation.1 | async-start | bytes 196608 | tf_op jit(solution)/shard_map/reduce_scatter | solution.py:51
  41.4 12.9 %copy-start.3 = (bf16[64,256]{1,0:T(8,128)(2,1)S(1)}, bf16[64,256]{1,0:T(8,128)(2,1)}, u32[]{:S(2)}) copy-start(bf16[64,256]{1,0:T(8,128)(2,1)} %param.17) | copy-start | bytes 98308
  41.4 13.2 %copy-start.1 = (bf16[64,256]{1,0:T(8,128)(2,1)S(1)}, bf16[64,256]{1,0:T(8,128)(2,1)}, u32[]{:S(2)}) copy-start(bf16[64,256]{1,0:T(8,128)(2,1)} %param.10) | copy-start | bytes 98308
  41.4 13.2 %copy-start.2 = (bf16[64,256]{1,0:T(8,128)(2,1)S(1)}, bf16[64,256]{1,0:T(8,128)(2,1)}, u32[]{:S(2)}) copy-start(bf16[64,256]{1,0:T(8,128)(2,1)} %param.16) | copy-start | bytes 98308
  41.4 14.1 %copy-start.7 = (s32[16]{0:T(128)S(1)}, s32[16]{0:T(128)}, u32[]{:S(2)}) copy-start(s32[16]{0:T(128)} %param.12) | copy-start | bytes 196
  53.6 2.6 %copy-start.4 = (s32[16,256]{1,0:T(8,128)S(1)}, s32[16,256]{1,0:T(8,128)}, u32[]{:S(2)}) copy-start(s32[16,256]{1,0:T(8,128)} %param.14) | copy-start | bytes 49156
  53.6 9.6 %copy-start.5 = (bf16[128,256]{1,0:T(8,128)(2,1)S(1)}, bf16[128,256]{1,0:T(8,128)(2,1)}, u32[]{:S(2)}) copy-start(bf16[128,256]{1,0:T(8,128)(2,1)} %param.19) | copy-start | bytes 196612
  53.6 9.6 %copy-start.6 = (f32[128]{0:T(128)S(1)}, f32[128]{0:T(128)}, u32[]{:S(2)}) copy-start(f32[128]{0:T(128)} %param.18) | copy-start | bytes 1540
  55.4 135.3 %all-reduce.3.cloned.1.call-start = ((), (), s32[]{:S(2)}) async-start(), calls=%async_computation.2 | async-start | bytes 786432 | tf_op jit(solution)/shard_map/psum | solution.py:83
Sparse Core Ops, SparseCore 0:
  55.6 7.5 reduce-scatter.1
  99.7 90.9 all-reduce.2
where the time goes:
time: 203 us; the launch traced here: 202 us
  blocking collectives  63.7 us (31%)
  waiting for transfers between devices  62.4 us (31%)
  other arithmetic  33.5 us (17%)
  local copies, waits for them, and re-layouts  21.8 us (11%)
  between operations  16.2 us (8%)
  matrix products  4.47 us (2%)
    psum x1, waiting for transfers between devices, per_device(): summed = lax.psum(kept, 'dom')  57.3 us
    psum x1, blocking collectives, per_device(): lax.psum((self_part, nbr_part, bias_part), 'dom')  32.5 us
    all_gather x1, blocking collectives, per_device(): sources = lax.all_gather(own_source, 'dom', axis=1, tiled=True)  26.2 us
    scatter-add x1, other arithmetic, per_device(): contrib = jnp.zeros((col_width, total_rows), jnp.float32).at[:, neighbour...  23.8 us
    gather x1, local copies, waits for them, and re-layouts, per_device(): gathered = sources[:, neighbours].astype(jnp.float32)  12.1 us
    reduce_scatter x1, waiting for transfers between devices, per_device(): lax.psum_scatter(partial_pre.astype(jnp.bfloat16), 'col', scatter_dimensi...  5.01 us
    unnamed x23, local copies, waits for them, and re-layouts  4.99 us
    all_gather x1, blocking collectives, per_device(): grad_full = lax.all_gather(grad_pre, 'col', axis=0, tiled=True)  4.93 us
  transfers between devices with their start and end apart: 2, of which 2 were waited for; matrix products, arithmetic and copies ran while one was open for 1% of the time, Pallas kernels for 0%

commit v1 on v0

--- a/solution.py
+++ b/solution.py
@@ -1,9 +1,306 @@
+import functools
+
 import jax
 import jax.numpy as jnp
 from jax import lax
+from jax.experimental import pallas as pl
+from jax.experimental.pallas import tpu as pltpu
 from jax.sharding import PartitionSpec as P
 
 LIMIT = 8
+LANES = 128
+BF16 = jnp.bfloat16
+F32 = jnp.float32
+SMEM = pl.BlockSpec(memory_space=pltpu.SMEM)
+VMEM = pl.BlockSpec(memory_space=pltpu.VMEM)
+PARAMS = pltpu.CompilerParams(vmem_limit_bytes=32 * 1024 * 1024)
+
+
+def call(body, outs, smem_count, vmem_count, scratch=(), flops=0, moved=0, **kw):
+    return pl.pallas_call(
+        body,
+        out_shape=outs,
+        in_specs=[SMEM] * smem_count + [VMEM] * vmem_count,
+        out_specs=jax.tree.map(lambda _: VMEM, outs),
+        scratch_shapes=list(scratch),
+        compiler_params=PARAMS,
+        cost_estimate=pl.CostEstimate(flops=flops, bytes_accessed=moved, transcendentals=0),
+        **kw,
+    )
+
+
+def count_body(stale_ref, nbr_ref, deg_ref, cache_ref, listed_ref, acc_ref, all_ref):
+    slots, nodes = nbr_ref.shape
+    parts = stale_ref.shape[0]
+    listed = listed_ref.shape[0] // nodes
+    used = lax.broadcasted_iota(jnp.int32, (slots, nodes), 0) < deg_ref[...]
+    index = jnp.where(used, nbr_ref[...], -1)
+    tall = 32
+
+    def per_rows(step, carry):
+        top = pl.multiple_of(step * tall, tall)
+        place = lax.broadcasted_iota(jnp.int32, (tall, nodes), 0) + top
+        total = jnp.zeros((tall, nodes), F32)
+        for k in range(slots):
+            total = total + jnp.where(index[k : k + 1, :] == place, F32(1), F32(0))
+        all_ref[pl.ds(top, tall), :] = total.astype(BF16)
+        return carry
+
+    lax.fori_loop(0, parts * nodes // tall, per_rows, jnp.int32(0))
+
+    def per_part(part, rank):
+        fresh = stale_ref[part] >= LIMIT
+        rows = pl.ds(pl.multiple_of(part * nodes, nodes), nodes)
+
+        @pl.when(fresh)
+        def _():
+            to = pl.multiple_of(jnp.minimum(rank, listed - 1) * nodes, nodes)
+            listed_ref[pl.ds(to, nodes), :] = all_ref[rows, :]
+            all_ref[rows, :] = jnp.zeros((nodes, nodes), BF16)
+
+        return rank + fresh.astype(jnp.int32)
+
+    lax.fori_loop(0, parts, per_part, jnp.int32(0))
+    acc_ref[...] = jnp.dot(cache_ref[...], all_ref[...], preferred_element_type=F32)
+
+
+def fold_body(x_ref, out_ref):
+    width, nodes = x_ref.shape
+    for h in range(nodes // LANES):
+        out_ref[h * width : (h + 1) * width, :] = x_ref[:, h * LANES : (h + 1) * LANES]
+
+
+def pick_body(stale_ref, got_ref, out_ref, wide, kept):
+    parts = stale_ref.shape[0]
+    tall = got_ref.shape[0] // parts
+    listed = kept.shape[0] // tall
+    wide[...] = got_ref[...].astype(F32)
+
+    def per_part(part, rank):
+        fresh = stale_ref[part] >= LIMIT
+
+        @pl.when(fresh)
+        def _():
+            row = pl.multiple_of(jnp.minimum(rank, listed - 1) * tall, tall)
+            kept[pl.ds(row, tall), :] = wide[pl.ds(pl.multiple_of(part * tall, tall), tall), :]
+
+        return rank + fresh.astype(jnp.int32)
+
+    lax.fori_loop(0, parts, per_part, jnp.int32(0))
+    slot = kept[...].astype(BF16)
+    for d in range(out_ref.shape[0]):
+        out_ref[d] = slot
+
+
+def node_weights(counts_ref, deg):
+    nodes = deg.shape[1]
+    live = (
+        lax.broadcasted_iota(jnp.int32, (1, nodes), 1) < counts_ref[lax.axis_index("dom")]
+    ).astype(F32)
+    return live, live / deg.astype(F32)
+
+
+def mean_body(counts_ref, deg_ref, acc_ref, fresh_ref, listed_ref, out_ref):
+    width, nodes = acc_ref.shape
+    listed = listed_ref.shape[0] // nodes
+    chunks, tall = fresh_ref.shape[0], fresh_ref.shape[1] // listed
+    halves = nodes // LANES
+    groups = chunks // halves
+    total = acc_ref[...]
+    fresh = fresh_ref[...].astype(F32).reshape(chunks, listed, tall, LANES)
+    for r in range(listed):
+        for h in range(halves):
+            piece = fresh[h * groups : (h + 1) * groups, r].reshape(width, LANES).astype(BF16)
+            row = r * nodes + h * LANES
+            total += jnp.dot(piece, listed_ref[row : row + LANES, :], preferred_element_type=F32)
+    _, weight = node_weights(counts_ref, deg_ref[...])
+    out_ref[...] = (total * weight).astype(BF16)
+
+
+def dense_body(n_col, dom, counts_ref, deg_ref, listed_ref, *refs):
+    ins = refs[: 6 * n_col]
+    act_ref, own_ref, slot_ref, cot_full, bias_full, full = refs[6 * n_col :]
+    feats, aggs, selfs, nbrs, biases, cots = [ins[i * n_col : (i + 1) * n_col] for i in range(6)]
+    width, nodes = feats[0].shape
+    part_h = cots[0].shape[0]
+    me = lax.axis_index("col")
+    live, weight = node_weights(counts_ref, deg_ref[...])
+    pre = jnp.zeros((part_h * n_col, nodes), F32)
+    for s in range(n_col):
+        rows = pl.ds(pl.multiple_of(lax.rem(me + n_col - s, n_col) * part_h, part_h), part_h)
+        cot_full[rows, :] = cots[s][...].astype(F32)
+        bias_full[rows, :] = jnp.broadcast_to(biases[s][...], (LANES, part_h)).T
+        for w, x in ((selfs[s], feats[s]), (nbrs[s], aggs[s])):
+            pre += jnp.dot(w[...].astype(F32).T.astype(BF16), x[...], preferred_element_type=F32)
+    pre += jnp.concatenate([bias_full[...]] * (nodes // LANES), 1)
+    sig = 1.0 / (1.0 + jnp.exp(-pre))
+    full[...] = live * pre * sig
+    own_rows = pl.ds(pl.multiple_of(me * part_h, part_h), part_h)
+    act_ref[...] = full[own_rows, :].astype(BF16)
+    grad = (live * cot_full[...] * sig * (1.0 + pre * (1.0 - sig))).astype(BF16)
+    cot_full[...] = grad.astype(F32)
+    back = jnp.dot(nbrs[0][...], grad, preferred_element_type=F32)
+    own_ref[...] = jnp.dot(selfs[0][...], grad, preferred_element_type=F32)
+    spread = (weight * back.astype(BF16).astype(F32)).astype(BF16)
+    contrib = lax.dot_general(
+        spread, listed_ref[...], (((1,), (1,)), ((), ())), preferred_element_type=F32
+    )
+    wgrads = [
+        lax.dot_general(x[...], grad, (((1,), (1,)), ((), ())), preferred_element_type=F32)
+        for x in (feats[0], aggs[0])
+    ]
+    ones = jnp.ones((16, nodes), BF16)
+    bias = lax.dot_general(
+        ones, cot_full[own_rows, :].astype(BF16), (((1,), (1,)), ((), ())), preferred_element_type=F32
+    )[:8]
+    high = bias.astype(BF16).astype(F32)
+    listed = listed_ref.shape[0] // nodes
+    halves = nodes // LANES
+    hidden = part_h * n_col
+    for d in range(dom):
+        s, h = d // halves, d % halves
+        pieces = [
+            contrib[8 * s : 8 * s + 8, r * nodes + h * LANES : r * nodes + (h + 1) * LANES]
+            for r in range(listed)
+        ]
+        which, row = divmod(8 * d, width)
+        pieces += [
+            wgrads[which][row : row + 8, i * LANES : (i + 1) * LANES] for i in range(hidden // LANES)
+        ]
+        slot_ref[d] = jnp.concatenate(pieces + [high, bias - high], 0).astype(BF16)
+
+
+def total_body(stale_ref, got_ref, out_ref, bias_ref, kept):
+    dom = got_ref.shape[0]
+    listed = stale_ref.shape[0] // 4
+    total = got_ref[0].astype(F32)
+    for d in range(1, dom):
+        total += got_ref[d].astype(F32)
+    split = 8 * listed
+    kept[...] = total[:split]
+    weight = total[split : split + 16]
+    bias_ref[...] = total[split + 16 : split + 24][:1] + total[split + 24 :][:1]
+
+    def per_part(part, rank):
+        mine = kept[pl.ds(pl.multiple_of(jnp.minimum(rank, listed - 1) * 8, 8), 8), :]
+        out_ref[part] = jnp.concatenate([weight, mine, jnp.zeros_like(mine)], 0).astype(BF16)
+        return rank + (stale_ref[part] >= LIMIT).astype(jnp.int32)
+
+    lax.fori_loop(0, dom, per_part, jnp.int32(0))
+
+
+def last_body(stale_ref, own_ref, got_ref, feat_ref, self_ref, nbr_ref):
+    width, nodes = own_ref.shape
+    fresh = (stale_ref[lax.axis_index("dom")] >= LIMIT).astype(F32)
+    dom = got_ref.shape[0]
+    halves = nodes // LANES
+    for s in range(width // 16):
+        rows = []
+        for g in (2 * s, 2 * s + 1):
+            rows.append(
+                jnp.concatenate([got_ref[g * halves + h, 16:32].astype(F32)[:8] for h in range(halves)], 1)
+            )
+        span = slice(16 * s, 16 * s + 16)
+        feat_ref[span, :] = (own_ref[span, :] + fresh * jnp.concatenate(rows, 0)).astype(BF16)
+    for d in range(dom):
+        part = got_ref[d, :16].astype(F32)
+        row = jnp.concatenate([part[:8], part[8:]], 1)
+        ref, at = (self_ref, d) if 8 * d < width else (nbr_ref, d - width // 8)
+        ref[8 * at : 8 * at + 8, :] = row
+
+
+def per_device(
+    n_col,
+    features,
+    cached_embed,
+    staleness,
+    node_counts,
+    neighbours,
+    degrees,
+    w_self,
+    w_nbr,
+    sage_bias,
+    cotangent,
+):
+    width, nodes = features.shape
+    hidden = w_self.shape[1]
+    dom = staleness.shape[0]
+    if width * nodes != dom * 8 * LANES or cotangent.shape[0] != LANES:
+        return plain(
+            features, cached_embed, staleness, node_counts, neighbours, degrees, w_self, w_nbr, sage_bias, cotangent
+        )
+    listed = dom // 4
+    part_h = cotangent.shape[0]
+    shape = jax.ShapeDtypeStruct
+
+    def around(block):
+        got = [block]
+        for shift in range(1, n_col):
+            got.append(
+                lax.ppermute(block, "col", [(i, (i + shift) % n_col) for i in range(n_col)])
+            )
+        return got
+
+    def exchange(slots):
+        return lax.all_to_all(slots, "dom", split_axis=0, concat_axis=0, tiled=True)
+
+    halves = nodes // LANES
+    chunks = call(fold_body, shape((width * halves, LANES), BF16), 0, 1, moved=4 * features.size)(features)
+    got = exchange(chunks.reshape(dom, width * halves // dom, LANES))
+    feats, selfs, nbrs = around(features), around(w_self), around(w_nbr)
+    biases, cots = around(sage_bias.reshape(1, part_h)), around(cotangent)
+    deg = degrees.reshape(1, nodes)
+    counts, acc = call(
+        count_body,
+        (shape((listed * nodes, nodes), BF16), shape((width, nodes), F32)),
+        1,
+        3,
+        [pltpu.VMEM((dom * nodes, nodes), BF16)],
+        flops=2 * width * dom * nodes * nodes,
+        moved=2 * (dom * nodes * width + listed * nodes * nodes),
+    )(staleness, neighbours, deg, cached_embed)
+    tall = width * halves // dom
+    picked = call(
+        pick_body,
+        shape((dom, listed * tall, LANES), BF16),
+        1,
+        1,
+        [pltpu.VMEM((dom * tall, LANES), F32), pltpu.VMEM((listed * tall, LANES), F32)],
+        moved=4 * got.size,
+    )(staleness, got.reshape(dom * tall, LANES))
+    fresh = exchange(picked)
+    agg = call(mean_body, shape((width, nodes), BF16), 1, 4, moved=2 * fresh.size)(
+        node_counts, deg, acc, fresh, counts
+    )
+    aggs = around(agg)
+    rows = 8 * listed + 8 * hidden // LANES + 16
+    act, own, slots = call(
+        functools.partial(dense_body, n_col, dom),
+        (shape((part_h, nodes), BF16), shape((width, nodes), F32), shape((dom, rows, LANES), BF16)),
+        1,
+        2 + 6 * n_col,
+        [pltpu.VMEM((hidden, nodes), F32), pltpu.VMEM((hidden, LANES), F32), pltpu.VMEM((hidden, nodes), F32)],
+        flops=2 * width * nodes * (hidden * 6 + listed * nodes),
+        moved=4 * dom * rows * LANES,
+    )(node_counts, deg, counts, *feats, *aggs, *selfs, *nbrs, *biases, *cots)
+    parts = exchange(slots)
+    back, bias = call(
+        total_body,
+        (shape((dom, 32, LANES), BF16), shape((1, LANES), F32)),
+        1,
+        1,
+        [pltpu.VMEM((8 * listed, LANES), F32)],
+        moved=4 * parts.size,
+    )(staleness, parts)
+    final = exchange(back)
+    grad_feat, grad_self, grad_nbr = call(
+        last_body,
+        (shape((width, nodes), BF16), shape((width, hidden), F32), shape((width, hidden), F32)),
+        1,
+        2,
+        moved=4 * final.size,
+    )(staleness, own, final)
+    return act, grad_feat, grad_self, grad_nbr, bias.reshape(-1)
 
 
 def left_product(weight, data):
@@ -18,7 +315,7 @@
     )
 
 
-def per_device(
+def plain(
     features,
     cached_embed,
     staleness,
@@ -103,7 +400,7 @@
         P("col", "dom"),
     )
     return jax.shard_map(
-        per_device,
+        functools.partial(per_device, mesh.shape["col"]),
         mesh=mesh,
         in_specs=placed,
         out_specs=(P("col", "dom"), P("col", "dom"), P("col", None), P("col", None), P("col")),

time: 203 us -> 73.1 us (0.36)
  waiting for transfers between devices: 62.4 us -> 3.37 us
  other arithmetic: 33.5 us -> 0 us
  blocking collectives: 63.7 us -> 40.3 us
  local copies, waits for them, and re-layouts: 21.8 us -> 2.86 us
  Pallas kernels: 0 us -> 15.5 us
  between operations: 16.2 us -> 0.74 us
  starting transfers between devices: 0.08 us -> 9.85 us
  matrix products: 4.47 us -> 0 us
    psum x1 -> x0, waiting for transfers between devices: 57.3 us -> none  [per_device(): summed = lax.psum(kept, 'dom')]
    all_to_all x0 -> x3, blocking collectives: none -> 40.3 us  [exchange(): return lax.all_to_all(slots, 'dom', split_axis=0, concat_axis=0, tiled=True)]
    psum x1 -> x0, blocking collectives: 32.5 us -> none  [per_device(): lax.psum((self_part, nbr_part, bias_part), 'dom')]
    all_gather x2 -> x0, blocking collectives: 31.2 us -> none  [the longest x1 26.2 us: per_device(): sources = lax.all_gather(own_source, 'dom', axis=1, tiled=True)]
    scatter-add x1 -> x0, other arithmetic: 23.8 us -> none  [per_device(): contrib = jnp.zeros((col_width, total_rows), jnp.float32).at[:, neighbour...]
    pallas_call x0 -> x7, Pallas kernels: none -> 15.5 us  [the longest x1 9.18 us: per_device(): call(count_body, (shape((listed * nodes, nodes), BF16), shape((width, nod...]
    gather x2 -> x0, local copies, waits for them, and re-layouts: 12.7 us -> none  [the longest x1 12.1 us: per_device(): gathered = sources[:, neighbours].astype(jnp.float32)]
    ppermute x0 -> x6, starting transfers between devices: none -> 6.21 us  [around(): lax.ppermute(block, 'col', [(i, (i + shift) % n_col) for i in range(n_col)])]
  transfers between devices with their start and end apart: 2 -> 7, of which waited for: 2 -> 1; matrix products, arithmetic and copies ran while one was open for 1% -> 0% of each run, Pallas kernels for 0% -> 14%
where the time goes in v1:
time: 73.1 us; the launch traced here: 72.7 us
  blocking collectives  40.3 us (55%)
  Pallas kernels  15.5 us (21%)
  starting transfers between devices  9.85 us (13%)
  waiting for transfers between devices  3.37 us (5%)
  local copies, waits for them, and re-layouts  2.86 us (4%)
  between operations  0.74 us (1%)
    all_to_all x3, blocking collectives, exchange(): return lax.all_to_all(slots, 'dom', split_axis=0, concat_axis=0, tiled=True)  40.3 us
    pallas_call x1, Pallas kernels, per_device(): call(count_body, (shape((listed * nodes, nodes), BF16), shape((width, nod...  9.18 us
    ppermute x6, starting transfers between devices, around(): lax.ppermute(block, 'col', [(i, (i + shift) % n_col) for i in range(n_col)])  6.21 us
    all_to_all x1, starting transfers between devices, exchange(): return lax.all_to_all(slots, 'dom', split_axis=0, concat_axis=0, tiled=True)  3.64 us
    ppermute x6, waiting for transfers between devices, around(): lax.ppermute(block, 'col', [(i, (i + shift) % n_col) for i in range(n_col)])  3.37 us
    unnamed x24, local copies, waits for them, and re-layouts  2.86 us
    pallas_call x1, Pallas kernels, per_device(): call(functools.partial(dense_body, n_col, dom), (shape((part_h, nodes), B...  1.74 us
  transfers between devices with their start and end apart: 7, of which 1 were waited for; matrix products, arithmetic and copies ran while one was open for 0% of the time, Pallas kernels for 14%

profile of v1, /device:TPU:0, one launch (start us, length us, event | category | flops | bytes accessed | tf_op | source)
XLA Modules:
  0.0 72.7 jit_solution(12461742276830826709)
XLA Ops:
  0.6 0.0 copy-start
  0.6 0.0 copy-start.1
  0.7 0.8 %copy-done.1 = bf16[64,256]{1,0:T(8,128)(2,1)S(1)} copy-done((bf16[64,256]{1,0:T(8,128)(2,1)S(1)}, bf16[64,256]{1,0:T(8,128)(2,1)}, u32[]{:S(2)}) %copy-start.1) | copy-done | bytes 32792
  1.5 13.8 %all_to_all.20 = bf16[16,8,128]{2,1,0:T(8,128)(2,1)S(1)} all-to-all(bf16[16,8,128]{2,1,0:T(8,128)(2,1)S(1)} %bitcast.6), channel_id=1, replica_groups=mesh['dom'=16,'col'=2] {'dom'}, dimensions={0} | all-to-all | bytes 65536 | tf_op jit(solution)/shard_map/all_to_all | solution.py:245
  15.3 0.0 copy-start.8
  15.3 0.7 copy-done.8
  15.9 1.4 %shard_map.139 = bf16[16,32,128]{2,1,0:T(8,128)(2,1)} custom-call(s32[16]{0:T(128)S(1)} %copy-done.8, bf16[128,128]{1,0:T(8,128)(2,1)S(1)} %bitcast.5), custom_call_target="tpu_custom_call" | custom-call | bytes 65536 | tf_op jit(solution)/shard_map/pallas_call | solution.py:263
  17.4 0.0 copy-start.2
  17.4 3.6 %all-to-all-start.1 = ((bf16[16,32,128]{2,1,0:T(8,128)(2,1)}), bf16[16,32,128]{2,1,0:T(8,128)(2,1)S(1)}, u32[]{:S(2)}, u32[]{:S(2)}) async-start(bf16[16,32,128]{2,1,0:T(8,128)(2,1)} %shard_map.139), calls=%async_computation.1 | async-start | bytes 262144 | tf_op jit(solution)/shard_map/all_to_all | solution.py:245
  21.0 0.0 copy-start.11
  21.0 1.6 %collective-permute-start.5 = (bf16[128,256]{1,0:T(8,128)(2,1)}, bf16[128,256]{1,0:T(8,128)(2,1)S(1)}, u32[]{:S(2)}, u32[]{:S(2)}) collective-permute-start(bf16[128,256]{1,0:T(8,128)(2,1)} %refs_10_.1), channel_id=1, source_target_pairs={{0,1},{1,0},{2,3},{3,2},{4,5},{5,4},{6,7},{7,6},{8,9},{9,8},{10,11... | collective-permute-start | bytes 196616 | tf_op jit(solution)/shard_map/ppermute | solution.py:240
  22.6 0.0 copy-done.2
  22.6 0.5 collective-permute-start
  23.1 0.0 copy-done.11
  23.1 0.0 copy-start.7
  23.1 0.0 copy-start.9
  23.1 1.5 %collective-permute-start.4 = (f32[1,128]{1,0:T(1,128)S(1)}, f32[1,128]{1,0:T(1,128)S(1)}, u32[]{:S(2)}, u32[]{:S(2)}) collective-permute-start(f32[1,128]{1,0:T(1,128)S(1)} %bitcast.10), channel_id=1, source_target_pairs={{0,1},{1,0},{2,3},{3,2},{4,5},{5,4},{6,7},{7,6},{8,9},{9,8},{10,11... | collective-permute-start | bytes 1544 | tf_op jit(solution)/shard_map/ppermute | solution.py:240
  24.6 0.5 collective-permute-start.2
  25.2 1.5 %collective-permute-start.3 = (bf16[64,256]{1,0:T(8,128)(2,1)}, bf16[64,256]{1,0:T(8,128)(2,1)S(1)}, u32[]{:S(2)}, u32[]{:S(2)}) collective-permute-start(bf16[64,256]{1,0:T(8,128)(2,1)} %refs_6_.1), channel_id=1, source_target_pairs={{0,1},{1,0},{2,3},{3,2},{4,5},{5,4},{6,7},{7,6},{8,9},{9,8},{10,11... | collective-permute-start | bytes 98312 | tf_op jit(solution)/shard_map/ppermute | solution.py:240
  26.7 0.0 copy-done
  26.7 0.0 copy-done.7
  26.7 0.0 copy-done.9
  26.7 0.0 copy-start.6
  26.7 0.7 copy-done.6
  27.4 9.2 %shard_map.137 = (bf16[1024,256]{1,0:T(8,128)(2,1)S(1)}, f32[64,256]{1,0:T(8,128)S(1)}) custom-call(s32[16]{0:T(128)S(1)} %copy-done.9, s32[16,256]{1,0:T(8,128)S(1)} %copy-done.6, s32[1,256]{1,0:T(1,128)S(1)} %bitcast.7, bf16[64,4096]{1,0:T(8,128)(2,1)S(1)} %copy-done), custom_call_target="tpu_custom_call" | custom-call | flops 134217728 | bytes 1048576 | tf_op jit(solution)/shard_map/pallas_call | solution.py:253
  36.6 0.0 all-to-all-done.1.fresh_ref
  36.6 0.0 copy-start.10
  36.6 0.6 copy-done.10
  37.2 0.0 copy-start.3
  37.2 0.0 copy-start.4
  37.2 0.0 copy-start.5
  37.2 0.8 %shard_map.140.refs_2_ = bf16[64,256]{1,0:T(8,128)(2,1)S(1)} custom-call(s32[16]{0:T(128)S(1)} %copy-done.10, s32[1,256]{1,0:T(1,128)S(1)} %bitcast.8, f32[64,256]{1,0:T(8,128)S(1)} %get-tuple-element.16.acc_ref, bf16[16,32,128]{2,1,0:T(8,128)(2,1)S(1)} %all-to-all-done.1.fresh_ref, bf16[1024,256]{1,0:T(8,128)(2,1)S(1)} %get-tuple-element.15.listed_ref), custom_call_target="tpu_custom_call" | custom-call | bytes 131072 | tf_op jit(solution)/shard_map/pallas_call | solution.py:272
  38.0 0.0 collective-permute-done.4.refs_9_
  38.0 0.6 collective-permute-start.1
  38.6 0.0 collective-permute-done.2.refs_5_
  38.6 0.0 collective-permute-done.3.refs_7_
  38.6 0.0 collective-permute-done.refs_1_
  38.6 0.0 collective-permute-done.5.refs_11_
  38.6 3.4 %collective-permute-done.1.refs_3_ = bf16[64,256]{1,0:T(8,128)(2,1)S(1)} collective-permute-done((bf16[64,256]{1,0:T(8,128)(2,1)S(1)}, bf16[64,256]{1,0:T(8,128)(2,1)S(1)}, u32[]{:S(2)}, u32[]{:S(2)}) %collective-permute-start.1) | collective-permute-done | bytes 32800 | tf_op jit(solution)/shard_map/ppermute | solution.py:240
  42.0 0.0 copy-done.3
  42.0 0.0 copy-done.4
  42.0 0.0 copy-done.5
  42.0 1.7 %shard_map.141 = (bf16[128,256]{1,0:T(8,128)(2,1)}, f32[64,256]{1,0:T(8,128)S(1)}, bf16[16,64,128]{2,1,0:T(8,128)(2,1)S(1)}) custom-call(s32[16]{0:T(128)S(1)} %copy-done.10, s32[1,256]{1,0:T(1,128)S(1)} %bitcast.9, bf16[1024,256]{1,0:T(8,128)(2,1)S(1)} %get-tuple-element.15.listed_ref, bf16[64,256]{1,0:T(8,128)(2,1)S(1)} %copy-done.2, ...), custom_call_target="tpu_custom_call" | custom-call | flops 83886080 | bytes 524288 | tf_op jit(solution)/shard_map/pallas_call | solution.py:277
  43.7 15.8 %all_to_all.21.got_ref = bf16[16,64,128]{2,1,0:T(8,128)(2,1)S(1)} all-to-all(bf16[16,64,128]{2,1,0:T(8,128)(2,1)S(1)} %get-tuple-element.19), channel_id=1, replica_groups=mesh['dom'=16,'col'=2] {'dom'}, dimensions={0} | all-to-all | bytes 524288 | tf_op jit(solution)/shard_map/all_to_all | solution.py:245
  59.5 1.2 %shard_map.142 = (bf16[16,32,128]{2,1,0:T(8,128)(2,1)S(1)}, f32[1,128]{1,0:T(1,128)}) custom-call(s32[16]{0:T(128)S(1)} %copy-done.9, bf16[16,64,128]{2,1,0:T(8,128)(2,1)S(1)} %all_to_all.21.got_ref), custom_call_target="tpu_custom_call" | custom-call | bytes 524288 | tf_op jit(solution)/shard_map/pallas_call | solution.py:287
  60.8 10.7 %all_to_all.22.got_ref = bf16[16,32,128]{2,1,0:T(8,128)(2,1)S(1)} all-to-all(bf16[16,32,128]{2,1,0:T(8,128)(2,1)S(1)} %get-tuple-element.20), channel_id=1, replica_groups=mesh['dom'=16,'col'=2] {'dom'}, dimensions={0} | all-to-all | bytes 262144 | tf_op jit(solution)/shard_map/all_to_all | solution.py:245
  71.5 1.2 %shard_map.143 = (bf16[64,256]{1,0:T(8,128)(2,1)}, f32[64,256]{1,0:T(8,128)}, f32[64,256]{1,0:T(8,128)}) custom-call(s32[16]{0:T(128)S(1)} %copy-done.9, f32[64,256]{1,0:T(8,128)S(1)} %get-tuple-element.18.own_ref, bf16[16,32,128]{2,1,0:T(8,128)(2,1)S(1)} %all_to_all.22.got_ref), custom_call_target="tpu_custom_call" | custom-call | bytes 262144 | tf_op jit(solution)/shard_map/pallas_call | solution.py:296
  (1 shorter events, 0.0 us)
Async XLA Ops:
  0.6 26.0 %copy-start = (bf16[64,4096]{1,0:T(8,128)(2,1)S(1)}, bf16[64,4096]{1,0:T(8,128)(2,1)}, u32[]{:S(2)}) copy-start(bf16[64,4096]{1,0:T(8,128)(2,1)} %cache_ref.1) | copy-start | bytes 1572868
  0.6 0.8 %copy-start.1 = (bf16[64,256]{1,0:T(8,128)(2,1)S(1)}, bf16[64,256]{1,0:T(8,128)(2,1)}, u32[]{:S(2)}) copy-start(bf16[64,256]{1,0:T(8,128)(2,1)} %refs_0_.1) | copy-start | bytes 98308
  15.3 0.7 copy-start.8
  17.4 5.2 %copy-start.2 = (bf16[64,256]{1,0:T(8,128)(2,1)S(1)}, bf16[64,256]{1,0:T(8,128)(2,1)}, u32[]{:S(2)}) copy-start(bf16[64,256]{1,0:T(8,128)(2,1)} %refs_0_.1) | copy-start | bytes 98308
  17.4 19.2 %all-to-all-start.1 = ((bf16[16,32,128]{2,1,0:T(8,128)(2,1)}), bf16[16,32,128]{2,1,0:T(8,128)(2,1)S(1)}, u32[]{:S(2)}, u32[]{:S(2)}) async-start(bf16[16,32,128]{2,1,0:T(8,128)(2,1)} %shard_map.139), calls=%async_computation.1 | async-start | bytes 262144 | tf_op jit(solution)/shard_map/all_to_all | solution.py:245
  21.0 2.1 %copy-start.11 = (f32[128]{0:T(128)S(1)}, f32[128]{0:T(128)}, u32[]{:S(2)}) copy-start(f32[128]{0:T(128)} %param.18) | copy-start | bytes 1540
  21.0 17.6 %collective-permute-start.5 = (bf16[128,256]{1,0:T(8,128)(2,1)}, bf16[128,256]{1,0:T(8,128)(2,1)S(1)}, u32[]{:S(2)}, u32[]{:S(2)}) collective-permute-start(bf16[128,256]{1,0:T(8,128)(2,1)} %refs_10_.1), channel_id=1, source_target_pairs={{0,1},{1,0},{2,3},{3,2},{4,5},{5,4},{6,7},{7,6},{8,9},{9,8},{10,11... | collective-permute-start | bytes 196616 | tf_op jit(solution)/shard_map/ppermute | solution.py:240
  22.6 16.0 %collective-permute-start = (bf16[64,256]{1,0:T(8,128)(2,1)S(1)}, bf16[64,256]{1,0:T(8,128)(2,1)S(1)}, u32[]{:S(2)}, u32[]{:S(2)}) collective-permute-start(bf16[64,256]{1,0:T(8,128)(2,1)S(1)} %copy-done.2), channel_id=1, source_target_pairs={{0,1},{1,0},{2,3},{3,2},{4,5},{5,4},{6,7},{7,6},{8,9},{9,8},{10,11... | collective-permute-start | bytes 98312 | tf_op jit(solution)/shard_map/ppermute | solution.py:240
  23.1 3.5 %copy-start.7 = (s32[256]{0:T(256)S(1)}, s32[256]{0:T(256)}, u32[]{:S(2)}) copy-start(s32[256]{0:T(256)} %param.15) | copy-start | bytes 3076
  23.1 3.5 %copy-start.9 = (s32[16]{0:T(128)S(1)}, s32[16]{0:T(128)}, u32[]{:S(2)}) copy-start(s32[16]{0:T(128)} %stale_ref.7) | copy-start | bytes 196
  23.1 14.9 %collective-permute-start.4 = (f32[1,128]{1,0:T(1,128)S(1)}, f32[1,128]{1,0:T(1,128)S(1)}, u32[]{:S(2)}, u32[]{:S(2)}) collective-permute-start(f32[1,128]{1,0:T(1,128)S(1)} %bitcast.10), channel_id=1, source_target_pairs={{0,1},{1,0},{2,3},{3,2},{4,5},{5,4},{6,7},{7,6},{8,9},{9,8},{10,11... | collective-permute-start | bytes 1544 | tf_op jit(solution)/shard_map/ppermute | solution.py:240
  24.6 14.0 %collective-permute-start.2 = (bf16[64,256]{1,0:T(8,128)(2,1)}, bf16[64,256]{1,0:T(8,128)(2,1)S(1)}, u32[]{:S(2)}, u32[]{:S(2)}) collective-permute-start(bf16[64,256]{1,0:T(8,128)(2,1)} %refs_4_.1), channel_id=1, source_target_pairs={{0,1},{1,0},{2,3},{3,2},{4,5},{5,4},{6,7},{7,6},{8,9},{9,8},{10,11... | collective-permute-start | bytes 98312 | tf_op jit(solution)/shard_map/ppermute | solution.py:240
  25.2 13.5 %collective-permute-start.3 = (bf16[64,256]{1,0:T(8,128)(2,1)}, bf16[64,256]{1,0:T(8,128)(2,1)S(1)}, u32[]{:S(2)}, u32[]{:S(2)}) collective-permute-start(bf16[64,256]{1,0:T(8,128)(2,1)} %refs_6_.1), channel_id=1, source_target_pairs={{0,1},{1,0},{2,3},{3,2},{4,5},{5,4},{6,7},{7,6},{8,9},{9,8},{10,11... | collective-permute-start | bytes 98312 | tf_op jit(solution)/shard_map/ppermute | solution.py:240
  26.7 0.7 copy-start.6
  36.6 0.7 copy-start.10
  37.2 4.8 %copy-start.3 = (bf16[128,256]{1,0:T(8,128)(2,1)S(1)}, bf16[128,256]{1,0:T(8,128)(2,1)}, u32[]{:S(2)}) copy-start(bf16[128,256]{1,0:T(8,128)(2,1)} %refs_10_.1) | copy-start | bytes 196612
  37.2 4.8 %copy-start.4 = (bf16[64,256]{1,0:T(8,128)(2,1)S(1)}, bf16[64,256]{1,0:T(8,128)(2,1)}, u32[]{:S(2)}) copy-start(bf16[64,256]{1,0:T(8,128)(2,1)} %refs_4_.1) | copy-start | bytes 98308
  37.2 4.8 %copy-start.5 = (bf16[64,256]{1,0:T(8,128)(2,1)S(1)}, bf16[64,256]{1,0:T(8,128)(2,1)}, u32[]{:S(2)}) copy-start(bf16[64,256]{1,0:T(8,128)(2,1)} %refs_6_.1) | copy-start | bytes 98308
  38.0 4.0 %collective-permute-start.1 = (bf16[64,256]{1,0:T(8,128)(2,1)S(1)}, bf16[64,256]{1,0:T(8,128)(2,1)S(1)}, u32[]{:S(2)}, u32[]{:S(2)}) collective-permute-start(bf16[64,256]{1,0:T(8,128)(2,1)S(1)} %shard_map.140.refs_2_), channel_id=1, source_target_pairs={{0,1},{1,0},{2,3},{3,2},{4,5},{5,4},{6,7},{7,6},{8,9},{9,8},{10,11... | collective-permute-start | bytes 98312 | tf_op jit(solution)/shard_map/ppermute | solution.py:240

commit v2 on v0

v2 whole, which is shorter than its diff:
```python
import functools

import jax
import jax.numpy as jnp
from jax import lax
from jax.experimental import pallas as pl
from jax.experimental.pallas import tpu as pltpu
from jax.sharding import PartitionSpec as P

LIMIT = 8
LANES = 128
LOW = 4
BF16 = jnp.bfloat16
F32 = jnp.float32
SMEM = pl.BlockSpec(memory_space=pltpu.SMEM)
VMEM = pl.BlockSpec(memory_space=pltpu.VMEM)
PARAMS = pltpu.CompilerParams(vmem_limit_bytes=32 * 1024 * 1024)


def call(body, outs, smem_count, vmem_count, scratch=(), flops=0, moved=0):
    return pl.pallas_call(
        body,
        out_shape=outs,
        in_specs=[SMEM] * smem_count + [VMEM] * vmem_count,
        out_specs=jax.tree.map(lambda _: VMEM, outs),
        scratch_shapes=list(scratch),
        compiler_params=PARAMS,
        cost_estimate=pl.CostEstimate(flops=flops, bytes_accessed=moved, transcendentals=0),
    )


def up16(rows):
    return -(-rows // 16) * 16


def is_fresh(stale_ref, part):
    return stale_ref[part] >= LIMIT


def rank_of(stale_ref, part):
    ahead = lax.fori_loop(
        0, part, lambda p, r: r + is_fresh(stale_ref, p).astype(jnp.int32), jnp.int32(0)
    )
    return jnp.minimum(ahead, stale_ref.shape[0] // 4 - 1)


def split3(x):
    high = x.astype(BF16).astype(F32)
    mid = (x - high).astype(BF16).astype(F32)
    return high, mid, x - high - mid


def count_body(start, total_parts, stale_ref, nbr_ref, deg_ref, cache_ref, *refs):
    slots, nodes = nbr_ref.shape
    *before, listed_ref, acc_ref, all_ref = refs
    listed = listed_ref.shape[0] // nodes
    parts = all_ref.shape[0] // nodes
    used = lax.broadcasted_iota(jnp.int32, (slots, nodes), 0) < deg_ref[...]
    index = jnp.where(used, nbr_ref[...] - start * nodes, -1)
    tall = 32

    def per_rows(step, carry):
        top = pl.multiple_of(step * tall, tall)
        place = lax.broadcasted_iota(jnp.int32, (tall, nodes), 0) + top
        total = jnp.zeros((tall, nodes), F32)
        for k in range(slots):
            total = total + jnp.where(index[k : k + 1, :] == place, F32(1), F32(0))
        all_ref[pl.ds(top, tall), :] = total.astype(BF16)
        return carry

    lax.fori_loop(0, parts * nodes // tall, per_rows, jnp.int32(0))
    if before:
        listed_ref[...] = before[0][...]
    else:
        listed_ref[...] = jnp.zeros_like(listed_ref)

    def per_part(part, rank):
        fresh = is_fresh(stale_ref, start + part)
        rows = pl.ds(pl.multiple_of(part * nodes, nodes), nodes)

        @pl.when(fresh)
        def _():
            to = pl.multiple_of(jnp.minimum(rank, listed - 1) * nodes, nodes)
            listed_ref[pl.ds(to, nodes), :] = all_ref[rows, :]
            all_ref[rows, :] = jnp.zeros((nodes, nodes), BF16)

        return rank + fresh.astype(jnp.int32)

    first = sum([is_fresh(stale_ref, p).astype(jnp.int32) for p in range(start)], jnp.int32(0))
    lax.fori_loop(0, parts, per_part, first)
    share = jnp.dot(
        cache_ref[:, start * nodes : (start + parts) * nodes], all_ref[...], preferred_element_type=F32
    )
    acc_ref[...] = before[1][...] + share if before else share


def pack_body(feat_ref, self_ref, nbr_ref, cot_ref, bias_ref, out_ref, wide):
    row = 0
    for ref in (feat_ref, self_ref, nbr_ref, cot_ref):
        out_ref[row : row + ref.shape[0], :] = ref[...]
        row += ref.shape[0]
    wide[...] = jnp.zeros_like(wide)
    for i, term in enumerate(split3(bias_ref[...])):
        wide[i : i + 1, : bias_ref.shape[1]] = term
    out_ref[row:, :] = wide[...].astype(BF16)


def stack_body(*refs):
    ins, out_ref = refs[:-1], refs[-1]
    rows = ins[0].shape[0]
    for i, ref in enumerate(ins):
        out_ref[i * rows : (i + 1) * rows, :] = ref[...]


def node_weights(counts_ref, deg):
    nodes = deg.shape[1]
    live = (
        lax.broadcasted_iota(jnp.int32, (1, nodes), 1) < counts_ref[lax.axis_index("dom")]
    ).astype(F32)
    return live, live / deg.astype(F32)


def mean_body(stale_ref, counts_ref, deg_ref, acc_ref, listed_ref, *refs):
    stacks, (out_ref, total) = refs[:LOW], refs[LOW:]
    width, nodes = acc_ref.shape
    me = lax.axis_index("dom")
    total[...] = acc_ref[...]
    for low in range(LOW):
        for high in range(stacks[0].shape[0] // width):
            part = jnp.bitwise_xor(me, low + LOW * high)

            @pl.when(is_fresh(stale_ref, part))
            def _(low=low, high=high, part=part):
                row = pl.multiple_of(rank_of(stale_ref, part) * nodes, nodes)
                total[...] += jnp.dot(
                    stacks[low][high * width : (high + 1) * width, :],
                    listed_ref[pl.ds(row, nodes), :],
                    preferred_element_type=F32,
                )

    _, weight = node_weights(counts_ref, deg_ref[...])
    out_ref[...] = (total[...] * weight).astype(BF16)


def dense_body(n_col, counts_ref, deg_ref, listed_ref, feat_ref, self_ref, nbr_ref, bias_ref, cot_ref, *refs):
    aggs, packs, refs = refs[:n_col], refs[n_col : 2 * n_col - 1], refs[2 * n_col - 1 :]
    act_ref, own_ref, slots, (cot_full, bias_full, full, wide) = refs[0], refs[1], refs[2 : 2 + LOW], refs[2 + LOW :]
    width, nodes = feat_ref.shape
    part_h = cot_ref.shape[0]
    hidden = part_h * n_col
    me = lax.axis_index("col")
    live, weight = node_weights(counts_ref, deg_ref[...])
    pre = jnp.zeros((hidden, nodes), F32)
    for s in range(n_col):
        if s == 0:
            feat, w_self, w_nbr, cot, bias = feat_ref[...], self_ref[...], nbr_ref[...], cot_ref[...], bias_ref[...]
        else:
            pack = packs[s - 1]
            feat, w_self, w_nbr = [pack[i * width : (i + 1) * width, :] for i in range(3)]
            cot = pack[3 * width : 3 * width + part_h, :]
            terms = pack[3 * width + part_h :, :].astype(F32)
            bias = (terms[0:1] + terms[1:2] + terms[2:3])[:, :part_h]
        rows = pl.ds(pl.multiple_of(lax.rem(me + n_col - s, n_col) * part_h, part_h), part_h)
        cot_full[rows, :] = cot.astype(F32)
        bias_full[rows, :] = jnp.broadcast_to(bias, (LANES, part_h)).T
        for w, x in ((w_self, feat), (w_nbr, aggs[s][...])):
            pre += jnp.dot(w.astype(F32).T.astype(BF16), x, preferred_element_type=F32)
    pre += jnp.concatenate([bias_full[...]] * (nodes // LANES), 1)
    sig = 1.0 / (1.0 + jnp.exp(-pre))
    full[...] = live * pre * sig
    own_rows = pl.ds(pl.multiple_of(me * part_h, part_h), part_h)
    act_ref[...] = full[own_rows, :].astype(BF16)
    grad = (live * cot_full[...] * sig * (1.0 + pre * (1.0 - sig))).astype(BF16)
    cot_full[...] = grad.astype(F32)
    back = jnp.dot(nbr_ref[...], grad, preferred_element_type=F32)
    own_ref[...] = jnp.dot(self_ref[...], grad, preferred_element_type=F32)
    spread = (weight * back.astype(BF16).astype(F32)).astype(BF16)
    contrib = lax.dot_general(
        spread, listed_ref[...], (((1,), (1,)), ((), ())), preferred_element_type=F32
    )
    wgrads = [
        lax.dot_general(x[...], grad, (((1,), (1,)), ((), ())), preferred_element_type=F32)
        for x in (feat_ref, aggs[0])
    ]
    ones = jnp.ones((16, nodes), BF16)
    bias = lax.dot_general(
        ones, cot_full[own_rows, :].astype(BF16), (((1,), (1,)), ((), ())), preferred_element_type=F32
    )[:1]
    high = bias.astype(BF16).astype(F32)
    group = listed_ref.shape[0] // nodes // LOW
    half = width // 2
    base = group * width + half
    for q in range(LOW):
        for g in range(group):
            r = q * group + g
            wide[q, g * width : (g + 1) * width, :] = contrib[:, r * nodes : (r + 1) * nodes]
        wide[q, base - half : base, :] = wgrads[q // 2][q % 2 * half : (q % 2 + 1) * half, :]
        wide[q, base:, :] = jnp.zeros((wide.shape[1] - base, nodes), F32)
        wide[q, base : base + 1, :part_h] = high
        wide[q, base + 1 : base + 2, :part_h] = bias - high
    low = lax.axis_index("dom") % LOW
    for m in range(LOW):
        slots[m][...] = wide[jnp.bitwise_xor(low, m)].astype(BF16)


def group_sum_body(base, *refs):
    got, (out_ref, wide, full) = refs[:LOW], refs[LOW:]
    low = lax.axis_index("dom") % LOW
    for m in range(LOW):
        wide[jnp.bitwise_xor(low, m)] = got[m][...].astype(F32)
    total = wide[0] + wide[1] + wide[2] + wide[3]
    full[...] = total
    bias = total[base : base + 1] + total[base + 1 : base + 2]
    high = bias.astype(BF16).astype(F32)
    full[base : base + 1, :] = high
    full[base + 1 : base + 2, :] = bias - high
    out_ref[...] = full[...].astype(BF16)


def line_sum_body(base, width, count, stale_ref, *refs):
    got, bias_ref, outs, (wide, full, piece) = refs[:count], refs[count], refs[count + 1 : count + 1 + LOW], refs[count + 1 + LOW :]
    me = lax.axis_index("dom")
    place = me // LOW
    for m in range(count):
        wide[jnp.bitwise_xor(place, m)] = got[m][...].astype(F32)
    total = wide[0]
    for m in range(1, count):
        total += wide[m]
    full[...] = total
    bias_ref[...] = (total[base : base + 1] + total[base + 1 : base + 2])[:, : bias_ref.shape[1]]
    half = width // 2
    group = (base - half) // width
    piece[...] = jnp.zeros_like(piece)
    piece[width : width + half, :] = full[base - half : base, :]
    for m in range(LOW):
        rank = rank_of(stale_ref, jnp.bitwise_xor(me, m))
        row = pl.multiple_of(lax.rem(rank, group) * width, 8)
        piece[:width, :] = full[pl.ds(row, width), :]
        outs[m][...] = piece[...].astype(BF16)


def last_body(group, stale_ref, own_ref, *refs):
    got, (feat_ref, self_ref, nbr_ref, wide) = refs[:LOW], refs[LOW:]
    width = own_ref.shape[0]
    me = lax.axis_index("dom")
    low = me % LOW
    for m in range(LOW):
        wide[jnp.bitwise_xor(low, m)] = got[m][...].astype(F32)
    fresh = is_fresh(stale_ref, me).astype(F32)
    back = wide[rank_of(stale_ref, me) // group][:width]
    feat_ref[...] = (own_ref[...] + fresh * back).astype(BF16)
    half = width // 2
    for q in range(LOW):
        ref = nbr_ref if q // 2 else self_ref
        ref[q % 2 * half : (q % 2 + 1) * half, :] = wide[q, width : width + half, :]


def per_device(
    n_col,
    features,
    cached_embed,
    staleness,
    node_counts,
    neighbours,
    degrees,
    w_self,
    w_nbr,
    sage_bias,
    cotangent,
):
    width, nodes = features.shape
    hidden = w_self.shape[1]
    dom = staleness.shape[0]
    listed = dom // 4
    part_h = cotangent.shape[0]
    shape = jax.ShapeDtypeStruct

    def hop(block, m):
        return lax.ppermute(block, "dom", [(i, i ^ m) for i in range(dom)])

    def along(block):
        return [block] + [hop(block, m) for m in range(LOW, dom, LOW)]

    def within(slots):
        return [slots[0]] + [hop(slots[m], m) for m in range(1, LOW)]

    def around(block):
        return [
            lax.ppermute(block, "col", [(i, (i + s) % n_col) for i in range(n_col)])
            for s in range(1, n_col)
        ]

    line = along(features)
    bias_row = sage_bias.reshape(1, part_h)
    packed = call(
        pack_body,
        shape((3 * width + part_h + 16, nodes), BF16),
        0,
        5,
        [pltpu.VMEM((16, nodes), F32)],
        moved=4 * (3 * width + part_h) * nodes,
    )(features, w_self, w_nbr, cotangent, bias_row)
    packs = around(packed)
    deg = degrees.reshape(1, nodes)
    half_parts = dom // 2

    def count(start, *before):
        return call(
            functools.partial(count_body, start, dom),
            (shape((listed * nodes, nodes), BF16), shape((width, nodes), F32)),
            1,
            3 + len(before),
            [pltpu.VMEM((half_parts * nodes, nodes), BF16)],
            flops=2 * width * half_parts * nodes * nodes,
            moved=half_parts * nodes * nodes * 16,
        )(staleness, neighbours, deg, cached_embed, *before)

    before = count(0)
    stacked = call(stack_body, shape((width * len(line), nodes), BF16), 0, len(line), moved=4 * dom * width * nodes // LOW)(
        *line
    )
    stacks = within([stacked] * LOW)
    counts, acc = count(half_parts, *before)
    agg = call(
        mean_body,
        shape((width, nodes), BF16),
        2,
        3 + LOW,
        [pltpu.VMEM((width, nodes), F32)],
        moved=2 * dom * width * nodes,
    )(staleness, node_counts, deg, acc, counts, *stacks)
    aggs = [agg] + around(agg)
    group = listed // LOW
    base = group * width + width // 2
    rows = up16(base + 2)
    act, own, *slots = call(
        functools.partial(dense_body, n_col),
        [shape((part_h, nodes), BF16), shape((width, nodes), F32)] + [shape((rows, nodes), BF16)] * LOW,
        1,
        7 + 2 * n_col - 1,
        [
            pltpu.VMEM((hidden, nodes), F32),
            pltpu.VMEM((hidden, LANES), F32),
            pltpu.VMEM((hidden, nodes), F32),
            pltpu.VMEM((LOW, rows, nodes), F32),
        ],
        flops=2 * width * nodes * (hidden * 6 + listed * nodes),
        moved=4 * LOW * rows * nodes,
    )(node_counts, deg, counts, features, w_self, w_nbr, bias_row, cotangent, *aggs, *packs)
    summed = call(
        functools.partial(group_sum_body, base),
        shape((rows, nodes), BF16),
        0,
        LOW,
        [pltpu.VMEM((LOW, rows, nodes), F32), pltpu.VMEM((rows, nodes), F32)],
        moved=2 * LOW * rows * nodes,
    )(*within(slots))
    lines = along(summed)
    tall = up16(width + width // 2)
    bias, *pieces = call(
        functools.partial(line_sum_body, base, width, len(lines)),
        [shape((1, part_h), F32)] + [shape((tall, nodes), BF16)] * LOW,
        1,
        len(lines),
        [
            pltpu.VMEM((len(lines), rows, nodes), F32),
            pltpu.VMEM((rows, nodes), F32),
            pltpu.VMEM((tall, nodes), F32),
        ],
        moved=2 * len(lines) * rows * nodes,
    )(staleness, *lines)
    grad_feat, grad_self, grad_nbr = call(
        functools.partial(last_body, group),
        (shape((width, nodes), BF16), shape((width, hidden), F32), shape((width, hidden), F32)),
        1,
        1 + LOW,
        [pltpu.VMEM((LOW, tall, nodes), F32)],
        moved=2 * LOW * tall * nodes,
    )(staleness, own, *within(pieces))
    return act, grad_feat, grad_self, grad_nbr, bias.reshape(-1)


def solution(mesh):
    placed = (
        P("col", "dom"),
        P("col", None),
        P(),
        P(),
        P(None, "dom"),
        P("dom"),
        P("col", None),
        P("col", None),
        P("col"),
        P("col", "dom"),
    )
    return jax.shard_map(
        functools.partial(per_device, mesh.shape["col"]),
        mesh=mesh,
        in_specs=placed,
        out_specs=(P("col", "dom"), P("col", "dom"), P("col", None), P("col", None), P("col")),
        check_vma=False,
    )
```

time: 203 us -> 55.6 us (0.27)
  blocking collectives: 63.7 us -> 0 us
  waiting for transfers between devices: 62.4 us -> 14.8 us
  other arithmetic: 33.5 us -> 0 us
  starting transfers between devices: 0.08 us -> 19.4 us
  local copies, waits for them, and re-layouts: 21.8 us -> 4.52 us
  Pallas kernels: 0 us -> 15.7 us
  between operations: 16.2 us -> 0.79 us
  matrix products: 4.47 us -> 0 us
    psum x1 -> x0, waiting for transfers between devices: 57.3 us -> none  [per_device(): summed = lax.psum(kept, 'dom')]
    psum x1 -> x0, blocking collectives: 32.5 us -> none  [per_device(): lax.psum((self_part, nbr_part, bias_part), 'dom')]
    all_gather x2 -> x0, blocking collectives: 31.2 us -> none  [the longest x1 26.2 us: per_device(): sources = lax.all_gather(own_source, 'dom', axis=1, tiled=True)]
    scatter-add x1 -> x0, other arithmetic: 23.8 us -> none  [per_device(): contrib = jnp.zeros((col_width, total_rows), jnp.float32).at[:, neighbour...]
    ppermute x0 -> x17, starting transfers between devices: none -> 19.4 us  [the longest x15 16.1 us: hop(): return lax.ppermute(block, 'dom', [(i, i ^ m) for i in range(dom)])]
    pallas_call x0 -> x9, Pallas kernels: none -> 15.7 us  [the longest x2 9.91 us: count(): call(functools.partial(count_body, start, dom), (shape((listed * nodes, n...]
    ppermute x0 -> x17, waiting for transfers between devices: none -> 14.8 us  [the longest x15 12.4 us: hop(): return lax.ppermute(block, 'dom', [(i, i ^ m) for i in range(dom)])]
    gather x2 -> x0, local copies, waits for them, and re-layouts: 12.7 us -> none  [the longest x1 12.1 us: per_device(): gathered = sources[:, neighbours].astype(jnp.float32)]
  transfers between devices with their start and end apart: 2 -> 17, of which waited for: 2 -> 8; matrix products, arithmetic and copies ran while one was open for 1% -> 0% of each run, Pallas kernels for 0% -> 20%
where the time goes in v2:
time: 55.6 us; the launch traced here: 55.2 us
  starting transfers between devices  19.4 us (35%)
  Pallas kernels  15.7 us (28%)
  waiting for transfers between devices  14.8 us (27%)
  local copies, waits for them, and re-layouts  4.52 us (8%)
  between operations  0.79 us (1%)
    ppermute x15, starting transfers between devices, hop(): return lax.ppermute(block, 'dom', [(i, i ^ m) for i in range(dom)])  16.1 us
    ppermute x15, waiting for transfers between devices, hop(): return lax.ppermute(block, 'dom', [(i, i ^ m) for i in range(dom)])  12.4 us
    pallas_call x2, Pallas kernels, count(): call(functools.partial(count_body, start, dom), (shape((listed * nodes, n...  9.91 us
    unnamed x30, local copies, waits for them, and re-layouts  4.52 us
    ppermute x2, starting transfers between devices, around(): lax.ppermute(block, 'col', [(i, (i + s) % n_col) for i in range(n_col)])  3.3 us
    ppermute x2, waiting for transfers between devices, around(): lax.ppermute(block, 'col', [(i, (i + s) % n_col) for i in range(n_col)])  2.42 us
    pallas_call x1, Pallas kernels, per_device(): call(functools.partial(dense_body, n_col), [shape((part_h, nodes), BF16),...  2.03 us
    pallas_call x1, Pallas kernels, per_device(): call(mean_body, shape((width, nodes), BF16), 2, 3 + LOW, [pltpu.VMEM((wid...  1.28 us
  transfers between devices with their start and end apart: 17, of which 8 were waited for; matrix products, arithmetic and copies ran while one was open for 0% of the time, Pallas kernels for 20%

profile of v2, /device:TPU:0, one launch (start us, length us, event | category | flops | bytes accessed | tf_op | source)
XLA Modules:
  0.0 55.2 jit_solution(14436718483139054067)
XLA Ops:
  0.6 0.0 copy-start
  0.6 3.1 %collective-permute-start = (bf16[64,256]{1,0:T(8,128)(2,1)}, bf16[64,256]{1,0:T(8,128)(2,1)S(1)}, u32[]{:S(2)}, u32[]{:S(2)}) collective-permute-start(bf16[64,256]{1,0:T(8,128)(2,1)} %feat_ref.3), channel_id=1, source_target_pairs={{0,8},{2,10},{4,12},{6,14},{8,0},{10,2},{12,4},{14,6},{16,24},{18,... | collective-permute-start | bytes 98312 | tf_op jit(solution)/shard_map/ppermute | solution.py:279
  3.7 2.6 %collective-permute-start.1 = (bf16[64,256]{1,0:T(8,128)(2,1)}, bf16[64,256]{1,0:T(8,128)(2,1)S(1)}, u32[]{:S(2)}, u32[]{:S(2)}) collective-permute-start(bf16[64,256]{1,0:T(8,128)(2,1)} %feat_ref.3), channel_id=1, source_target_pairs={{0,16},{2,18},{4,20},{6,22},{8,24},{10,26},{12,28},{14,30},{16,0},... | collective-permute-start | bytes 98312 | tf_op jit(solution)/shard_map/ppermute | solution.py:279
  6.3 0.0 collective-permute-start.2
  6.3 0.0 copy-start.1
  6.3 0.8 %copy-done.1 = bf16[64,256]{1,0:T(8,128)(2,1)S(1)} copy-done((bf16[64,256]{1,0:T(8,128)(2,1)S(1)}, bf16[64,256]{1,0:T(8,128)(2,1)}, u32[]{:S(2)}) %copy-start.1) | copy-done | bytes 32792
  7.1 0.0 copy-start.3
  7.1 0.8 %copy-done.3 = bf16[128,256]{1,0:T(8,128)(2,1)S(1)} copy-done((bf16[128,256]{1,0:T(8,128)(2,1)S(1)}, bf16[128,256]{1,0:T(8,128)(2,1)}, u32[]{:S(2)}) %copy-start.3) | copy-done | bytes 65560
  8.0 0.0 copy-start.5
  8.0 0.8 %copy-done.5 = bf16[64,256]{1,0:T(8,128)(2,1)S(1)} copy-done((bf16[64,256]{1,0:T(8,128)(2,1)S(1)}, bf16[64,256]{1,0:T(8,128)(2,1)}, u32[]{:S(2)}) %copy-start.5) | copy-done | bytes 32792
  8.7 0.8 %copy-done.7 = bf16[64,256]{1,0:T(8,128)(2,1)S(1)} copy-done((bf16[64,256]{1,0:T(8,128)(2,1)S(1)}, bf16[64,256]{1,0:T(8,128)(2,1)}, u32[]{:S(2)}) %copy-start.7) | copy-done | bytes 32792
  9.5 0.7 %copy-done.13 = f32[128]{0:T(128)S(1)} copy-done((f32[128]{0:T(128)S(1)}, f32[128]{0:T(128)}, u32[]{:S(2)}) %copy-start.13) | copy-done | bytes 536
  10.2 1.7 %collective-permute-start.7 = (bf16[336,256]{1,0:T(8,128)(2,1)S(1)}, bf16[336,256]{1,0:T(8,128)(2,1)S(1)}, u32[]{:S(2)}, u32[]{:S(2)}) collective-permute-start(bf16[336,256]{1,0:T(8,128)(2,1)S(1)} %shard_map.141), channel_id=1, source_target_pairs={{0,1},{1,0},{2,3},{3,2},{4,5},{5,4},{6,7},{7,6},{8,9},{9,8},{10,11... | collective-permute-start | bytes 516104 | tf_op jit(solution)/shard_map/ppermute | solution.py:289
  11.9 0.0 collective-permute-done.refs_1_
  11.9 0.0 collective-permute-done.1.refs_2_
  11.9 0.3 collective-permute-done.2.refs_3_
  12.3 0.0 copy-start.10
  12.3 0.0 copy-start.11
  12.3 0.1 collective-permute-start.3
  12.4 1.6 %collective-permute-start.4 = (bf16[256,256]{1,0:T(8,128)(2,1)S(1)}, bf16[256,256]{1,0:T(8,128)(2,1)S(1)}, u32[]{:S(2)}, u32[]{:S(2)}) collective-permute-start(bf16[256,256]{1,0:T(8,128)(2,1)S(1)} %shard_map.139.refs_0_), channel_id=1, source_target_pairs={{0,4},{2,6},{4,0},{6,2},{8,12},{10,14},{12,8},{14,10},{16,20},{18,... | collective-permute-start | bytes 393224 | tf_op jit(solution)/shard_map/ppermute | solution.py:279
  13.9 0.3 collective-permute-start.5
  14.2 0.0 copy-done
  14.2 0.0 copy-done.9
  14.2 0.0 copy-done.10
  14.2 0.0 copy-done.11
  14.2 5.0 %shard_map.137 = (bf16[1024,256]{1,0:T(8,128)(2,1)S(1)}, f32[64,256]{1,0:T(8,128)S(1)}) custom-call(s32[16]{0:T(128)S(1)} %copy-done.11, s32[16,256]{1,0:T(8,128)S(1)} %copy-done.9, s32[1,256]{1,0:T(1,128)S(1)} %bitcast.3, bf16[64,4096]{1,0:T(8,128)(2,1)S(1)} %copy-done), custom_call_target="tpu_custom_call" | custom-call | flops 67108864 | bytes 8388608 | tf_op jit(solution)/shard_map/pallas_call | solution.py:308
  19.2 4.9 %shard_map.138 = (bf16[1024,256]{1,0:T(8,128)(2,1)S(1)}, f32[64,256]{1,0:T(8,128)S(1)}) custom-call(s32[16]{0:T(128)S(1)} %copy-done.11, s32[16,256]{1,0:T(8,128)S(1)} %copy-done.9, s32[1,256]{1,0:T(1,128)S(1)} %bitcast.4, bf16[64,4096]{1,0:T(8,128)(2,1)S(1)} %copy-done, bf16[1024,256]{1,0:T(8,128)(2,1)S(1)} %get-tuple-element.23.refs_0_, ...), custom_call_target="tpu_custom_call" | custom-call | flops 67108864 | bytes 8388608 | tf_op jit(solution)/shard_map/pallas_call | solution.py:308
  24.2 0.0 collective-permute-done.3.refs_1_
  24.2 0.0 collective-permute-done.4.refs_2_
  24.2 0.0 collective-permute-done.5.refs_3_
  24.2 0.0 copy-start.12
  24.2 0.6 %copy-done.12 = s32[16]{0:T(128)S(1)} copy-done((s32[16]{0:T(128)S(1)}, s32[16]{0:T(128)}, u32[]{:S(2)}) %copy-start.12) | copy-done | bytes 88
  24.9 0.0 copy-start.14
  24.9 1.3 %shard_map.140.refs_0_ = bf16[64,256]{1,0:T(8,128)(2,1)S(1)} custom-call(s32[16]{0:T(128)S(1)} %copy-done.11, s32[16]{0:T(128)S(1)} %copy-done.12, s32[1,256]{1,0:T(1,128)S(1)} %bitcast.5, f32[64,256]{1,0:T(8,128)S(1)} %get-tuple-element.26.acc_ref, bf16[1024,256]{1,0:T(8,128)(2,1)S(1)} %get-tuple-element.25.listed_ref, ...), custom_call_target="tpu_custom_call" | custom-call | bytes 524288 | tf_op jit(solution)/shard_map/pallas_call | solution.py:324
  26.2 1.6 %collective-permute-start.6 = (bf16[64,256]{1,0:T(8,128)(2,1)S(1)}, bf16[64,256]{1,0:T(8,128)(2,1)S(1)}, u32[]{:S(2)}, u32[]{:S(2)}) collective-permute-start(bf16[64,256]{1,0:T(8,128)(2,1)S(1)} %shard_map.140.refs_0_), channel_id=1, source_target_pairs={{0,1},{1,0},{2,3},{3,2},{4,5},{5,4},{6,7},{7,6},{8,9},{9,8},{10,11... | collective-permute-start | bytes 98312 | tf_op jit(solution)/shard_map/ppermute | solution.py:289
  27.7 0.0 collective-permute-done.7.refs_2_
  27.7 2.4 %collective-permute-done.6.refs_1_ = bf16[64,256]{1,0:T(8,128)(2,1)S(1)} collective-permute-done((bf16[64,256]{1,0:T(8,128)(2,1)S(1)}, bf16[64,256]{1,0:T(8,128)(2,1)S(1)}, u32[]{:S(2)}, u32[]{:S(2)}) %collective-permute-start.6) | collective-permute-done | bytes 32800 | tf_op jit(solution)/shard_map/ppermute | solution.py:289
  30.1 0.0 copy-done.2
  30.1 0.0 copy-done.4
  30.1 0.0 copy-done.6
  30.2 0.0 copy-done.8
  30.2 0.0 copy-done.14
  30.2 2.0 %shard_map.142 = (bf16[128,256]{1,0:T(8,128)(2,1)}, f32[64,256]{1,0:T(8,128)S(1)}, bf16[112,256]{1,0:T(8,128)(2,1)S(1)}, bf16[112,256]{1,0:T(8,128)(2,1)S(1)}, b...) custom-call(s32[16]{0:T(128)S(1)} %copy-done.12, s32[1,256]{1,0:T(1,128)S(1)} %bitcast.6, ...), custom_call_target="tpu_custom_call" | custom-call | flops 83886080 | bytes 458752 | tf_op jit(solution)/shard_map/pallas_call | solution.py:336
  32.2 0.3 collective-permute-start.10
  32.5 1.4 %collective-permute-start.8 = (bf16[112,256]{1,0:T(8,128)(2,1)S(1)}, bf16[112,256]{1,0:T(8,128)(2,1)S(1)}, u32[]{:S(2)}, u32[]{:S(2)}) collective-permute-start(bf16[112,256]{1,0:T(8,128)(2,1)S(1)} %get-tuple-element.30), channel_id=1, source_target_pairs={{0,2},{2,0},{4,6},{6,4},{8,10},{10,8},{12,14},{14,12},{16,18},{18,... | collective-permute-start | bytes 172040 | tf_op jit(solution)/shard_map/ppermute | solution.py:279
  33.9 0.5 collective-permute-start.9
  34.3 2.0 %collective-permute-done.10.refs_3_ = bf16[112,256]{1,0:T(8,128)(2,1)S(1)} collective-permute-done((bf16[112,256]{1,0:T(8,128)(2,1)S(1)}, bf16[112,256]{1,0:T(8,128)(2,1)S(1)}, u32[]{:S(2)}, u32[]{:S(2)}) %collective-permute-start.10) | collective-permute-done | bytes 57376 | tf_op jit(solution)/shard_map/ppermute | solution.py:279
  36.3 0.0 collective-permute-done.8.refs_1_
  36.3 1.7 %collective-permute-done.9.refs_2_ = bf16[112,256]{1,0:T(8,128)(2,1)S(1)} collective-permute-done((bf16[112,256]{1,0:T(8,128)(2,1)S(1)}, bf16[112,256]{1,0:T(8,128)(2,1)S(1)}, u32[]{:S(2)}, u32[]{:S(2)}) %collective-permute-start.9) | collective-permute-done | bytes 57376 | tf_op jit(solution)/shard_map/ppermute | solution.py:279
  38.1 0.1 shard_map.143.refs_0_
  38.1 0.4 collective-permute-start.11
  38.6 3.5 %collective-permute-start.12 = (bf16[112,256]{1,0:T(8,128)(2,1)S(1)}, bf16[112,256]{1,0:T(8,128)(2,1)S(1)}, u32[]{:S(2)}, u32[]{:S(2)}) collective-permute-start(bf16[112,256]{1,0:T(8,128)(2,1)S(1)} %shard_map.143.refs_0_), channel_id=1, source_target_pairs={{0,16},{2,18},{4,20},{6,22},{8,24},{10,26},{12,28},{14,30},{16,0},... | collective-permute-start | bytes 172040 | tf_op jit(solution)/shard_map/ppermute | solution.py:279
  42.0 0.5 collective-permute-start.13
  42.6 0.0 collective-permute-done.11.refs_1_
  42.6 1.6 %collective-permute-done.12.refs_2_ = bf16[112,256]{1,0:T(8,128)(2,1)S(1)} collective-permute-done((bf16[112,256]{1,0:T(8,128)(2,1)S(1)}, bf16[112,256]{1,0:T(8,128)(2,1)S(1)}, u32[]{:S(2)}, u32[]{:S(2)}) %collective-permute-start.12) | collective-permute-done | bytes 57376 | tf_op jit(solution)/shard_map/ppermute | solution.py:279
  44.2 3.8 %collective-permute-done.13.refs_3_ = bf16[112,256]{1,0:T(8,128)(2,1)S(1)} collective-permute-done((bf16[112,256]{1,0:T(8,128)(2,1)S(1)}, bf16[112,256]{1,0:T(8,128)(2,1)S(1)}, u32[]{:S(2)}, u32[]{:S(2)}) %collective-permute-start.13) | collective-permute-done | bytes 57376 | tf_op jit(solution)/shard_map/ppermute | solution.py:279
  48.0 1.1 %shard_map.144 = (f32[1,128]{1,0:T(1,128)}, bf16[96,256]{1,0:T(8,128)(2,1)S(1)}, bf16[96,256]{1,0:T(8,128)(2,1)S(1)}, bf16[96,256]{1,0:T(8,128)(2,1)S(1)}, bf16[96,256]{1,0:T(8,128)(2,1)S(1)}) custom-call(s32[16]{0:T(128)S(1)} %copy-done.11, bf16[112,256]{1,0:T(8,128)(2,1)S(1)} %shard_map.143.refs_0_, bf16[112,256]{1,0:T(8,128)(2,1)S(1)} %collective-permute-done.11.refs_1_, ...), custom_call_target="tpu_custom_call" | custom-call | bytes 229376 | tf_op jit(solution)/shard_map/pallas_call | solution.py:360
  49.1 0.0 collective-permute-start.14
  49.1 0.5 collective-permute-start.15
  49.7 1.3 %collective-permute-start.16 = (bf16[96,256]{1,0:T(8,128)(2,1)S(1)}, bf16[96,256]{1,0:T(8,128)(2,1)S(1)}, u32[]{:S(2)}, u32[]{:S(2)}) collective-permute-start(bf16[96,256]{1,0:T(8,128)(2,1)S(1)} %get-tuple-element.36), channel_id=1, source_target_pairs={{0,6},{2,4},{4,2},{6,0},{8,14},{10,12},{12,10},{14,8},{16,22},{18,... | collective-permute-start | bytes 147464 | tf_op jit(solution)/shard_map/ppermute | solution.py:279
  51.0 0.0 collective-permute-done.14.refs_1_
  51.0 2.7 %collective-permute-done.15.refs_2_ = bf16[96,256]{1,0:T(8,128)(2,1)S(1)} collective-permute-done((bf16[96,256]{1,0:T(8,128)(2,1)S(1)}, bf16[96,256]{1,0:T(8,128)(2,1)S(1)}, u32[]{:S(2)}, u32[]{:S(2)}) %collective-permute-start.15) | collective-permute-done | bytes 49184 | tf_op jit(solution)/shard_map/ppermute | solution.py:279
  53.7 0.3 collective-permute-done.16.refs_3_
  54.0 1.3 %shard_map.145 = (bf16[64,256]{1,0:T(8,128)(2,1)}, f32[64,256]{1,0:T(8,128)}, f32[64,256]{1,0:T(8,128)}) custom-call(s32[16]{0:T(128)S(1)} %copy-done.11, f32[64,256]{1,0:T(8,128)S(1)} %get-tuple-element.28.own_ref, bf16[96,256]{1,0:T(8,128)(2,1)S(1)} %get-tuple-element.33.refs_0_, bf16[96,256]{1,0:T(8,128)(2,1)S(1)} %collective-permute-done.14.refs_1_, ...), custom_call_target="tpu_custom_call" | custom-call | bytes 196608 | tf_op jit(solution)/shard_map/pallas_call | solution.py:372
  (9 shorter events, 0.0 us)
Async XLA Ops:
  0.6 13.6 %copy-start = (bf16[64,4096]{1,0:T(8,128)(2,1)S(1)}, bf16[64,4096]{1,0:T(8,128)(2,1)}, u32[]{:S(2)}) copy-start(bf16[64,4096]{1,0:T(8,128)(2,1)} %cache_ref.3) | copy-start | bytes 1572868
  0.6 11.3 %collective-permute-start = (bf16[64,256]{1,0:T(8,128)(2,1)}, bf16[64,256]{1,0:T(8,128)(2,1)S(1)}, u32[]{:S(2)}, u32[]{:S(2)}) collective-permute-start(bf16[64,256]{1,0:T(8,128)(2,1)} %feat_ref.3), channel_id=1, source_target_pairs={{0,8},{2,10},{4,12},{6,14},{8,0},{10,2},{12,4},{14,6},{16,24},{18,... | collective-permute-start | bytes 98312 | tf_op jit(solution)/shard_map/ppermute | solution.py:279
  3.7 8.2 %collective-permute-start.1 = (bf16[64,256]{1,0:T(8,128)(2,1)}, bf16[64,256]{1,0:T(8,128)(2,1)S(1)}, u32[]{:S(2)}, u32[]{:S(2)}) collective-permute-start(bf16[64,256]{1,0:T(8,128)(2,1)} %feat_ref.3), channel_id=1, source_target_pairs={{0,16},{2,18},{4,20},{6,22},{8,24},{10,26},{12,28},{14,30},{16,0},... | collective-permute-start | bytes 98312 | tf_op jit(solution)/shard_map/ppermute | solution.py:279
  6.3 5.9 %collective-permute-start.2 = (bf16[64,256]{1,0:T(8,128)(2,1)}, bf16[64,256]{1,0:T(8,128)(2,1)S(1)}, u32[]{:S(2)}, u32[]{:S(2)}) collective-permute-start(bf16[64,256]{1,0:T(8,128)(2,1)} %feat_ref.3), channel_id=1, source_target_pairs={{0,24},{2,26},{4,28},{6,30},{8,16},{10,18},{12,20},{14,22},{16,8},... | collective-permute-start | bytes 98312 | tf_op jit(solution)/shard_map/ppermute | solution.py:279
  6.3 0.8 %copy-start.1 = (bf16[64,256]{1,0:T(8,128)(2,1)S(1)}, bf16[64,256]{1,0:T(8,128)(2,1)}, u32[]{:S(2)}) copy-start(bf16[64,256]{1,0:T(8,128)(2,1)} %feat_ref.3) | copy-start | bytes 98308
  7.1 0.8 %copy-start.3 = (bf16[128,256]{1,0:T(8,128)(2,1)S(1)}, bf16[128,256]{1,0:T(8,128)(2,1)}, u32[]{:S(2)}) copy-start(bf16[128,256]{1,0:T(8,128)(2,1)} %cot_ref.3) | copy-start | bytes 196612
  8.0 0.8 %copy-start.5 = (bf16[64,256]{1,0:T(8,128)(2,1)S(1)}, bf16[64,256]{1,0:T(8,128)(2,1)}, u32[]{:S(2)}) copy-start(bf16[64,256]{1,0:T(8,128)(2,1)} %self_ref.3) | copy-start | bytes 98308
  8.7 0.8 %copy-start.7 = (bf16[64,256]{1,0:T(8,128)(2,1)S(1)}, bf16[64,256]{1,0:T(8,128)(2,1)}, u32[]{:S(2)}) copy-start(bf16[64,256]{1,0:T(8,128)(2,1)} %nbr_ref.7) | copy-start | bytes 98308
  9.5 0.7 %copy-start.13 = (f32[128]{0:T(128)S(1)}, f32[128]{0:T(128)}, u32[]{:S(2)}) copy-start(f32[128]{0:T(128)} %param.18) | copy-start | bytes 1540
  10.2 4.0 %copy-start.9 = (s32[16,256]{1,0:T(8,128)S(1)}, s32[16,256]{1,0:T(8,128)}, u32[]{:S(2)}) copy-start(s32[16,256]{1,0:T(8,128)} %nbr_ref.5) | copy-start | bytes 49156
  10.2 17.5 %collective-permute-start.7 = (bf16[336,256]{1,0:T(8,128)(2,1)S(1)}, bf16[336,256]{1,0:T(8,128)(2,1)S(1)}, u32[]{:S(2)}, u32[]{:S(2)}) collective-permute-start(bf16[336,256]{1,0:T(8,128)(2,1)S(1)} %shard_map.141), channel_id=1, source_target_pairs={{0,1},{1,0},{2,3},{3,2},{4,5},{5,4},{6,7},{7,6},{8,9},{9,8},{10,11... | collective-permute-start | bytes 516104 | tf_op jit(solution)/shard_map/ppermute | solution.py:289
  12.3 2.0 %copy-start.10 = (s32[256]{0:T(256)S(1)}, s32[256]{0:T(256)}, u32[]{:S(2)}) copy-start(s32[256]{0:T(256)} %param.15) | copy-start | bytes 3076
  12.3 2.0 %copy-start.11 = (s32[16]{0:T(128)S(1)}, s32[16]{0:T(128)}, u32[]{:S(2)}) copy-start(s32[16]{0:T(128)} %stale_ref.9) | copy-start | bytes 196
  12.3 11.9 %collective-permute-start.3 = (bf16[256,256]{1,0:T(8,128)(2,1)S(1)}, bf16[256,256]{1,0:T(8,128)(2,1)S(1)}, u32[]{:S(2)}, u32[]{:S(2)}) collective-permute-start(bf16[256,256]{1,0:T(8,128)(2,1)S(1)} %shard_map.139.refs_0_), channel_id=1, source_target_pairs={{0,2},{2,0},{4,6},{6,4},{8,10},{10,8},{12,14},{14,12},{16,18},{18,... | collective-permute-start | bytes 393224 | tf_op jit(solution)/shard_map/ppermute | solution.py:279
  12.4 11.8 %collective-permute-start.4 = (bf16[256,256]{1,0:T(8,128)(2,1)S(1)}, bf16[256,256]{1,0:T(8,128)(2,1)S(1)}, u32[]{:S(2)}, u32[]{:S(2)}) collective-permute-start(bf16[256,256]{1,0:T(8,128)(2,1)S(1)} %shard_map.139.refs_0_), channel_id=1, source_target_pairs={{0,4},{2,6},{4,0},{6,2},{8,12},{10,14},{12,8},{14,10},{16,20},{18,... | collective-permute-start | bytes 393224 | tf_op jit(solution)/shard_map/ppermute | solution.py:279
  13.9 10.2 %collective-permute-start.5 = (bf16[256,256]{1,0:T(8,128)(2,1)S(1)}, bf16[256,256]{1,0:T(8,128)(2,1)S(1)}, u32[]{:S(2)}, u32[]{:S(2)}) collective-permute-start(bf16[256,256]{1,0:T(8,128)(2,1)S(1)} %shard_map.139.refs_0_), channel_id=1, source_target_pairs={{0,6},{2,4},{4,2},{6,0},{8,14},{10,12},{12,10},{14,8},{16,22},{18,... | collective-permute-start | bytes 393224 | tf_op jit(solution)/shard_map/ppermute | solution.py:279
  24.2 0.7 %copy-start.12 = (s32[16]{0:T(128)S(1)}, s32[16]{0:T(128)}, u32[]{:S(2)}) copy-start(s32[16]{0:T(128)} %counts_ref.3) | copy-start | bytes 196
  24.8 5.3 %copy-start.2 = (bf16[64,256]{1,0:T(8,128)(2,1)S(1)}, bf16[64,256]{1,0:T(8,128)(2,1)}, u32[]{:S(2)}) copy-start(bf16[64,256]{1,0:T(8,128)(2,1)} %feat_ref.3) | copy-start | bytes 98308
  24.9 5.3 %copy-start.4 = (bf16[128,256]{1,0:T(8,128)(2,1)S(1)}, bf16[128,256]{1,0:T(8,128)(2,1)}, u32[]{:S(2)}) copy-start(bf16[128,256]{1,0:T(8,128)(2,1)} %cot_ref.3) | copy-start | bytes 196612
  24.9 5.3 %copy-start.6 = (bf16[64,256]{1,0:T(8,128)(2,1)S(1)}, bf16[64,256]{1,0:T(8,128)(2,1)}, u32[]{:S(2)}) copy-start(bf16[64,256]{1,0:T(8,128)(2,1)} %self_ref.3) | copy-start | bytes 98308
  24.9 5.3 %copy-start.8 = (bf16[64,256]{1,0:T(8,128)(2,1)S(1)}, bf16[64,256]{1,0:T(8,128)(2,1)}, u32[]{:S(2)}) copy-start(bf16[64,256]{1,0:T(8,128)(2,1)} %nbr_ref.7) | copy-start | bytes 98308
  24.9 5.3 %copy-start.14 = (f32[128]{0:T(128)S(1)}, f32[128]{0:T(128)}, u32[]{:S(2)}) copy-start(f32[128]{0:T(128)} %param.18) | copy-start | bytes 1540
  26.2 4.0 %collective-permute-start.6 = (bf16[64,256]{1,0:T(8,128)(2,1)S(1)}, bf16[64,256]{1,0:T(8,128)(2,1)S(1)}, u32[]{:S(2)}, u32[]{:S(2)}) collective-permute-start(bf16[64,256]{1,0:T(8,128)(2,1)S(1)} %shard_map.140.refs_0_), channel_id=1, source_target_pairs={{0,1},{1,0},{2,3},{3,2},{4,5},{5,4},{6,7},{7,6},{8,9},{9,8},{10,11... | collective-permute-start | bytes 98312 | tf_op jit(solution)/shard_map/ppermute | solution.py:289
  32.2 4.1 %collective-permute-start.10 = (bf16[112,256]{1,0:T(8,128)(2,1)S(1)}, bf16[112,256]{1,0:T(8,128)(2,1)S(1)}, u32[]{:S(2)}, u32[]{:S(2)}) collective-permute-start(bf16[112,256]{1,0:T(8,128)(2,1)S(1)} %get-tuple-element.32), channel_id=1, source_target_pairs={{0,6},{2,4},{4,2},{6,0},{8,14},{10,12},{12,10},{14,8},{16,22},{18,... | collective-permute-start | bytes 172040 | tf_op jit(solution)/shard_map/ppermute | solution.py:279
  32.5 3.8 %collective-permute-start.8 = (bf16[112,256]{1,0:T(8,128)(2,1)S(1)}, bf16[112,256]{1,0:T(8,128)(2,1)S(1)}, u32[]{:S(2)}, u32[]{:S(2)}) collective-permute-start(bf16[112,256]{1,0:T(8,128)(2,1)S(1)} %get-tuple-element.30), channel_id=1, source_target_pairs={{0,2},{2,0},{4,6},{6,4},{8,10},{10,8},{12,14},{14,12},{16,18},{18,... | collective-permute-start | bytes 172040 | tf_op jit(solution)/shard_map/ppermute | solution.py:279
  33.9 4.2 %collective-permute-start.9 = (bf16[112,256]{1,0:T(8,128)(2,1)S(1)}, bf16[112,256]{1,0:T(8,128)(2,1)S(1)}, u32[]{:S(2)}, u32[]{:S(2)}) collective-permute-start(bf16[112,256]{1,0:T(8,128)(2,1)S(1)} %get-tuple-element.31), channel_id=1, source_target_pairs={{0,4},{2,6},{4,0},{6,2},{8,12},{10,14},{12,8},{14,10},{16,20},{18,... | collective-permute-start | bytes 172040 | tf_op jit(solution)/shard_map/ppermute | solution.py:279
  38.1 4.5 %collective-permute-start.11 = (bf16[112,256]{1,0:T(8,128)(2,1)S(1)}, bf16[112,256]{1,0:T(8,128)(2,1)S(1)}, u32[]{:S(2)}, u32[]{:S(2)}) collective-permute-start(bf16[112,256]{1,0:T(8,128)(2,1)S(1)} %shard_map.143.refs_0_), channel_id=1, source_target_pairs={{0,8},{2,10},{4,12},{6,14},{8,0},{10,2},{12,4},{14,6},{16,24},{18,... | collective-permute-start | bytes 172040 | tf_op jit(solution)/shard_map/ppermute | solution.py:279
  38.6 5.6 %collective-permute-start.12 = (bf16[112,256]{1,0:T(8,128)(2,1)S(1)}, bf16[112,256]{1,0:T(8,128)(2,1)S(1)}, u32[]{:S(2)}, u32[]{:S(2)}) collective-permute-start(bf16[112,256]{1,0:T(8,128)(2,1)S(1)} %shard_map.143.refs_0_), channel_id=1, source_target_pairs={{0,16},{2,18},{4,20},{6,22},{8,24},{10,26},{12,28},{14,30},{16,0},... | collective-permute-start | bytes 172040 | tf_op jit(solution)/shard_map/ppermute | solution.py:279
  42.0 6.0 %collective-permute-start.13 = (bf16[112,256]{1,0:T(8,128)(2,1)S(1)}, bf16[112,256]{1,0:T(8,128)(2,1)S(1)}, u32[]{:S(2)}, u32[]{:S(2)}) collective-permute-start(bf16[112,256]{1,0:T(8,128)(2,1)S(1)} %shard_map.143.refs_0_), channel_id=1, source_target_pairs={{0,24},{2,26},{4,28},{6,30},{8,16},{10,18},{12,20},{14,22},{16,8},... | collective-permute-start | bytes 172040 | tf_op jit(solution)/shard_map/ppermute | solution.py:279
  49.1 1.9 %collective-permute-start.14 = (bf16[96,256]{1,0:T(8,128)(2,1)S(1)}, bf16[96,256]{1,0:T(8,128)(2,1)S(1)}, u32[]{:S(2)}, u32[]{:S(2)}) collective-permute-start(bf16[96,256]{1,0:T(8,128)(2,1)S(1)} %get-tuple-element.34), channel_id=1, source_target_pairs={{0,2},{2,0},{4,6},{6,4},{8,10},{10,8},{12,14},{14,12},{16,18},{18,... | collective-permute-start | bytes 147464 | tf_op jit(solution)/shard_map/ppermute | solution.py:279
  49.1 4.5 %collective-permute-start.15 = (bf16[96,256]{1,0:T(8,128)(2,1)S(1)}, bf16[96,256]{1,0:T(8,128)(2,1)S(1)}, u32[]{:S(2)}, u32[]{:S(2)}) collective-permute-start(bf16[96,256]{1,0:T(8,128)(2,1)S(1)} %get-tuple-element.35), channel_id=1, source_target_pairs={{0,4},{2,6},{4,0},{6,2},{8,12},{10,14},{12,8},{14,10},{16,20},{18,... | collective-permute-start | bytes 147464 | tf_op jit(solution)/shard_map/ppermute | solution.py:279
  49.7 4.3 %collective-permute-start.16 = (bf16[96,256]{1,0:T(8,128)(2,1)S(1)}, bf16[96,256]{1,0:T(8,128)(2,1)S(1)}, u32[]{:S(2)}, u32[]{:S(2)}) collective-permute-start(bf16[96,256]{1,0:T(8,128)(2,1)S(1)} %get-tuple-element.36), channel_id=1, source_target_pairs={{0,6},{2,4},{4,2},{6,0},{8,14},{10,12},{12,10},{14,8},{16,22},{18,... | collective-permute-start | bytes 147464 | tf_op jit(solution)/shard_map/ppermute | solution.py:279

commit v3 on v2

v3 whole, which is shorter than its diff:
```python
import functools

import jax
import jax.numpy as jnp
from jax import lax
from jax.experimental import pallas as pl
from jax.experimental.pallas import tpu as pltpu
from jax.sharding import PartitionSpec as P

LIMIT = 8
LANES = 128
LOW = 4
BF16 = jnp.bfloat16
F32 = jnp.float32
SMEM = pl.BlockSpec(memory_space=pltpu.SMEM)
VMEM = pl.BlockSpec(memory_space=pltpu.VMEM)
PARAMS = pltpu.CompilerParams(vmem_limit_bytes=32 * 1024 * 1024)


def call(body, outs, smem_count, vmem_count, scratch=(), flops=0, moved=0):
    return pl.pallas_call(
        body,
        out_shape=outs,
        in_specs=[SMEM] * smem_count + [VMEM] * vmem_count,
        out_specs=jax.tree.map(lambda _: VMEM, outs),
        scratch_shapes=list(scratch),
        compiler_params=PARAMS,
        cost_estimate=pl.CostEstimate(flops=flops, bytes_accessed=moved, transcendentals=0),
    )


def up16(rows):
    return -(-rows // 16) * 16


def is_fresh(stale_ref, part):
    return stale_ref[part] >= LIMIT


def fill_ranks(stale_ref, ranks):
    rank = jnp.int32(0)
    for p in range(stale_ref.shape[0]):
        ranks[p] = jnp.minimum(rank, stale_ref.shape[0] // 4 - 1)
        rank += is_fresh(stale_ref, p).astype(jnp.int32)


def split3(x):
    high = x.astype(BF16).astype(F32)
    mid = (x - high).astype(BF16).astype(F32)
    return high, mid, x - high - mid


def count_body(start, stale_ref, *refs):
    if start:
        nbr_ref, deg_ref, cache_ref, before, share, listed_ref, acc_ref, all_ref = refs
    else:
        counts_ref, nbr_ref, deg_ref, cache_ref, listed_ref, acc_ref, scale_ref, all_ref = refs
    slots, nodes = nbr_ref.shape
    listed = listed_ref.shape[0] // nodes
    parts = all_ref.shape[0] // nodes
    used = lax.broadcasted_iota(jnp.int32, (slots, nodes), 0) < deg_ref[...]
    index = jnp.where(used, nbr_ref[...], -1)
    tall = 16
    if start:
        listed_ref[...] = before[...]
    else:
        listed_ref[...] = jnp.zeros_like(listed_ref)
        live = (
            lax.broadcasted_iota(jnp.int32, (1, nodes), 1) < counts_ref[lax.axis_index("dom")]
        ).astype(F32)
        scale_ref[0:8, :] = jnp.broadcast_to(live, (8, nodes))
        scale_ref[8:16, :] = jnp.broadcast_to(live / deg_ref[...].astype(F32), (8, nodes))

    def per_part(part, rank):
        fresh = is_fresh(stale_ref, start + part)
        local = index - (start + part) * nodes
        local = jnp.where((local >= 0) & (local < nodes), local, -1).astype(F32)
        rows = [jnp.broadcast_to(local[k : k + 1, :], (tall, nodes)).astype(BF16) for k in range(slots)]
        for top in range(0, nodes, tall):
            place = (lax.broadcasted_iota(jnp.int32, (tall, nodes), 0) + top).astype(F32).astype(BF16)
            total = jnp.zeros((tall, nodes), BF16)
            for k in range(slots):
                total = total + jnp.where(rows[k] == place, BF16(1), BF16(0))
            all_ref[pl.ds(pl.multiple_of(part * nodes + top, tall), tall), :] = total
        block = pl.ds(pl.multiple_of(part * nodes, nodes), nodes)

        @pl.when(fresh)
        def _():
            to = pl.multiple_of(jnp.minimum(rank, listed - 1) * nodes, nodes)
            listed_ref[pl.ds(to, nodes), :] = all_ref[block, :]
            all_ref[block, :] = jnp.zeros((nodes, nodes), BF16)

        return rank + fresh.astype(jnp.int32)

    first = sum([is_fresh(stale_ref, p).astype(jnp.int32) for p in range(start)], jnp.int32(0))
    lax.fori_loop(0, parts, per_part, first)
    own = jnp.dot(
        cache_ref[:, start * nodes : (start + parts) * nodes], all_ref[...], preferred_element_type=F32
    )
    acc_ref[...] = share[...] + own if start else own


def pack_body(feat_ref, self_ref, nbr_ref, cot_ref, bias_ref, out_ref, bias, wide, sems):
    row = 0
    copies = []
    for i, ref in enumerate((feat_ref, self_ref, nbr_ref, cot_ref)):
        copies.append(pltpu.make_async_copy(ref, out_ref.at[row : row + ref.shape[0], :], sems.at[i]))
        row += ref.shape[0]
    copies.append(pltpu.make_async_copy(bias_ref, bias, sems.at[4]))
    for copy in copies:
        copy.start()
    wide[...] = jnp.zeros_like(wide)
    copies[4].wait()
    for i, term in enumerate(split3(bias[...])):
        wide[i : i + 1, : bias.shape[1]] = term
    out_ref[row:, :] = wide[...].astype(BF16)
    for copy in copies[:4]:
        copy.wait()


def stack_body(*refs):
    ins, out_ref = refs[:-1], refs[-1]
    rows = ins[0].shape[0]
    for i, ref in enumerate(ins):
        out_ref[i * rows : (i + 1) * rows, :] = ref[...]


def mean_body(stale_ref, scale_ref, acc_ref, listed_ref, *refs):
    stacks, (out_ref, blocks, ranks) = refs[:LOW], refs[LOW:]
    width, nodes = acc_ref.shape
    me = lax.axis_index("dom")
    fill_ranks(stale_ref, ranks)
    for low in range(LOW):
        for high in range(stacks[0].shape[0] // width):
            part = jnp.bitwise_xor(me, low + LOW * high)

            @pl.when(is_fresh(stale_ref, part))
            def _(low=low, high=high, part=part):
                blocks[ranks[part]] = stacks[low][high * width : (high + 1) * width, :]

    total = acc_ref[...]
    for r in range(blocks.shape[0]):
        total += jnp.dot(
            blocks[r], listed_ref[r * nodes : (r + 1) * nodes, :], preferred_element_type=F32
        )
    out_ref[...] = (total * scale_ref[8:9, :]).astype(BF16)


def dense_body(n_col, scale_ref, listed_ref, feat_ref, self_ref, nbr_ref, bias_ref, cot_ref, *refs):
    aggs, packs, refs = refs[:n_col], refs[n_col : 2 * n_col - 1], refs[2 * n_col - 1 :]
    act_ref, own_ref, slots, (cot_full, bias_full, full, wide) = refs[0], refs[1], refs[2 : 2 + LOW], refs[2 + LOW :]
    width, nodes = feat_ref.shape
    part_h = cot_ref.shape[0]
    hidden = part_h * n_col
    me = lax.axis_index("col")
    live, weight = scale_ref[0:1, :], scale_ref[8:9, :]
    pre = jnp.zeros((hidden, nodes), F32)
    for s in range(n_col):
        if s == 0:
            feat, w_self, w_nbr, cot, bias = feat_ref[...], self_ref[...], nbr_ref[...], cot_ref[...], bias_ref[...]
        else:
            pack = packs[s - 1]
            feat, w_self, w_nbr = [pack[i * width : (i + 1) * width, :] for i in range(3)]
            cot = pack[3 * width : 3 * width + part_h, :]
            terms = pack[3 * width + part_h :, :].astype(F32)
            bias = (terms[0:1] + terms[1:2] + terms[2:3])[:, :part_h]
        rows = pl.ds(pl.multiple_of(lax.rem(me + n_col - s, n_col) * part_h, part_h), part_h)
        cot_full[rows, :] = cot.astype(F32)
        bias_full[rows, :] = jnp.broadcast_to(bias, (LANES, part_h)).T
        for w, x in ((w_self, feat), (w_nbr, aggs[s][...])):
            pre += jnp.dot(w.astype(F32).T.astype(BF16), x, preferred_element_type=F32)
    pre += jnp.concatenate([bias_full[...]] * (nodes // LANES), 1)
    sig = 1.0 / (1.0 + jnp.exp(-pre))
    full[...] = live * pre * sig
    own_rows = pl.ds(pl.multiple_of(me * part_h, part_h), part_h)
    act_ref[...] = full[own_rows, :].astype(BF16)
    grad = (live * cot_full[...] * sig * (1.0 + pre * (1.0 - sig))).astype(BF16)
    cot_full[...] = grad.astype(F32)
    back = jnp.dot(nbr_ref[...], grad, preferred_element_type=F32)
    own_ref[...] = jnp.dot(self_ref[...], grad, preferred_element_type=F32)
    spread = (weight * back.astype(BF16).astype(F32)).astype(BF16)
    contrib = lax.dot_general(
        spread, listed_ref[...], (((1,), (1,)), ((), ())), preferred_element_type=F32
    )
    wgrads = [
        lax.dot_general(x[...], grad, (((1,), (1,)), ((), ())), preferred_element_type=F32)
        for x in (feat_ref, aggs[0])
    ]
    ones = jnp.ones((16, nodes), BF16)
    bias = lax.dot_general(
        ones, cot_full[own_rows, :].astype(BF16), (((1,), (1,)), ((), ())), preferred_element_type=F32
    )[:1]
    high = bias.astype(BF16).astype(F32)
    listed = listed_ref.shape[0] // nodes
    half, short = width // 2, width // LOW
    base = listed * short + half
    for q in range(LOW):
        for r in range(listed):
            wide[q, r * short : (r + 1) * short, :] = contrib[
                q * short : (q + 1) * short, r * nodes : (r + 1) * nodes
            ]
        wide[q, base - half : base, :] = wgrads[q // 2][q % 2 * half : (q % 2 + 1) * half, :]
        wide[q, base:, :] = jnp.zeros((wide.shape[1] - base, nodes), F32)
        wide[q, base : base + 1, :part_h] = high
        wide[q, base + 1 : base + 2, :part_h] = bias - high
    low = lax.axis_index("dom") % LOW
    for m in range(LOW):
        slots[m][...] = wide[jnp.bitwise_xor(low, m)].astype(BF16)


def group_sum_body(base, *refs):
    got, (out_ref, wide, full) = refs[:LOW], refs[LOW:]
    low = lax.axis_index("dom") % LOW
    for m in range(LOW):
        wide[jnp.bitwise_xor(low, m)] = got[m][...].astype(F32)
    total = wide[0] + wide[1] + wide[2] + wide[3]
    full[...] = total
    bias = total[base : base + 1] + total[base + 1 : base + 2]
    high = bias.astype(BF16).astype(F32)
    full[base : base + 1, :] = high
    full[base + 1 : base + 2, :] = bias - high
    out_ref[...] = full[...].astype(BF16)


def line_sum_body(base, width, count, stale_ref, *refs):
    got, bias_ref, outs = refs[:count], refs[count], refs[count + 1 : count + 1 + LOW]
    wide, kept, piece, ranks = refs[count + 1 + LOW :]
    me = lax.axis_index("dom")
    place = me // LOW
    for m in range(count):
        wide[jnp.bitwise_xor(place, m)] = got[m][...].astype(F32)
    total = wide[0]
    for m in range(1, count):
        total += wide[m]
    bias_ref[...] = (total[base : base + 1] + total[base + 1 : base + 2])[:, : bias_ref.shape[1]]
    half, short = width // 2, width // LOW
    for r in range(kept.shape[0]):
        kept[r] = total[r * short : (r + 1) * short]
    piece[...] = jnp.zeros_like(piece)
    piece[short : short + half, :] = total[base - half : base]
    fill_ranks(stale_ref, ranks)
    for m in range(LOW):
        piece[:short, :] = kept[ranks[jnp.bitwise_xor(me, m)]]
        outs[m][...] = piece[...].astype(BF16)


def last_body(stale_ref, own_ref, *refs):
    got, (feat_ref, self_ref, nbr_ref, wide, back) = refs[:LOW], refs[LOW:]
    width = own_ref.shape[0]
    me = lax.axis_index("dom")
    low = me % LOW
    half, short = width // 2, width // LOW
    for m in range(LOW):
        wide[jnp.bitwise_xor(low, m)] = got[m][...].astype(F32)
    fresh = is_fresh(stale_ref, me).astype(F32)
    for q in range(LOW):
        back[q * short : (q + 1) * short, :] = wide[q, :short]
        ref = nbr_ref if q // 2 else self_ref
        ref[q % 2 * half : (q % 2 + 1) * half, :] = wide[q, short : short + half]
    feat_ref[...] = (own_ref[...] + fresh * back[...]).astype(BF16)


def per_device(
    n_col,
    features,
    cached_embed,
    staleness,
    node_counts,
    neighbours,
    degrees,
    w_self,
    w_nbr,
    sage_bias,
    cotangent,
):
    width, nodes = features.shape
    hidden = w_self.shape[1]
    dom = staleness.shape[0]
    listed = dom // 4
    part_h = cotangent.shape[0]
    shape = jax.ShapeDtypeStruct

    def hop(block, m):
        return lax.ppermute(block, "dom", [(i, i ^ m) for i in range(dom)])

    def along(block):
        return [block] + [hop(block, m) for m in range(LOW, dom, LOW)]

    def within(slots):
        return [slots[0]] + [hop(slots[m], m) for m in range(1, LOW)]

    def around(block):
        return [
            lax.ppermute(block, "col", [(i, (i + s) % n_col) for i in range(n_col)])
            for s in range(1, n_col)
        ]

    line = along(features)
    bias_row = sage_bias.reshape(1, part_h)
    packed = pl.pallas_call(
        pack_body,
        out_shape=shape((3 * width + part_h + 16, nodes), BF16),
        in_specs=[pl.BlockSpec(memory_space=pltpu.HBM)] * 5,
        out_specs=VMEM,
        scratch_shapes=[
            pltpu.VMEM((1, part_h), F32),
            pltpu.VMEM((16, nodes), F32),
            pltpu.SemaphoreType.DMA((5,)),
        ],
        compiler_params=PARAMS,
        cost_estimate=pl.CostEstimate(
            flops=0, bytes_accessed=4 * (3 * width + part_h) * nodes, transcendentals=0
        ),
    )(features, w_self, w_nbr, cotangent, bias_row)
    packs = around(packed)
    deg = degrees.reshape(1, nodes)
    half_parts = dom // 2

    sums = (shape((listed * nodes, nodes), BF16), shape((width, nodes), F32))
    counting = dict(
        scratch=[pltpu.VMEM((half_parts * nodes, nodes), BF16)],
        flops=2 * width * half_parts * nodes * nodes,
        moved=half_parts * nodes * nodes * 16,
    )
    before, share, scale = call(
        functools.partial(count_body, 0), sums + (shape((16, nodes), F32),), 2, 3, **counting
    )(staleness, node_counts, neighbours, deg, cached_embed)
    *others, before = lax.optimization_barrier((*line[1:], before))
    line = line[:1] + others
    stacked = call(stack_body, shape((width * len(line), nodes), BF16), 0, len(line), moved=4 * dom * width * nodes // LOW)(
        *line
    )
    stacks = within([stacked] * LOW)
    counts, acc = call(functools.partial(count_body, half_parts), sums, 1, 5, **counting)(
        staleness, neighbours, deg, cached_embed, before, share
    )
    agg = call(
        mean_body,
        shape((width, nodes), BF16),
        1,
        3 + LOW,
        [pltpu.VMEM((listed, width, nodes), BF16), pltpu.SMEM((dom,), jnp.int32)],
        moved=2 * dom * width * nodes,
    )(staleness, scale, acc, counts, *stacks)
    aggs = [agg] + around(agg)
    base = listed * (width // LOW) + width // 2
    rows = up16(base + 2)
    act, own, *slots = call(
        functools.partial(dense_body, n_col),
        [shape((part_h, nodes), BF16), shape((width, nodes), F32)] + [shape((rows, nodes), BF16)] * LOW,
        0,
        7 + 2 * n_col - 1,
        [
            pltpu.VMEM((hidden, nodes), F32),
            pltpu.VMEM((hidden, LANES), F32),
            pltpu.VMEM((hidden, nodes), F32),
            pltpu.VMEM((LOW, rows, nodes), F32),
        ],
        flops=2 * width * nodes * (hidden * 6 + listed * nodes),
        moved=4 * LOW * rows * nodes,
    )(scale, counts, features, w_self, w_nbr, bias_row, cotangent, *aggs, *packs)
    summed = call(
        functools.partial(group_sum_body, base),
        shape((rows, nodes), BF16),
        0,
        LOW,
        [pltpu.VMEM((LOW, rows, nodes), F32), pltpu.VMEM((rows, nodes), F32)],
        moved=2 * LOW * rows * nodes,
    )(*within(slots))
    lines = along(summed)
    tall = up16(width // LOW + width // 2)
    bias, *pieces = call(
        functools.partial(line_sum_body, base, width, len(lines)),
        [shape((1, part_h), F32)] + [shape((tall, nodes), BF16)] * LOW,
        1,
        len(lines),
        [
            pltpu.VMEM((len(lines), rows, nodes), F32),
            pltpu.VMEM((listed, width // LOW, nodes), F32),
            pltpu.VMEM((tall, nodes), F32),
            pltpu.SMEM((dom,), jnp.int32),
        ],
        moved=2 * len(lines) * rows * nodes,
    )(staleness, *lines)
    grad_feat, grad_self, grad_nbr = call(
        last_body,
        (shape((width, nodes), BF16), shape((width, hidden), F32), shape((width, hidden), F32)),
        1,
        1 + LOW,
        [pltpu.VMEM((LOW, tall, nodes), F32), pltpu.VMEM((width, nodes), F32)],
        moved=2 * LOW * tall * nodes,
    )(staleness, own, *within(pieces))
    return act, grad_feat, grad_self, grad_nbr, bias.reshape(-1)


def solution(mesh):
    placed = (
        P("col", "dom"),
        P("col", None),
        P(),
        P(),
        P(None, "dom"),
        P("dom"),
        P("col", None),
        P("col", None),
        P("col"),
        P("col", "dom"),
    )
    return jax.shard_map(
        functools.partial(per_device, mesh.shape["col"]),
        mesh=mesh,
        in_specs=placed,
        out_specs=(P("col", "dom"), P("col", "dom"), P("col", None), P("col", None), P("col")),
        check_vma=False,
    )
```

time: 55.6 us -> 53.4 us (0.960)
  Pallas kernels: 15.7 us -> 10.8 us
  waiting for transfers between devices: 14.8 us -> 18.9 us
  starting transfers between devices: 19.4 us -> 18.2 us
    pallas_call x5, Pallas kernels: 12.5 us -> 8.15 us  [the longest x1 2.88 us: per_device(): call(functools.partial(count_body, 0), sums + (shape((16, nodes), F32),),...]
    ppermute x15, waiting for transfers between devices: 12.4 us -> 15.5 us  [hop(): return lax.ppermute(block, 'dom', [(i, i ^ m) for i in range(dom)])]
    ppermute x2, starting transfers between devices: 3.3 us -> 2.4 us  [around(): lax.ppermute(block, 'col', [(i, (i + s) % n_col) for i in range(n_col)])]
    ppermute x2, waiting for transfers between devices: 2.42 us -> 3.32 us  [around(): lax.ppermute(block, 'col', [(i, (i + s) % n_col) for i in range(n_col)])]
  transfers between devices with their start and end apart: 17 -> 17, of which waited for: 8 -> 9; matrix products, arithmetic and copies ran while one was open for 0% -> 0% of each run, Pallas kernels for 20% -> 13%
where the time goes in v3:
time: 53.4 us; the launch traced here: 52.9 us
  waiting for transfers between devices  18.9 us (35%)
  starting transfers between devices  18.2 us (34%)
  Pallas kernels  10.8 us (20%)
  local copies, waits for them, and re-layouts  4.25 us (8%)
  between operations  0.78 us (1%)
    ppermute x15, starting transfers between devices, hop(): return lax.ppermute(block, 'dom', [(i, i ^ m) for i in range(dom)])  15.8 us
    ppermute x15, waiting for transfers between devices, hop(): return lax.ppermute(block, 'dom', [(i, i ^ m) for i in range(dom)])  15.5 us
    unnamed x30, local copies, waits for them, and re-layouts  4.25 us
    ppermute x2, waiting for transfers between devices, around(): lax.ppermute(block, 'col', [(i, (i + s) % n_col) for i in range(n_col)])  3.32 us
    pallas_call x1, Pallas kernels, per_device(): call(functools.partial(count_body, 0), sums + (shape((16, nodes), F32),),...  2.88 us
    pallas_call x1, Pallas kernels, per_device(): call(functools.partial(count_body, half_parts), sums, 1, 5, **counting)  2.83 us
    ppermute x2, starting transfers between devices, around(): lax.ppermute(block, 'col', [(i, (i + s) % n_col) for i in range(n_col)])  2.4 us
    pallas_call x1, Pallas kernels, per_device(): call(functools.partial(dense_body, n_col), [shape((part_h, nodes), BF16),...  1.48 us
  transfers between devices with their start and end apart: 17, of which 9 were waited for; matrix products, arithmetic and copies ran while one was open for 0% of the time, Pallas kernels for 13%

profile of v3, /device:TPU:0, one launch (start us, length us, event | category | flops | bytes accessed | tf_op | source)
XLA Modules:
  0.0 52.9 jit_solution(12253555175961577910)
XLA Ops:
  0.6 0.0 copy-start.13
  0.6 3.1 %collective-permute-start = (bf16[64,256]{1,0:T(8,128)(2,1)}, bf16[64,256]{1,0:T(8,128)(2,1)S(1)}, u32[]{:S(2)}, u32[]{:S(2)}) collective-permute-start(bf16[64,256]{1,0:T(8,128)(2,1)} %feat_ref.3), channel_id=1, source_target_pairs={{0,8},{2,10},{4,12},{6,14},{8,0},{10,2},{12,4},{14,6},{16,24},{18,... | collective-permute-start | bytes 98312 | tf_op jit(solution)/shard_map/ppermute | solution.py:284
  3.7 2.6 %collective-permute-start.1 = (bf16[64,256]{1,0:T(8,128)(2,1)}, bf16[64,256]{1,0:T(8,128)(2,1)S(1)}, u32[]{:S(2)}, u32[]{:S(2)}) collective-permute-start(bf16[64,256]{1,0:T(8,128)(2,1)} %feat_ref.3), channel_id=1, source_target_pairs={{0,16},{2,18},{4,20},{6,22},{8,24},{10,26},{12,28},{14,30},{16,0},... | collective-permute-start | bytes 98312 | tf_op jit(solution)/shard_map/ppermute | solution.py:284
  6.3 0.0 collective-permute-start.2
  6.3 0.0 copy-done.13
  6.3 0.0 copy-start.2
  6.3 0.8 %copy-done.2 = bf16[64,256]{1,0:T(8,128)(2,1)S(1)} copy-done((bf16[64,256]{1,0:T(8,128)(2,1)S(1)}, bf16[64,256]{1,0:T(8,128)(2,1)}, u32[]{:S(2)}) %copy-start.2) | copy-done | bytes 32792
  7.1 0.0 copy-start.4
  7.2 0.8 %copy-done.4 = bf16[128,256]{1,0:T(8,128)(2,1)S(1)} copy-done((bf16[128,256]{1,0:T(8,128)(2,1)S(1)}, bf16[128,256]{1,0:T(8,128)(2,1)}, u32[]{:S(2)}) %copy-start.4) | copy-done | bytes 65560
  8.0 0.0 copy-start.6
  8.0 0.8 %copy-done.6 = bf16[64,256]{1,0:T(8,128)(2,1)S(1)} copy-done((bf16[64,256]{1,0:T(8,128)(2,1)S(1)}, bf16[64,256]{1,0:T(8,128)(2,1)}, u32[]{:S(2)}) %copy-start.6) | copy-done | bytes 32792
  8.7 0.8 %copy-done.8 = bf16[64,256]{1,0:T(8,128)(2,1)S(1)} copy-done((bf16[64,256]{1,0:T(8,128)(2,1)S(1)}, bf16[64,256]{1,0:T(8,128)(2,1)}, u32[]{:S(2)}) %copy-start.8) | copy-done | bytes 32792
  9.5 0.3 shard_map.141
  9.8 0.0 copy-start.11
  9.8 0.0 copy-start.12
  9.8 1.7 %collective-permute-start.7 = (bf16[336,256]{1,0:T(8,128)(2,1)S(1)}, bf16[336,256]{1,0:T(8,128)(2,1)S(1)}, u32[]{:S(2)}, u32[]{:S(2)}) collective-permute-start(bf16[336,256]{1,0:T(8,128)(2,1)S(1)} %shard_map.141), channel_id=1, source_target_pairs={{0,1},{1,0},{2,3},{3,2},{4,5},{5,4},{6,7},{7,6},{8,9},{9,8},{10,11... | collective-permute-start | bytes 516104 | tf_op jit(solution)/shard_map/ppermute | solution.py:294
  11.6 0.0 copy-done.10
  11.6 0.0 copy-done.14
  11.6 0.0 copy-done.11
  11.6 0.0 copy-done.12
  11.6 0.0 copy-start
  11.6 1.0 %copy-done = bf16[64,4096]{1,0:T(8,128)(2,1)S(1)} copy-done((bf16[64,4096]{1,0:T(8,128)(2,1)S(1)}, bf16[64,4096]{1,0:T(8,128)(2,1)}, u32[]{:S(2)}) %copy-start) | copy-done | bytes 524312
  12.6 2.9 %shard_map.137 = (bf16[1024,256]{1,0:T(8,128)(2,1)S(1)}, f32[64,256]{1,0:T(8,128)S(1)}, f32[16,256]{1,0:T(8,128)S(1)}) custom-call(s32[16]{0:T(128)S(1)} %copy-done.11, s32[16]{0:T(128)S(1)} %copy-done.14, s32[16,256]{1,0:T(8,128)S(1)} %copy-done.10, s32[1,256]{1,0:T(1,128)S(1)} %bitcast.3, bf16[64,4096]{1,0:T(8,128)(2,1)S(1)} %copy-done), custom_call_target="tpu_custom_call" | custom-call | flops 67108864 | bytes 8388608 | tf_op jit(solution)/shard_map/pallas_call | solution.py:325
  15.5 0.0 collective-permute-done.refs_1_
  15.5 0.0 collective-permute-done.1.refs_2_
  15.5 0.0 collective-permute-done.2.refs_3_
  15.5 0.0 copy-done.3
  15.6 0.1 collective-permute-start.3
  15.6 1.6 %collective-permute-start.4 = (bf16[256,256]{1,0:T(8,128)(2,1)S(1)}, bf16[256,256]{1,0:T(8,128)(2,1)S(1)}, u32[]{:S(2)}, u32[]{:S(2)}) collective-permute-start(bf16[256,256]{1,0:T(8,128)(2,1)S(1)} %shard_map.139.refs_0_), channel_id=1, source_target_pairs={{0,4},{2,6},{4,0},{6,2},{8,12},{10,14},{12,8},{14,10},{16,20},{18,... | collective-permute-start | bytes 393224 | tf_op jit(solution)/shard_map/ppermute | solution.py:284
  17.2 0.3 collective-permute-start.5
  17.5 0.0 copy-done.1
  17.5 2.8 %shard_map.138 = (bf16[1024,256]{1,0:T(8,128)(2,1)S(1)}, f32[64,256]{1,0:T(8,128)S(1)}) custom-call(s32[16]{0:T(128)S(1)} %copy-done.11, s32[16,256]{1,0:T(8,128)S(1)} %copy-done.10, s32[1,256]{1,0:T(1,128)S(1)} %bitcast.4, bf16[64,4096]{1,0:T(8,128)(2,1)S(1)} %copy-done.1, bf16[1024,256]{1,0:T(8,128)(2,1)S(1)} %get-tuple-element.30.refs_3_, ...), custom_call_target="tpu_custom_call" | custom-call | flops 67108864 | bytes 8388608 | tf_op jit(solution)/shard_map/pallas_call | solution.py:334
  20.4 0.0 collective-permute-done.3.refs_1_
  20.4 1.6 %collective-permute-done.4.refs_2_ = bf16[256,256]{1,0:T(8,128)(2,1)S(1)} collective-permute-done((bf16[256,256]{1,0:T(8,128)(2,1)S(1)}, bf16[256,256]{1,0:T(8,128)(2,1)S(1)}, u32[]{:S(2)}, u32[]{:S(2)}) %collective-permute-start.4) | collective-permute-done | bytes 131104 | tf_op jit(solution)/shard_map/ppermute | solution.py:284
  22.0 1.9 %collective-permute-done.5.refs_3_ = bf16[256,256]{1,0:T(8,128)(2,1)S(1)} collective-permute-done((bf16[256,256]{1,0:T(8,128)(2,1)S(1)}, bf16[256,256]{1,0:T(8,128)(2,1)S(1)}, u32[]{:S(2)}, u32[]{:S(2)}) %collective-permute-start.5) | collective-permute-done | bytes 131104 | tf_op jit(solution)/shard_map/ppermute | solution.py:284
  23.9 0.9 %shard_map.140.refs_0_ = bf16[64,256]{1,0:T(8,128)(2,1)S(1)} custom-call(s32[16]{0:T(128)S(1)} %copy-done.11, f32[16,256]{1,0:T(8,128)S(1)} %get-tuple-element.28.scale_ref, f32[64,256]{1,0:T(8,128)S(1)} %get-tuple-element.33.acc_ref, bf16[1024,256]{1,0:T(8,128)(2,1)S(1)} %get-tuple-element.32.listed_ref, bf16[256,256]{1,0:T(8,128)(2,1)S(1)} %shard_map.139.refs_0_, ...), custom_call_target="tpu_custom_call" | custom-call | bytes 524288 | tf_op jit(solution)/shard_map/pallas_call | solution.py:337
  24.9 0.7 %collective-permute-start.6 = (bf16[64,256]{1,0:T(8,128)(2,1)S(1)}, bf16[64,256]{1,0:T(8,128)(2,1)S(1)}, u32[]{:S(2)}, u32[]{:S(2)}) collective-permute-start(bf16[64,256]{1,0:T(8,128)(2,1)S(1)} %shard_map.140.refs_0_), channel_id=1, source_target_pairs={{0,1},{1,0},{2,3},{3,2},{4,5},{5,4},{6,7},{7,6},{8,9},{9,8},{10,11... | collective-permute-start | bytes 98312 | tf_op jit(solution)/shard_map/ppermute | solution.py:294
  25.5 0.0 collective-permute-done.7.refs_2_
  25.5 3.3 %collective-permute-done.6.refs_1_ = bf16[64,256]{1,0:T(8,128)(2,1)S(1)} collective-permute-done((bf16[64,256]{1,0:T(8,128)(2,1)S(1)}, bf16[64,256]{1,0:T(8,128)(2,1)S(1)}, u32[]{:S(2)}, u32[]{:S(2)}) %collective-permute-start.6) | collective-permute-done | bytes 32800 | tf_op jit(solution)/shard_map/ppermute | solution.py:294
  28.8 0.0 copy-done.5
  28.8 0.0 copy-done.7
  28.9 0.0 copy-done.9
  28.9 1.5 %shard_map.142 = (bf16[128,256]{1,0:T(8,128)(2,1)}, f32[64,256]{1,0:T(8,128)S(1)}, bf16[112,256]{1,0:T(8,128)(2,1)S(1)}, bf16[112,256]{1,0:T(8,128)(2,1)S(1)}, b...) custom-call(f32[16,256]{1,0:T(8,128)S(1)} %get-tuple-element.28.scale_ref, ...), custom_call_target="tpu_custom_call" | custom-call | flops 83886080 | bytes 458752 | tf_op jit(solution)/shard_map/pallas_call | solution.py:348
  30.3 0.0 collective-permute-start.8
  30.3 1.5 %collective-permute-start.9 = (bf16[112,256]{1,0:T(8,128)(2,1)S(1)}, bf16[112,256]{1,0:T(8,128)(2,1)S(1)}, u32[]{:S(2)}, u32[]{:S(2)}) collective-permute-start(bf16[112,256]{1,0:T(8,128)(2,1)S(1)} %get-tuple-element.41), channel_id=1, source_target_pairs={{0,4},{2,6},{4,0},{6,2},{8,12},{10,14},{12,8},{14,10},{16,20},{18,... | collective-permute-start | bytes 172040 | tf_op jit(solution)/shard_map/ppermute | solution.py:284
  31.9 0.3 collective-permute-start.10
  32.2 0.0 collective-permute-done.8.refs_1_
  32.2 2.5 %collective-permute-done.9.refs_2_ = bf16[112,256]{1,0:T(8,128)(2,1)S(1)} collective-permute-done((bf16[112,256]{1,0:T(8,128)(2,1)S(1)}, bf16[112,256]{1,0:T(8,128)(2,1)S(1)}, u32[]{:S(2)}, u32[]{:S(2)}) %collective-permute-start.9) | collective-permute-done | bytes 57376 | tf_op jit(solution)/shard_map/ppermute | solution.py:284
  34.7 1.1 %collective-permute-done.10.refs_3_ = bf16[112,256]{1,0:T(8,128)(2,1)S(1)} collective-permute-done((bf16[112,256]{1,0:T(8,128)(2,1)S(1)}, bf16[112,256]{1,0:T(8,128)(2,1)S(1)}, u32[]{:S(2)}, u32[]{:S(2)}) %collective-permute-start.10) | collective-permute-done | bytes 57376 | tf_op jit(solution)/shard_map/ppermute | solution.py:284
  35.8 0.1 shard_map.143.refs_0_
  35.8 0.7 %collective-permute-start.11 = (bf16[112,256]{1,0:T(8,128)(2,1)S(1)}, bf16[112,256]{1,0:T(8,128)(2,1)S(1)}, u32[]{:S(2)}, u32[]{:S(2)}) collective-permute-start(bf16[112,256]{1,0:T(8,128)(2,1)S(1)} %shard_map.143.refs_0_), channel_id=1, source_target_pairs={{0,8},{2,10},{4,12},{6,14},{8,0},{10,2},{12,4},{14,6},{16,24},{18,... | collective-permute-start | bytes 172040 | tf_op jit(solution)/shard_map/ppermute | solution.py:284
  36.6 3.5 %collective-permute-start.12 = (bf16[112,256]{1,0:T(8,128)(2,1)S(1)}, bf16[112,256]{1,0:T(8,128)(2,1)S(1)}, u32[]{:S(2)}, u32[]{:S(2)}) collective-permute-start(bf16[112,256]{1,0:T(8,128)(2,1)S(1)} %shard_map.143.refs_0_), channel_id=1, source_target_pairs={{0,16},{2,18},{4,20},{6,22},{8,24},{10,26},{12,28},{14,30},{16,0},... | collective-permute-start | bytes 172040 | tf_op jit(solution)/shard_map/ppermute | solution.py:284
  40.1 0.2 collective-permute-start.13
  40.3 0.0 collective-permute-done.11.refs_1_
  40.3 3.4 %collective-permute-done.12.refs_2_ = bf16[112,256]{1,0:T(8,128)(2,1)S(1)} collective-permute-done((bf16[112,256]{1,0:T(8,128)(2,1)S(1)}, bf16[112,256]{1,0:T(8,128)(2,1)S(1)}, u32[]{:S(2)}, u32[]{:S(2)}) %collective-permute-start.12) | collective-permute-done | bytes 57376 | tf_op jit(solution)/shard_map/ppermute | solution.py:284
  43.7 2.4 %collective-permute-done.13.refs_3_ = bf16[112,256]{1,0:T(8,128)(2,1)S(1)} collective-permute-done((bf16[112,256]{1,0:T(8,128)(2,1)S(1)}, bf16[112,256]{1,0:T(8,128)(2,1)S(1)}, u32[]{:S(2)}, u32[]{:S(2)}) %collective-permute-start.13) | collective-permute-done | bytes 57376 | tf_op jit(solution)/shard_map/ppermute | solution.py:284
  46.0 1.1 %shard_map.144 = (f32[1,128]{1,0:T(1,128)}, bf16[48,256]{1,0:T(8,128)(2,1)S(1)}, bf16[48,256]{1,0:T(8,128)(2,1)S(1)}, bf16[48,256]{1,0:T(8,128)(2,1)S(1)}, bf16[48,256]{1,0:T(8,128)(2,1)S(1)}) custom-call(s32[16]{0:T(128)S(1)} %copy-done.11, bf16[112,256]{1,0:T(8,128)(2,1)S(1)} %shard_map.143.refs_0_, bf16[112,256]{1,0:T(8,128)(2,1)S(1)} %collective-permute-done.11.refs_1_, ...), custom_call_target="tpu_custom_call" | custom-call | bytes 229376 | tf_op jit(solution)/shard_map/pallas_call | solution.py:372
  47.2 0.0 collective-permute-start.14
  47.2 1.3 %collective-permute-start.15 = (bf16[48,256]{1,0:T(8,128)(2,1)S(1)}, bf16[48,256]{1,0:T(8,128)(2,1)S(1)}, u32[]{:S(2)}, u32[]{:S(2)}) collective-permute-start(bf16[48,256]{1,0:T(8,128)(2,1)S(1)} %get-tuple-element.45), channel_id=1, source_target_pairs={{0,4},{2,6},{4,0},{6,2},{8,12},{10,14},{12,8},{14,10},{16,20},{18,... | collective-permute-start | bytes 73736 | tf_op jit(solution)/shard_map/ppermute | solution.py:284
  48.4 0.6 %collective-permute-start.16 = (bf16[48,256]{1,0:T(8,128)(2,1)S(1)}, bf16[48,256]{1,0:T(8,128)(2,1)S(1)}, u32[]{:S(2)}, u32[]{:S(2)}) collective-permute-start(bf16[48,256]{1,0:T(8,128)(2,1)S(1)} %get-tuple-element.46), channel_id=1, source_target_pairs={{0,6},{2,4},{4,2},{6,0},{8,14},{10,12},{12,10},{14,8},{16,22},{18,... | collective-permute-start | bytes 73736 | tf_op jit(solution)/shard_map/ppermute | solution.py:284
  49.0 0.0 collective-permute-done.14.refs_1_
  49.0 2.0 %collective-permute-done.15.refs_2_ = bf16[48,256]{1,0:T(8,128)(2,1)S(1)} collective-permute-done((bf16[48,256]{1,0:T(8,128)(2,1)S(1)}, bf16[48,256]{1,0:T(8,128)(2,1)S(1)}, u32[]{:S(2)}, u32[]{:S(2)}) %collective-permute-start.15) | collective-permute-done | bytes 24608 | tf_op jit(solution)/shard_map/ppermute | solution.py:284
  51.0 0.7 %collective-permute-done.16.refs_3_ = bf16[48,256]{1,0:T(8,128)(2,1)S(1)} collective-permute-done((bf16[48,256]{1,0:T(8,128)(2,1)S(1)}, bf16[48,256]{1,0:T(8,128)(2,1)S(1)}, u32[]{:S(2)}, u32[]{:S(2)}) %collective-permute-start.16) | collective-permute-done | bytes 24608 | tf_op jit(solution)/shard_map/ppermute | solution.py:284
  51.7 1.2 %shard_map.145 = (bf16[64,256]{1,0:T(8,128)(2,1)}, f32[64,256]{1,0:T(8,128)}, f32[64,256]{1,0:T(8,128)}) custom-call(s32[16]{0:T(128)S(1)} %copy-done.11, f32[64,256]{1,0:T(8,128)S(1)} %get-tuple-element.38.own_ref, bf16[48,256]{1,0:T(8,128)(2,1)S(1)} %get-tuple-element.43.refs_0_, bf16[48,256]{1,0:T(8,128)(2,1)S(1)} %collective-permute-done.14.refs_1_, ...), custom_call_target="tpu_custom_call" | custom-call | bytes 98304 | tf_op jit(solution)/shard_map/pallas_call | solution.py:385
  (9 shorter events, 0.0 us)
Async XLA Ops:
  0.6 5.7 %copy-start.13 = (f32[128]{0:T(128)S(1)}, f32[128]{0:T(128)}, u32[]{:S(2)}) copy-start(f32[128]{0:T(128)} %param.18) | copy-start | bytes 1540
  0.6 14.9 %collective-permute-start = (bf16[64,256]{1,0:T(8,128)(2,1)}, bf16[64,256]{1,0:T(8,128)(2,1)S(1)}, u32[]{:S(2)}, u32[]{:S(2)}) collective-permute-start(bf16[64,256]{1,0:T(8,128)(2,1)} %feat_ref.3), channel_id=1, source_target_pairs={{0,8},{2,10},{4,12},{6,14},{8,0},{10,2},{12,4},{14,6},{16,24},{18,... | collective-permute-start | bytes 98312 | tf_op jit(solution)/shard_map/ppermute | solution.py:284
  3.7 11.8 %collective-permute-start.1 = (bf16[64,256]{1,0:T(8,128)(2,1)}, bf16[64,256]{1,0:T(8,128)(2,1)S(1)}, u32[]{:S(2)}, u32[]{:S(2)}) collective-permute-start(bf16[64,256]{1,0:T(8,128)(2,1)} %feat_ref.3), channel_id=1, source_target_pairs={{0,16},{2,18},{4,20},{6,22},{8,24},{10,26},{12,28},{14,30},{16,0},... | collective-permute-start | bytes 98312 | tf_op jit(solution)/shard_map/ppermute | solution.py:284
  6.3 9.2 %collective-permute-start.2 = (bf16[64,256]{1,0:T(8,128)(2,1)}, bf16[64,256]{1,0:T(8,128)(2,1)S(1)}, u32[]{:S(2)}, u32[]{:S(2)}) collective-permute-start(bf16[64,256]{1,0:T(8,128)(2,1)} %feat_ref.3), channel_id=1, source_target_pairs={{0,24},{2,26},{4,28},{6,30},{8,16},{10,18},{12,20},{14,22},{16,8},... | collective-permute-start | bytes 98312 | tf_op jit(solution)/shard_map/ppermute | solution.py:284
  6.3 0.8 %copy-start.2 = (bf16[64,256]{1,0:T(8,128)(2,1)S(1)}, bf16[64,256]{1,0:T(8,128)(2,1)}, u32[]{:S(2)}) copy-start(bf16[64,256]{1,0:T(8,128)(2,1)} %feat_ref.3) | copy-start | bytes 98308
  7.1 0.8 %copy-start.4 = (bf16[128,256]{1,0:T(8,128)(2,1)S(1)}, bf16[128,256]{1,0:T(8,128)(2,1)}, u32[]{:S(2)}) copy-start(bf16[128,256]{1,0:T(8,128)(2,1)} %cot_ref.3) | copy-start | bytes 196612
  8.0 0.8 %copy-start.6 = (bf16[64,256]{1,0:T(8,128)(2,1)S(1)}, bf16[64,256]{1,0:T(8,128)(2,1)}, u32[]{:S(2)}) copy-start(bf16[64,256]{1,0:T(8,128)(2,1)} %self_ref.3) | copy-start | bytes 98308
  8.7 0.8 %copy-start.8 = (bf16[64,256]{1,0:T(8,128)(2,1)S(1)}, bf16[64,256]{1,0:T(8,128)(2,1)}, u32[]{:S(2)}) copy-start(bf16[64,256]{1,0:T(8,128)(2,1)} %nbr_ref.3) | copy-start | bytes 98308
  9.5 2.1 %copy-start.10 = (s32[16,256]{1,0:T(8,128)S(1)}, s32[16,256]{1,0:T(8,128)}, u32[]{:S(2)}) copy-start(s32[16,256]{1,0:T(8,128)} %refs_0_.4) | copy-start | bytes 49156
  9.5 2.1 %copy-start.14 = (s32[16]{0:T(128)S(1)}, s32[16]{0:T(128)}, u32[]{:S(2)}) copy-start(s32[16]{0:T(128)} %refs_0_.3) | copy-start | bytes 196
  9.5 6.0 %copy-start.3 = (bf16[64,256]{1,0:T(8,128)(2,1)S(1)}, bf16[64,256]{1,0:T(8,128)(2,1)}, u32[]{:S(2)}) copy-start(bf16[64,256]{1,0:T(8,128)(2,1)} %feat_ref.3) | copy-start | bytes 98308
  9.8 1.8 %copy-start.11 = (s32[16]{0:T(128)S(1)}, s32[16]{0:T(128)}, u32[]{:S(2)}) copy-start(s32[16]{0:T(128)} %stale_ref.9) | copy-start | bytes 196
  9.8 1.8 %copy-start.12 = (s32[256]{0:T(256)S(1)}, s32[256]{0:T(256)}, u32[]{:S(2)}) copy-start(s32[256]{0:T(256)} %param.15) | copy-start | bytes 3076
  9.8 15.7 %collective-permute-start.7 = (bf16[336,256]{1,0:T(8,128)(2,1)S(1)}, bf16[336,256]{1,0:T(8,128)(2,1)S(1)}, u32[]{:S(2)}, u32[]{:S(2)}) collective-permute-start(bf16[336,256]{1,0:T(8,128)(2,1)S(1)} %shard_map.141), channel_id=1, source_target_pairs={{0,1},{1,0},{2,3},{3,2},{4,5},{5,4},{6,7},{7,6},{8,9},{9,8},{10,11... | collective-permute-start | bytes 516104 | tf_op jit(solution)/shard_map/ppermute | solution.py:294
  11.6 1.0 %copy-start = (bf16[64,4096]{1,0:T(8,128)(2,1)S(1)}, bf16[64,4096]{1,0:T(8,128)(2,1)}, u32[]{:S(2)}) copy-start(bf16[64,4096]{1,0:T(8,128)(2,1)} %refs_2_.1) | copy-start | bytes 1572868
  12.6 4.9 %copy-start.1 = (bf16[64,4096]{1,0:T(8,128)(2,1)S(1)}, bf16[64,4096]{1,0:T(8,128)(2,1)}, u32[]{:S(2)}) copy-start(bf16[64,4096]{1,0:T(8,128)(2,1)} %refs_2_.1) | copy-start | bytes 1572868
  15.6 4.8 %collective-permute-start.3 = (bf16[256,256]{1,0:T(8,128)(2,1)S(1)}, bf16[256,256]{1,0:T(8,128)(2,1)S(1)}, u32[]{:S(2)}, u32[]{:S(2)}) collective-permute-start(bf16[256,256]{1,0:T(8,128)(2,1)S(1)} %shard_map.139.refs_0_), channel_id=1, source_target_pairs={{0,2},{2,0},{4,6},{6,4},{8,10},{10,8},{12,14},{14,12},{16,18},{18,... | collective-permute-start | bytes 393224 | tf_op jit(solution)/shard_map/ppermute | solution.py:284
  15.6 6.4 %collective-permute-start.4 = (bf16[256,256]{1,0:T(8,128)(2,1)S(1)}, bf16[256,256]{1,0:T(8,128)(2,1)S(1)}, u32[]{:S(2)}, u32[]{:S(2)}) collective-permute-start(bf16[256,256]{1,0:T(8,128)(2,1)S(1)} %shard_map.139.refs_0_), channel_id=1, source_target_pairs={{0,4},{2,6},{4,0},{6,2},{8,12},{10,14},{12,8},{14,10},{16,20},{18,... | collective-permute-start | bytes 393224 | tf_op jit(solution)/shard_map/ppermute | solution.py:284
  17.2 6.7 %collective-permute-start.5 = (bf16[256,256]{1,0:T(8,128)(2,1)S(1)}, bf16[256,256]{1,0:T(8,128)(2,1)S(1)}, u32[]{:S(2)}, u32[]{:S(2)}) collective-permute-start(bf16[256,256]{1,0:T(8,128)(2,1)S(1)} %shard_map.139.refs_0_), channel_id=1, source_target_pairs={{0,6},{2,4},{4,2},{6,0},{8,14},{10,12},{12,10},{14,8},{16,22},{18,... | collective-permute-start | bytes 393224 | tf_op jit(solution)/shard_map/ppermute | solution.py:284
  23.9 4.9 %copy-start.5 = (bf16[128,256]{1,0:T(8,128)(2,1)S(1)}, bf16[128,256]{1,0:T(8,128)(2,1)}, u32[]{:S(2)}) copy-start(bf16[128,256]{1,0:T(8,128)(2,1)} %cot_ref.3) | copy-start | bytes 196612
  23.9 4.9 %copy-start.7 = (bf16[64,256]{1,0:T(8,128)(2,1)S(1)}, bf16[64,256]{1,0:T(8,128)(2,1)}, u32[]{:S(2)}) copy-start(bf16[64,256]{1,0:T(8,128)(2,1)} %self_ref.3) | copy-start | bytes 98308
  23.9 4.9 %copy-start.9 = (bf16[64,256]{1,0:T(8,128)(2,1)S(1)}, bf16[64,256]{1,0:T(8,128)(2,1)}, u32[]{:S(2)}) copy-start(bf16[64,256]{1,0:T(8,128)(2,1)} %nbr_ref.3) | copy-start | bytes 98308
  24.9 4.0 %collective-permute-start.6 = (bf16[64,256]{1,0:T(8,128)(2,1)S(1)}, bf16[64,256]{1,0:T(8,128)(2,1)S(1)}, u32[]{:S(2)}, u32[]{:S(2)}) collective-permute-start(bf16[64,256]{1,0:T(8,128)(2,1)S(1)} %shard_map.140.refs_0_), channel_id=1, source_target_pairs={{0,1},{1,0},{2,3},{3,2},{4,5},{5,4},{6,7},{7,6},{8,9},{9,8},{10,11... | collective-permute-start | bytes 98312 | tf_op jit(solution)/shard_map/ppermute | solution.py:294
  30.3 1.9 %collective-permute-start.8 = (bf16[112,256]{1,0:T(8,128)(2,1)S(1)}, bf16[112,256]{1,0:T(8,128)(2,1)S(1)}, u32[]{:S(2)}, u32[]{:S(2)}) collective-permute-start(bf16[112,256]{1,0:T(8,128)(2,1)S(1)} %get-tuple-element.40), channel_id=1, source_target_pairs={{0,2},{2,0},{4,6},{6,4},{8,10},{10,8},{12,14},{14,12},{16,18},{18,... | collective-permute-start | bytes 172040 | tf_op jit(solution)/shard_map/ppermute | solution.py:284
  30.3 4.3 %collective-permute-start.9 = (bf16[112,256]{1,0:T(8,128)(2,1)S(1)}, bf16[112,256]{1,0:T(8,128)(2,1)S(1)}, u32[]{:S(2)}, u32[]{:S(2)}) collective-permute-start(bf16[112,256]{1,0:T(8,128)(2,1)S(1)} %get-tuple-element.41), channel_id=1, source_target_pairs={{0,4},{2,6},{4,0},{6,2},{8,12},{10,14},{12,8},{14,10},{16,20},{18,... | collective-permute-start | bytes 172040 | tf_op jit(solution)/shard_map/ppermute | solution.py:284
  31.9 3.9 %collective-permute-start.10 = (bf16[112,256]{1,0:T(8,128)(2,1)S(1)}, bf16[112,256]{1,0:T(8,128)(2,1)S(1)}, u32[]{:S(2)}, u32[]{:S(2)}) collective-permute-start(bf16[112,256]{1,0:T(8,128)(2,1)S(1)} %get-tuple-element.42), channel_id=1, source_target_pairs={{0,6},{2,4},{4,2},{6,0},{8,14},{10,12},{12,10},{14,8},{16,22},{18,... | collective-permute-start | bytes 172040 | tf_op jit(solution)/shard_map/ppermute | solution.py:284
  35.8 4.5 %collective-permute-start.11 = (bf16[112,256]{1,0:T(8,128)(2,1)S(1)}, bf16[112,256]{1,0:T(8,128)(2,1)S(1)}, u32[]{:S(2)}, u32[]{:S(2)}) collective-permute-start(bf16[112,256]{1,0:T(8,128)(2,1)S(1)} %shard_map.143.refs_0_), channel_id=1, source_target_pairs={{0,8},{2,10},{4,12},{6,14},{8,0},{10,2},{12,4},{14,6},{16,24},{18,... | collective-permute-start | bytes 172040 | tf_op jit(solution)/shard_map/ppermute | solution.py:284
  36.6 7.1 %collective-permute-start.12 = (bf16[112,256]{1,0:T(8,128)(2,1)S(1)}, bf16[112,256]{1,0:T(8,128)(2,1)S(1)}, u32[]{:S(2)}, u32[]{:S(2)}) collective-permute-start(bf16[112,256]{1,0:T(8,128)(2,1)S(1)} %shard_map.143.refs_0_), channel_id=1, source_target_pairs={{0,16},{2,18},{4,20},{6,22},{8,24},{10,26},{12,28},{14,30},{16,0},... | collective-permute-start | bytes 172040 | tf_op jit(solution)/shard_map/ppermute | solution.py:284
  40.1 6.0 %collective-permute-start.13 = (bf16[112,256]{1,0:T(8,128)(2,1)S(1)}, bf16[112,256]{1,0:T(8,128)(2,1)S(1)}, u32[]{:S(2)}, u32[]{:S(2)}) collective-permute-start(bf16[112,256]{1,0:T(8,128)(2,1)S(1)} %shard_map.143.refs_0_), channel_id=1, source_target_pairs={{0,24},{2,26},{4,28},{6,30},{8,16},{10,18},{12,20},{14,22},{16,8},... | collective-permute-start | bytes 172040 | tf_op jit(solution)/shard_map/ppermute | solution.py:284
  47.2 1.9 %collective-permute-start.14 = (bf16[48,256]{1,0:T(8,128)(2,1)S(1)}, bf16[48,256]{1,0:T(8,128)(2,1)S(1)}, u32[]{:S(2)}, u32[]{:S(2)}) collective-permute-start(bf16[48,256]{1,0:T(8,128)(2,1)S(1)} %get-tuple-element.44), channel_id=1, source_target_pairs={{0,2},{2,0},{4,6},{6,4},{8,10},{10,8},{12,14},{14,12},{16,18},{18,... | collective-permute-start | bytes 73736 | tf_op jit(solution)/shard_map/ppermute | solution.py:284
  47.2 3.8 %collective-permute-start.15 = (bf16[48,256]{1,0:T(8,128)(2,1)S(1)}, bf16[48,256]{1,0:T(8,128)(2,1)S(1)}, u32[]{:S(2)}, u32[]{:S(2)}) collective-permute-start(bf16[48,256]{1,0:T(8,128)(2,1)S(1)} %get-tuple-element.45), channel_id=1, source_target_pairs={{0,4},{2,6},{4,0},{6,2},{8,12},{10,14},{12,8},{14,10},{16,20},{18,... | collective-permute-start | bytes 73736 | tf_op jit(solution)/shard_map/ppermute | solution.py:284
  48.4 3.3 %collective-permute-start.16 = (bf16[48,256]{1,0:T(8,128)(2,1)S(1)}, bf16[48,256]{1,0:T(8,128)(2,1)S(1)}, u32[]{:S(2)}, u32[]{:S(2)}) collective-permute-start(bf16[48,256]{1,0:T(8,128)(2,1)S(1)} %get-tuple-element.46), channel_id=1, source_target_pairs={{0,6},{2,4},{4,2},{6,0},{8,14},{10,12},{12,10},{14,8},{16,22},{18,... | collective-permute-start | bytes 73736 | tf_op jit(solution)/shard_map/ppermute | solution.py:284

commit v4 on v3

--- a/solution.py
+++ b/solution.py
@@ -14,17 +14,19 @@
 F32 = jnp.float32
 SMEM = pl.BlockSpec(memory_space=pltpu.SMEM)
 VMEM = pl.BlockSpec(memory_space=pltpu.VMEM)
+HBM = pl.BlockSpec(memory_space=pltpu.HBM)
 PARAMS = pltpu.CompilerParams(vmem_limit_bytes=32 * 1024 * 1024)
-
-
-def call(body, outs, smem_count, vmem_count, scratch=(), flops=0, moved=0):
+WHOLE = pltpu.CompilerParams(vmem_limit_bytes=60 * 1024 * 1024)
+
+
+def call(body, outs, smem_count, vmem_count, scratch=(), flops=0, moved=0, hbm_count=0):
     return pl.pallas_call(
         body,
         out_shape=outs,
-        in_specs=[SMEM] * smem_count + [VMEM] * vmem_count,
+        in_specs=[SMEM] * smem_count + [HBM] * hbm_count + [VMEM] * vmem_count,
         out_specs=jax.tree.map(lambda _: VMEM, outs),
         scratch_shapes=list(scratch),
-        compiler_params=PARAMS,
+        compiler_params=WHOLE if hbm_count else PARAMS,
         cost_estimate=pl.CostEstimate(flops=flops, bytes_accessed=moved, transcendentals=0),
     )
 
@@ -50,30 +52,21 @@
     return high, mid, x - high - mid
 
 
-def count_body(start, stale_ref, *refs):
-    if start:
-        nbr_ref, deg_ref, cache_ref, before, share, listed_ref, acc_ref, all_ref = refs
-    else:
-        counts_ref, nbr_ref, deg_ref, cache_ref, listed_ref, acc_ref, scale_ref, all_ref = refs
+def count_body(stale_ref, counts_ref, nbr_ref, deg_ref, cache_ref, listed_ref, acc_ref, scale_ref, all_ref):
     slots, nodes = nbr_ref.shape
     listed = listed_ref.shape[0] // nodes
-    parts = all_ref.shape[0] // nodes
     used = lax.broadcasted_iota(jnp.int32, (slots, nodes), 0) < deg_ref[...]
     index = jnp.where(used, nbr_ref[...], -1)
     tall = 16
-    if start:
-        listed_ref[...] = before[...]
-    else:
-        listed_ref[...] = jnp.zeros_like(listed_ref)
-        live = (
-            lax.broadcasted_iota(jnp.int32, (1, nodes), 1) < counts_ref[lax.axis_index("dom")]
-        ).astype(F32)
-        scale_ref[0:8, :] = jnp.broadcast_to(live, (8, nodes))
-        scale_ref[8:16, :] = jnp.broadcast_to(live / deg_ref[...].astype(F32), (8, nodes))
+    live = (
+        lax.broadcasted_iota(jnp.int32, (1, nodes), 1) < counts_ref[lax.axis_index("dom")]
+    ).astype(F32)
+    scale_ref[0:8, :] = jnp.broadcast_to(live, (8, nodes))
+    scale_ref[8:16, :] = jnp.broadcast_to(live / deg_ref[...].astype(F32), (8, nodes))
 
     def per_part(part, rank):
-        fresh = is_fresh(stale_ref, start + part)
-        local = index - (start + part) * nodes
+        fresh = is_fresh(stale_ref, part)
+        local = index - part * nodes
         local = jnp.where((local >= 0) & (local < nodes), local, -1).astype(F32)
         rows = [jnp.broadcast_to(local[k : k + 1, :], (tall, nodes)).astype(BF16) for k in range(slots)]
         for top in range(0, nodes, tall):
@@ -92,12 +85,8 @@
 
         return rank + fresh.astype(jnp.int32)
 
-    first = sum([is_fresh(stale_ref, p).astype(jnp.int32) for p in range(start)], jnp.int32(0))
-    lax.fori_loop(0, parts, per_part, first)
-    own = jnp.dot(
-        cache_ref[:, start * nodes : (start + parts) * nodes], all_ref[...], preferred_element_type=F32
-    )
-    acc_ref[...] = share[...] + own if start else own
+    lax.fori_loop(0, stale_ref.shape[0], per_part, jnp.int32(0))
+    acc_ref[...] = jnp.dot(cache_ref[...], all_ref[...], preferred_element_type=F32)
 
 
 def pack_body(feat_ref, self_ref, nbr_ref, cot_ref, bias_ref, out_ref, bias, wide, sems):
@@ -232,7 +221,7 @@
     total = wide[0]
     for m in range(1, count):
         total += wide[m]
-    bias_ref[...] = (total[base : base + 1] + total[base + 1 : base + 2])[:, : bias_ref.shape[1]]
+    bias_ref[...] = jnp.broadcast_to(total[base : base + 1] + total[base + 1 : base + 2], bias_ref.shape)
     half, short = width // 2, width // LOW
     for r in range(kept.shape[0]):
         kept[r] = total[r * short : (r + 1) * short]
@@ -244,8 +233,10 @@
         outs[m][...] = piece[...].astype(BF16)
 
 
-def last_body(stale_ref, own_ref, *refs):
-    got, (feat_ref, self_ref, nbr_ref, wide, back) = refs[:LOW], refs[LOW:]
+def last_body(stale_ref, act_ref, bias_ref, own_ref, *refs):
+    got, (act_out, feat_ref, self_ref, nbr_ref, bias_out, wide, back) = refs[:LOW], refs[LOW:]
+    act_out[...] = act_ref[...]
+    bias_out[...] = bias_ref[:1, : bias_out.shape[1]]
     width = own_ref.shape[0]
     me = lax.axis_index("dom")
     low = me % LOW
@@ -297,43 +288,30 @@
 
     line = along(features)
     bias_row = sage_bias.reshape(1, part_h)
-    packed = pl.pallas_call(
+    packed = call(
         pack_body,
-        out_shape=shape((3 * width + part_h + 16, nodes), BF16),
-        in_specs=[pl.BlockSpec(memory_space=pltpu.HBM)] * 5,
-        out_specs=VMEM,
-        scratch_shapes=[
-            pltpu.VMEM((1, part_h), F32),
-            pltpu.VMEM((16, nodes), F32),
-            pltpu.SemaphoreType.DMA((5,)),
-        ],
-        compiler_params=PARAMS,
-        cost_estimate=pl.CostEstimate(
-            flops=0, bytes_accessed=4 * (3 * width + part_h) * nodes, transcendentals=0
-        ),
+        shape((3 * width + part_h + 16, nodes), BF16),
+        0,
+        0,
+        [pltpu.VMEM((1, part_h), F32), pltpu.VMEM((16, nodes), F32), pltpu.SemaphoreType.DMA((5,))],
+        moved=4 * (3 * width + part_h) * nodes,
+        hbm_count=5,
     )(features, w_self, w_nbr, cotangent, bias_row)
     packs = around(packed)
     deg = degrees.reshape(1, nodes)
-    half_parts = dom // 2
-
-    sums = (shape((listed * nodes, nodes), BF16), shape((width, nodes), F32))
-    counting = dict(
-        scratch=[pltpu.VMEM((half_parts * nodes, nodes), BF16)],
-        flops=2 * width * half_parts * nodes * nodes,
-        moved=half_parts * nodes * nodes * 16,
-    )
-    before, share, scale = call(
-        functools.partial(count_body, 0), sums + (shape((16, nodes), F32),), 2, 3, **counting
-    )(staleness, node_counts, neighbours, deg, cached_embed)
-    *others, before = lax.optimization_barrier((*line[1:], before))
-    line = line[:1] + others
     stacked = call(stack_body, shape((width * len(line), nodes), BF16), 0, len(line), moved=4 * dom * width * nodes // LOW)(
         *line
     )
     stacks = within([stacked] * LOW)
-    counts, acc = call(functools.partial(count_body, half_parts), sums, 1, 5, **counting)(
-        staleness, neighbours, deg, cached_embed, before, share
-    )
+    counts, acc, scale = call(
+        count_body,
+        (shape((listed * nodes, nodes), BF16), shape((width, nodes), F32), shape((16, nodes), F32)),
+        2,
+        3,
+        [pltpu.VMEM((dom * nodes, nodes), BF16)],
+        flops=2 * width * dom * nodes * nodes,
+        moved=dom * nodes * nodes * 16,
+    )(staleness, node_counts, neighbours, deg, cached_embed)
     agg = call(
         mean_body,
         shape((width, nodes), BF16),
@@ -371,7 +349,7 @@
     tall = up16(width // LOW + width // 2)
     bias, *pieces = call(
         functools.partial(line_sum_body, base, width, len(lines)),
-        [shape((1, part_h), F32)] + [shape((tall, nodes), BF16)] * LOW,
+        [shape((8, nodes), F32)] + [shape((tall, nodes), BF16)] * LOW,
         1,
         len(lines),
         [
@@ -382,14 +360,20 @@
         ],
         moved=2 * len(lines) * rows * nodes,
     )(staleness, *lines)
-    grad_feat, grad_self, grad_nbr = call(
+    act, grad_feat, grad_self, grad_nbr, bias = call(
         last_body,
-        (shape((width, nodes), BF16), shape((width, hidden), F32), shape((width, hidden), F32)),
+        (
+            shape((part_h, nodes), BF16),
+            shape((width, nodes), BF16),
+            shape((width, hidden), F32),
+            shape((width, hidden), F32),
+            shape((1, part_h), F32),
+        ),
         1,
-        1 + LOW,
+        3 + LOW,
         [pltpu.VMEM((LOW, tall, nodes), F32), pltpu.VMEM((width, nodes), F32)],
         moved=2 * LOW * tall * nodes,
-    )(staleness, own, *within(pieces))
+    )(staleness, act, bias, own, *within(pieces))
     return act, grad_feat, grad_self, grad_nbr, bias.reshape(-1)
 
 

time: 53.4 us -> 47.5 us (0.89)
  local copies, waits for them, and re-layouts: 4.25 us -> 0.8 us
  waiting for transfers between devices: 18.9 us -> 15.6 us
  starting transfers between devices: 18.2 us -> 19.5 us
    unnamed x30 -> x22, local copies, waits for them, and re-layouts: 4.25 us -> 0.8 us
    ppermute x15, waiting for transfers between devices: 15.5 us -> 13.2 us  [hop(): return lax.ppermute(block, 'dom', [(i, i ^ m) for i in range(dom)])]
    ppermute x2, starting transfers between devices: 2.4 us -> 3.33 us  [around(): lax.ppermute(block, 'col', [(i, (i + s) % n_col) for i in range(n_col)])]
    ppermute x2, waiting for transfers between devices: 3.32 us -> 2.42 us  [around(): lax.ppermute(block, 'col', [(i, (i + s) % n_col) for i in range(n_col)])]
    pallas_call x5 -> x4, Pallas kernels: 8.34 us -> 8.46 us  [the longest x1 4.99 us: per_device(): call(count_body, (shape((listed * nodes, nodes), BF16), shape((width, nod...]
  transfers between devices with their start and end apart: 17 -> 17, of which waited for: 9 -> 9; matrix products, arithmetic and copies ran while one was open for 0% -> 0% of each run, Pallas kernels for 13% -> 16%
where the time goes in v4:
time: 47.5 us; the launch traced here: 47.3 us
  starting transfers between devices  19.5 us (41%)
  waiting for transfers between devices  15.6 us (33%)
  Pallas kernels  10.6 us (22%)
  local copies, waits for them, and re-layouts  0.8 us (2%)
  between operations  0.8 us (2%)
    ppermute x15, starting transfers between devices, hop(): return lax.ppermute(block, 'dom', [(i, i ^ m) for i in range(dom)])  16.2 us
    ppermute x15, waiting for transfers between devices, hop(): return lax.ppermute(block, 'dom', [(i, i ^ m) for i in range(dom)])  13.2 us
    pallas_call x1, Pallas kernels, per_device(): call(count_body, (shape((listed * nodes, nodes), BF16), shape((width, nod...  4.99 us
    ppermute x2, starting transfers between devices, around(): lax.ppermute(block, 'col', [(i, (i + s) % n_col) for i in range(n_col)])  3.33 us
    ppermute x2, waiting for transfers between devices, around(): lax.ppermute(block, 'col', [(i, (i + s) % n_col) for i in range(n_col)])  2.42 us
    pallas_call x1, Pallas kernels, per_device(): call(pack_body, shape((3 * width + part_h + 16, nodes), BF16), 0, 0, [plt...  1.61 us
    pallas_call x1, Pallas kernels, per_device(): call(last_body, (shape((part_h, nodes), BF16), shape((width, nodes), BF16...  1.25 us
    pallas_call x1, Pallas kernels, per_device(): call(functools.partial(dense_body, n_col), [shape((part_h, nodes), BF16),...  1.07 us
  transfers between devices with their start and end apart: 17, of which 9 were waited for; matrix products, arithmetic and copies ran while one was open for 0% of the time, Pallas kernels for 16%

profile of v4, /device:TPU:0, one launch (start us, length us, event | category | flops | bytes accessed | tf_op | source)
XLA Modules:
  0.0 47.3 jit_solution(15929332283087936790)
XLA Ops:
  0.6 0.0 copy-start
  0.6 3.1 %collective-permute-start = (bf16[64,256]{1,0:T(8,128)(2,1)}, bf16[64,256]{1,0:T(8,128)(2,1)S(1)}, u32[]{:S(2)}, u32[]{:S(2)}) collective-permute-start(bf16[64,256]{1,0:T(8,128)(2,1)} %feat_ref.3), channel_id=1, source_target_pairs={{0,8},{2,10},{4,12},{6,14},{8,0},{10,2},{12,4},{14,6},{16,24},{18,... | collective-permute-start | bytes 98312 | tf_op jit(solution)/shard_map/ppermute | solution.py:275
  3.7 2.6 %collective-permute-start.1 = (bf16[64,256]{1,0:T(8,128)(2,1)}, bf16[64,256]{1,0:T(8,128)(2,1)S(1)}, u32[]{:S(2)}, u32[]{:S(2)}) collective-permute-start(bf16[64,256]{1,0:T(8,128)(2,1)} %feat_ref.3), channel_id=1, source_target_pairs={{0,16},{2,18},{4,20},{6,22},{8,24},{10,26},{12,28},{14,30},{16,0},... | collective-permute-start | bytes 98312 | tf_op jit(solution)/shard_map/ppermute | solution.py:275
  6.3 0.0 collective-permute-start.2
  6.3 1.6 %shard_map.140 = bf16[336,256]{1,0:T(8,128)(2,1)} custom-call(bf16[64,256]{1,0:T(8,128)(2,1)} %feat_ref.3, bf16[64,256]{1,0:T(8,128)(2,1)} %self_ref.3, bf16[64,256]{1,0:T(8,128)(2,1)} %nbr_ref.5, bf16[128,256]{1,0:T(8,128)(2,1)} %cot_ref.3, f32[1,128]{1,0:T(1,128)} %bitcast.3), custom_call_target="tpu_custom_call" | custom-call | bytes 327680 | tf_op jit(solution)/shard_map/pallas_call | solution.py:291
  7.9 1.8 %collective-permute-start.7 = (bf16[336,256]{1,0:T(8,128)(2,1)}, bf16[336,256]{1,0:T(8,128)(2,1)S(1)}, u32[]{:S(2)}, u32[]{:S(2)}) collective-permute-start(bf16[336,256]{1,0:T(8,128)(2,1)} %shard_map.140), channel_id=1, source_target_pairs={{0,1},{1,0},{2,3},{3,2},{4,5},{5,4},{6,7},{7,6},{8,9},{9,8},{10,11... | collective-permute-start | bytes 516104 | tf_op jit(solution)/shard_map/ppermute | solution.py:285
  9.7 0.0 collective-permute-done.refs_1_
  9.7 0.0 collective-permute-done.1.refs_2_
  9.7 2.5 %collective-permute-done.2.refs_3_ = bf16[64,256]{1,0:T(8,128)(2,1)S(1)} collective-permute-done((bf16[64,256]{1,0:T(8,128)(2,1)}, bf16[64,256]{1,0:T(8,128)(2,1)S(1)}, u32[]{:S(2)}, u32[]{:S(2)}) %collective-permute-start.2) | collective-permute-done | bytes 32800 | tf_op jit(solution)/shard_map/ppermute | solution.py:275
  12.2 0.0 copy-start.1
  12.2 0.8 %copy-done.1 = bf16[64,256]{1,0:T(8,128)(2,1)S(1)} copy-done((bf16[64,256]{1,0:T(8,128)(2,1)S(1)}, bf16[64,256]{1,0:T(8,128)(2,1)}, u32[]{:S(2)}) %copy-start.1) | copy-done | bytes 32792
  13.0 0.0 copy-start.6
  13.0 0.0 copy-start.10
  13.0 0.0 copy-start.7
  13.0 0.0 copy-start.9
  13.0 0.1 collective-permute-start.3
  13.1 1.6 %collective-permute-start.4 = (bf16[256,256]{1,0:T(8,128)(2,1)S(1)}, bf16[256,256]{1,0:T(8,128)(2,1)S(1)}, u32[]{:S(2)}, u32[]{:S(2)}) collective-permute-start(bf16[256,256]{1,0:T(8,128)(2,1)S(1)} %shard_map.138.refs_0_), channel_id=1, source_target_pairs={{0,4},{2,6},{4,0},{6,2},{8,12},{10,14},{12,8},{14,10},{16,20},{18,... | collective-permute-start | bytes 393224 | tf_op jit(solution)/shard_map/ppermute | solution.py:275
  14.7 0.3 collective-permute-start.5
  15.0 0.0 copy-done
  15.0 0.0 copy-done.6
  15.0 0.0 copy-done.10
  15.0 0.0 copy-done.7
  15.0 0.0 copy-done.9
  15.0 5.0 %shard_map.137 = (bf16[1024,256]{1,0:T(8,128)(2,1)S(1)}, f32[64,256]{1,0:T(8,128)S(1)}, f32[16,256]{1,0:T(8,128)S(1)}) custom-call(s32[16]{0:T(128)S(1)} %copy-done.7, s32[16]{0:T(128)S(1)} %copy-done.10, s32[16,256]{1,0:T(8,128)S(1)} %copy-done.6, s32[1,256]{1,0:T(1,128)S(1)} %bitcast.5, bf16[64,4096]{1,0:T(8,128)(2,1)S(1)} %copy-done), custom_call_target="tpu_custom_call" | custom-call | flops 134217728 | bytes 16777216 | tf_op jit(solution)/shard_map/pallas_call | solution.py:306
  20.0 0.0 collective-permute-done.3.refs_1_
  20.0 0.0 collective-permute-done.4.refs_2_
  20.0 1.4 %collective-permute-done.5.refs_3_ = bf16[256,256]{1,0:T(8,128)(2,1)S(1)} collective-permute-done((bf16[256,256]{1,0:T(8,128)(2,1)S(1)}, bf16[256,256]{1,0:T(8,128)(2,1)S(1)}, u32[]{:S(2)}, u32[]{:S(2)}) %collective-permute-start.5) | collective-permute-done | bytes 131104 | tf_op jit(solution)/shard_map/ppermute | solution.py:275
  21.4 0.0 copy-start.2
  21.4 0.0 copy-start.3
  21.4 0.0 copy-start.4
  21.4 0.0 copy-start.5
  21.4 0.0 copy-start.8
  21.4 0.9 %shard_map.139.refs_0_ = bf16[64,256]{1,0:T(8,128)(2,1)S(1)} custom-call(s32[16]{0:T(128)S(1)} %copy-done.7, f32[16,256]{1,0:T(8,128)S(1)} %get-tuple-element.24.scale_ref, f32[64,256]{1,0:T(8,128)S(1)} %get-tuple-element.26.acc_ref, bf16[1024,256]{1,0:T(8,128)(2,1)S(1)} %get-tuple-element.25.listed_ref, bf16[256,256]{1,0:T(8,128)(2,1)S(1)} %shard_map.138.refs_0_, ...), custom_call_target="tpu_custom_call" | custom-call | bytes 524288 | tf_op jit(solution)/shard_map/pallas_call | solution.py:315
  22.4 1.6 %collective-permute-start.6 = (bf16[64,256]{1,0:T(8,128)(2,1)S(1)}, bf16[64,256]{1,0:T(8,128)(2,1)S(1)}, u32[]{:S(2)}, u32[]{:S(2)}) collective-permute-start(bf16[64,256]{1,0:T(8,128)(2,1)S(1)} %shard_map.139.refs_0_), channel_id=1, source_target_pairs={{0,1},{1,0},{2,3},{3,2},{4,5},{5,4},{6,7},{7,6},{8,9},{9,8},{10,11... | collective-permute-start | bytes 98312 | tf_op jit(solution)/shard_map/ppermute | solution.py:285
  23.9 0.0 collective-permute-done.7.refs_2_
  23.9 2.4 %collective-permute-done.6.refs_1_ = bf16[64,256]{1,0:T(8,128)(2,1)S(1)} collective-permute-done((bf16[64,256]{1,0:T(8,128)(2,1)S(1)}, bf16[64,256]{1,0:T(8,128)(2,1)S(1)}, u32[]{:S(2)}, u32[]{:S(2)}) %collective-permute-start.6) | collective-permute-done | bytes 32800 | tf_op jit(solution)/shard_map/ppermute | solution.py:285
  26.3 0.0 copy-done.2
  26.3 0.0 copy-done.3
  26.3 0.0 copy-done.4
  26.3 0.0 copy-done.5
  26.4 0.0 copy-done.8
  26.4 1.1 %shard_map.141 = (bf16[128,256]{1,0:T(8,128)(2,1)S(1)}, f32[64,256]{1,0:T(8,128)S(1)}, bf16[112,256]{1,0:T(8,128)(2,1)S(1)}, bf16[112,256]{1,0:T(8,128)(2,1)S(1)...) custom-call(f32[16,256]{1,0:T(8,128)S(1)} %get-tuple-element.24.scale_ref, ...), custom_call_target="tpu_custom_call" | custom-call | flops 83886080 | bytes 458752 | tf_op jit(solution)/shard_map/pallas_call | solution.py:326
  27.4 0.3 collective-permute-start.10
  27.8 1.4 %collective-permute-start.8 = (bf16[112,256]{1,0:T(8,128)(2,1)S(1)}, bf16[112,256]{1,0:T(8,128)(2,1)S(1)}, u32[]{:S(2)}, u32[]{:S(2)}) collective-permute-start(bf16[112,256]{1,0:T(8,128)(2,1)S(1)} %get-tuple-element.29), channel_id=1, source_target_pairs={{0,2},{2,0},{4,6},{6,4},{8,10},{10,8},{12,14},{14,12},{16,18},{18,... | collective-permute-start | bytes 172040 | tf_op jit(solution)/shard_map/ppermute | solution.py:275
  29.1 0.5 %collective-permute-start.9 = (bf16[112,256]{1,0:T(8,128)(2,1)S(1)}, bf16[112,256]{1,0:T(8,128)(2,1)S(1)}, u32[]{:S(2)}, u32[]{:S(2)}) collective-permute-start(bf16[112,256]{1,0:T(8,128)(2,1)S(1)} %get-tuple-element.30), channel_id=1, source_target_pairs={{0,4},{2,6},{4,0},{6,2},{8,12},{10,14},{12,8},{14,10},{16,20},{18,... | collective-permute-start | bytes 172040 | tf_op jit(solution)/shard_map/ppermute | solution.py:275
  29.7 2.0 %collective-permute-done.10.refs_3_ = bf16[112,256]{1,0:T(8,128)(2,1)S(1)} collective-permute-done((bf16[112,256]{1,0:T(8,128)(2,1)S(1)}, bf16[112,256]{1,0:T(8,128)(2,1)S(1)}, u32[]{:S(2)}, u32[]{:S(2)}) %collective-permute-start.10) | collective-permute-done | bytes 57376 | tf_op jit(solution)/shard_map/ppermute | solution.py:275
  31.7 0.0 collective-permute-done.8.refs_1_
  31.7 1.7 %collective-permute-done.9.refs_2_ = bf16[112,256]{1,0:T(8,128)(2,1)S(1)} collective-permute-done((bf16[112,256]{1,0:T(8,128)(2,1)S(1)}, bf16[112,256]{1,0:T(8,128)(2,1)S(1)}, u32[]{:S(2)}, u32[]{:S(2)}) %collective-permute-start.9) | collective-permute-done | bytes 57376 | tf_op jit(solution)/shard_map/ppermute | solution.py:275
  33.3 0.1 shard_map.142.refs_0_
  33.4 0.1 collective-permute-start.11
  33.5 1.6 %collective-permute-start.12 = (bf16[112,256]{1,0:T(8,128)(2,1)S(1)}, bf16[112,256]{1,0:T(8,128)(2,1)S(1)}, u32[]{:S(2)}, u32[]{:S(2)}) collective-permute-start(bf16[112,256]{1,0:T(8,128)(2,1)S(1)} %shard_map.142.refs_0_), channel_id=1, source_target_pairs={{0,16},{2,18},{4,20},{6,22},{8,24},{10,26},{12,28},{14,30},{16,0},... | collective-permute-start | bytes 172040 | tf_op jit(solution)/shard_map/ppermute | solution.py:275
  35.1 2.7 %collective-permute-start.13 = (bf16[112,256]{1,0:T(8,128)(2,1)S(1)}, bf16[112,256]{1,0:T(8,128)(2,1)S(1)}, u32[]{:S(2)}, u32[]{:S(2)}) collective-permute-start(bf16[112,256]{1,0:T(8,128)(2,1)S(1)} %shard_map.142.refs_0_), channel_id=1, source_target_pairs={{0,24},{2,26},{4,28},{6,30},{8,16},{10,18},{12,20},{14,22},{16,8},... | collective-permute-start | bytes 172040 | tf_op jit(solution)/shard_map/ppermute | solution.py:275
  37.9 0.0 collective-permute-done.11.refs_1_
  37.9 1.2 %collective-permute-done.12.refs_2_ = bf16[112,256]{1,0:T(8,128)(2,1)S(1)} collective-permute-done((bf16[112,256]{1,0:T(8,128)(2,1)S(1)}, bf16[112,256]{1,0:T(8,128)(2,1)S(1)}, u32[]{:S(2)}, u32[]{:S(2)}) %collective-permute-start.12) | collective-permute-done | bytes 57376 | tf_op jit(solution)/shard_map/ppermute | solution.py:275
  39.0 2.1 %collective-permute-done.13.refs_3_ = bf16[112,256]{1,0:T(8,128)(2,1)S(1)} collective-permute-done((bf16[112,256]{1,0:T(8,128)(2,1)S(1)}, bf16[112,256]{1,0:T(8,128)(2,1)S(1)}, u32[]{:S(2)}, u32[]{:S(2)}) %collective-permute-start.13) | collective-permute-done | bytes 57376 | tf_op jit(solution)/shard_map/ppermute | solution.py:275
  41.1 0.6 %shard_map.143 = (f32[8,256]{1,0:T(8,128)S(1)}, bf16[48,256]{1,0:T(8,128)(2,1)S(1)}, bf16[48,256]{1,0:T(8,128)(2,1)S(1)}, bf16[48,256]{1,0:T(8,128)(2,1)S(1)}, bf16[48,256]{1,0:T(8,128)(2,1)S(1)}) custom-call(s32[16]{0:T(128)S(1)} %copy-done.7, bf16[112,256]{1,0:T(8,128)(2,1)S(1)} %shard_map.142.refs_0_, ...), custom_call_target="tpu_custom_call" | custom-call | bytes 229376 | tf_op jit(solution)/shard_map/pallas_call | solution.py:350
  41.7 0.1 collective-permute-start.14
  41.8 0.7 %collective-permute-start.15 = (bf16[48,256]{1,0:T(8,128)(2,1)S(1)}, bf16[48,256]{1,0:T(8,128)(2,1)S(1)}, u32[]{:S(2)}, u32[]{:S(2)}) collective-permute-start(bf16[48,256]{1,0:T(8,128)(2,1)S(1)} %get-tuple-element.36), channel_id=1, source_target_pairs={{0,4},{2,6},{4,0},{6,2},{8,12},{10,14},{12,8},{14,10},{16,20},{18,... | collective-permute-start | bytes 73736 | tf_op jit(solution)/shard_map/ppermute | solution.py:275
  42.5 1.2 %collective-permute-start.16 = (bf16[48,256]{1,0:T(8,128)(2,1)S(1)}, bf16[48,256]{1,0:T(8,128)(2,1)S(1)}, u32[]{:S(2)}, u32[]{:S(2)}) collective-permute-start(bf16[48,256]{1,0:T(8,128)(2,1)S(1)} %get-tuple-element.37), channel_id=1, source_target_pairs={{0,6},{2,4},{4,2},{6,0},{8,14},{10,12},{12,10},{14,8},{16,22},{18,... | collective-permute-start | bytes 73736 | tf_op jit(solution)/shard_map/ppermute | solution.py:275
  43.7 0.0 collective-permute-done.14.refs_1_
  43.7 2.2 %collective-permute-done.15.refs_2_ = bf16[48,256]{1,0:T(8,128)(2,1)S(1)} collective-permute-done((bf16[48,256]{1,0:T(8,128)(2,1)S(1)}, bf16[48,256]{1,0:T(8,128)(2,1)S(1)}, u32[]{:S(2)}, u32[]{:S(2)}) %collective-permute-start.15) | collective-permute-done | bytes 24608 | tf_op jit(solution)/shard_map/ppermute | solution.py:275
  45.9 0.1 collective-permute-done.16.refs_3_
  46.0 1.2 %shard_map.144 = (bf16[128,256]{1,0:T(8,128)(2,1)}, bf16[64,256]{1,0:T(8,128)(2,1)}, f32[64,256]{1,0:T(8,128)}, f32[64,256]{1,0:T(8,128)}, f32[1,128]{1,0:T(1,128)}) custom-call(s32[16]{0:T(128)S(1)} %copy-done.7, bf16[128,256]{1,0:T(8,128)(2,1)S(1)} %get-tuple-element.27.act_ref, f32[8,256]{1,0:T(8,128)S(1)} %get-tuple-element.32.bias_ref, ...), custom_call_target="tpu_custom_call" | custom-call | bytes 98304 | tf_op jit(solution)/shard_map/pallas_call | solution.py:363
  (1 shorter events, 0.0 us)
Async XLA Ops:
  0.6 14.4 %copy-start = (bf16[64,4096]{1,0:T(8,128)(2,1)S(1)}, bf16[64,4096]{1,0:T(8,128)(2,1)}, u32[]{:S(2)}) copy-start(bf16[64,4096]{1,0:T(8,128)(2,1)} %cache_ref.1) | copy-start | bytes 1572868
  0.6 9.1 %collective-permute-start = (bf16[64,256]{1,0:T(8,128)(2,1)}, bf16[64,256]{1,0:T(8,128)(2,1)S(1)}, u32[]{:S(2)}, u32[]{:S(2)}) collective-permute-start(bf16[64,256]{1,0:T(8,128)(2,1)} %feat_ref.3), channel_id=1, source_target_pairs={{0,8},{2,10},{4,12},{6,14},{8,0},{10,2},{12,4},{14,6},{16,24},{18,... | collective-permute-start | bytes 98312 | tf_op jit(solution)/shard_map/ppermute | solution.py:275
  3.7 6.0 %collective-permute-start.1 = (bf16[64,256]{1,0:T(8,128)(2,1)}, bf16[64,256]{1,0:T(8,128)(2,1)S(1)}, u32[]{:S(2)}, u32[]{:S(2)}) collective-permute-start(bf16[64,256]{1,0:T(8,128)(2,1)} %feat_ref.3), channel_id=1, source_target_pairs={{0,16},{2,18},{4,20},{6,22},{8,24},{10,26},{12,28},{14,30},{16,0},... | collective-permute-start | bytes 98312 | tf_op jit(solution)/shard_map/ppermute | solution.py:275
  6.3 5.9 %collective-permute-start.2 = (bf16[64,256]{1,0:T(8,128)(2,1)}, bf16[64,256]{1,0:T(8,128)(2,1)S(1)}, u32[]{:S(2)}, u32[]{:S(2)}) collective-permute-start(bf16[64,256]{1,0:T(8,128)(2,1)} %feat_ref.3), channel_id=1, source_target_pairs={{0,24},{2,26},{4,28},{6,30},{8,16},{10,18},{12,20},{14,22},{16,8},... | collective-permute-start | bytes 98312 | tf_op jit(solution)/shard_map/ppermute | solution.py:275
  7.9 16.0 %collective-permute-start.7 = (bf16[336,256]{1,0:T(8,128)(2,1)}, bf16[336,256]{1,0:T(8,128)(2,1)S(1)}, u32[]{:S(2)}, u32[]{:S(2)}) collective-permute-start(bf16[336,256]{1,0:T(8,128)(2,1)} %shard_map.140), channel_id=1, source_target_pairs={{0,1},{1,0},{2,3},{3,2},{4,5},{5,4},{6,7},{7,6},{8,9},{9,8},{10,11... | collective-permute-start | bytes 516104 | tf_op jit(solution)/shard_map/ppermute | solution.py:285
  12.2 0.8 %copy-start.1 = (bf16[64,256]{1,0:T(8,128)(2,1)S(1)}, bf16[64,256]{1,0:T(8,128)(2,1)}, u32[]{:S(2)}) copy-start(bf16[64,256]{1,0:T(8,128)(2,1)} %feat_ref.3) | copy-start | bytes 98308
  13.0 2.0 %copy-start.6 = (s32[16,256]{1,0:T(8,128)S(1)}, s32[16,256]{1,0:T(8,128)}, u32[]{:S(2)}) copy-start(s32[16,256]{1,0:T(8,128)} %nbr_ref.3) | copy-start | bytes 49156
  13.0 2.0 %copy-start.10 = (s32[16]{0:T(128)S(1)}, s32[16]{0:T(128)}, u32[]{:S(2)}) copy-start(s32[16]{0:T(128)} %counts_ref.1) | copy-start | bytes 196
  13.0 2.0 %copy-start.7 = (s32[16]{0:T(128)S(1)}, s32[16]{0:T(128)}, u32[]{:S(2)}) copy-start(s32[16]{0:T(128)} %stale_ref.7) | copy-start | bytes 196
  13.0 2.0 %copy-start.9 = (s32[256]{0:T(256)S(1)}, s32[256]{0:T(256)}, u32[]{:S(2)}) copy-start(s32[256]{0:T(256)} %param.15) | copy-start | bytes 3076
  13.0 7.0 %collective-permute-start.3 = (bf16[256,256]{1,0:T(8,128)(2,1)S(1)}, bf16[256,256]{1,0:T(8,128)(2,1)S(1)}, u32[]{:S(2)}, u32[]{:S(2)}) collective-permute-start(bf16[256,256]{1,0:T(8,128)(2,1)S(1)} %shard_map.138.refs_0_), channel_id=1, source_target_pairs={{0,2},{2,0},{4,6},{6,4},{8,10},{10,8},{12,14},{14,12},{16,18},{18,... | collective-permute-start | bytes 393224 | tf_op jit(solution)/shard_map/ppermute | solution.py:275
  13.1 6.9 %collective-permute-start.4 = (bf16[256,256]{1,0:T(8,128)(2,1)S(1)}, bf16[256,256]{1,0:T(8,128)(2,1)S(1)}, u32[]{:S(2)}, u32[]{:S(2)}) collective-permute-start(bf16[256,256]{1,0:T(8,128)(2,1)S(1)} %shard_map.138.refs_0_), channel_id=1, source_target_pairs={{0,4},{2,6},{4,0},{6,2},{8,12},{10,14},{12,8},{14,10},{16,20},{18,... | collective-permute-start | bytes 393224 | tf_op jit(solution)/shard_map/ppermute | solution.py:275
  14.7 6.7 %collective-permute-start.5 = (bf16[256,256]{1,0:T(8,128)(2,1)S(1)}, bf16[256,256]{1,0:T(8,128)(2,1)S(1)}, u32[]{:S(2)}, u32[]{:S(2)}) collective-permute-start(bf16[256,256]{1,0:T(8,128)(2,1)S(1)} %shard_map.138.refs_0_), channel_id=1, source_target_pairs={{0,6},{2,4},{4,2},{6,0},{8,14},{10,12},{12,10},{14,8},{16,22},{18,... | collective-permute-start | bytes 393224 | tf_op jit(solution)/shard_map/ppermute | solution.py:275
  21.4 4.9 %copy-start.2 = (bf16[64,256]{1,0:T(8,128)(2,1)S(1)}, bf16[64,256]{1,0:T(8,128)(2,1)}, u32[]{:S(2)}) copy-start(bf16[64,256]{1,0:T(8,128)(2,1)} %feat_ref.3) | copy-start | bytes 98308
  21.4 4.9 %copy-start.3 = (bf16[128,256]{1,0:T(8,128)(2,1)S(1)}, bf16[128,256]{1,0:T(8,128)(2,1)}, u32[]{:S(2)}) copy-start(bf16[128,256]{1,0:T(8,128)(2,1)} %cot_ref.3) | copy-start | bytes 196612
  21.4 4.9 %copy-start.4 = (bf16[64,256]{1,0:T(8,128)(2,1)S(1)}, bf16[64,256]{1,0:T(8,128)(2,1)}, u32[]{:S(2)}) copy-start(bf16[64,256]{1,0:T(8,128)(2,1)} %self_ref.3) | copy-start | bytes 98308
  21.4 5.0 %copy-start.5 = (bf16[64,256]{1,0:T(8,128)(2,1)S(1)}, bf16[64,256]{1,0:T(8,128)(2,1)}, u32[]{:S(2)}) copy-start(bf16[64,256]{1,0:T(8,128)(2,1)} %nbr_ref.5) | copy-start | bytes 98308
  21.4 5.0 %copy-start.8 = (f32[128]{0:T(128)S(1)}, f32[128]{0:T(128)}, u32[]{:S(2)}) copy-start(f32[128]{0:T(128)} %param.18) | copy-start | bytes 1540
  22.4 4.0 %collective-permute-start.6 = (bf16[64,256]{1,0:T(8,128)(2,1)S(1)}, bf16[64,256]{1,0:T(8,128)(2,1)S(1)}, u32[]{:S(2)}, u32[]{:S(2)}) collective-permute-start(bf16[64,256]{1,0:T(8,128)(2,1)S(1)} %shard_map.139.refs_0_), channel_id=1, source_target_pairs={{0,1},{1,0},{2,3},{3,2},{4,5},{5,4},{6,7},{7,6},{8,9},{9,8},{10,11... | collective-permute-start | bytes 98312 | tf_op jit(solution)/shard_map/ppermute | solution.py:285
  27.4 4.2 %collective-permute-start.10 = (bf16[112,256]{1,0:T(8,128)(2,1)S(1)}, bf16[112,256]{1,0:T(8,128)(2,1)S(1)}, u32[]{:S(2)}, u32[]{:S(2)}) collective-permute-start(bf16[112,256]{1,0:T(8,128)(2,1)S(1)} %get-tuple-element.31), channel_id=1, source_target_pairs={{0,6},{2,4},{4,2},{6,0},{8,14},{10,12},{12,10},{14,8},{16,22},{18,... | collective-permute-start | bytes 172040 | tf_op jit(solution)/shard_map/ppermute | solution.py:275
  27.8 3.9 %collective-permute-start.8 = (bf16[112,256]{1,0:T(8,128)(2,1)S(1)}, bf16[112,256]{1,0:T(8,128)(2,1)S(1)}, u32[]{:S(2)}, u32[]{:S(2)}) collective-permute-start(bf16[112,256]{1,0:T(8,128)(2,1)S(1)} %get-tuple-element.29), channel_id=1, source_target_pairs={{0,2},{2,0},{4,6},{6,4},{8,10},{10,8},{12,14},{14,12},{16,18},{18,... | collective-permute-start | bytes 172040 | tf_op jit(solution)/shard_map/ppermute | solution.py:275
  29.1 4.2 %collective-permute-start.9 = (bf16[112,256]{1,0:T(8,128)(2,1)S(1)}, bf16[112,256]{1,0:T(8,128)(2,1)S(1)}, u32[]{:S(2)}, u32[]{:S(2)}) collective-permute-start(bf16[112,256]{1,0:T(8,128)(2,1)S(1)} %get-tuple-element.30), channel_id=1, source_target_pairs={{0,4},{2,6},{4,0},{6,2},{8,12},{10,14},{12,8},{14,10},{16,20},{18,... | collective-permute-start | bytes 172040 | tf_op jit(solution)/shard_map/ppermute | solution.py:275
  33.4 4.5 %collective-permute-start.11 = (bf16[112,256]{1,0:T(8,128)(2,1)S(1)}, bf16[112,256]{1,0:T(8,128)(2,1)S(1)}, u32[]{:S(2)}, u32[]{:S(2)}) collective-permute-start(bf16[112,256]{1,0:T(8,128)(2,1)S(1)} %shard_map.142.refs_0_), channel_id=1, source_target_pairs={{0,8},{2,10},{4,12},{6,14},{8,0},{10,2},{12,4},{14,6},{16,24},{18,... | collective-permute-start | bytes 172040 | tf_op jit(solution)/shard_map/ppermute | solution.py:275
  33.5 5.6 %collective-permute-start.12 = (bf16[112,256]{1,0:T(8,128)(2,1)S(1)}, bf16[112,256]{1,0:T(8,128)(2,1)S(1)}, u32[]{:S(2)}, u32[]{:S(2)}) collective-permute-start(bf16[112,256]{1,0:T(8,128)(2,1)S(1)} %shard_map.142.refs_0_), channel_id=1, source_target_pairs={{0,16},{2,18},{4,20},{6,22},{8,24},{10,26},{12,28},{14,30},{16,0},... | collective-permute-start | bytes 172040 | tf_op jit(solution)/shard_map/ppermute | solution.py:275
  35.1 6.0 %collective-permute-start.13 = (bf16[112,256]{1,0:T(8,128)(2,1)S(1)}, bf16[112,256]{1,0:T(8,128)(2,1)S(1)}, u32[]{:S(2)}, u32[]{:S(2)}) collective-permute-start(bf16[112,256]{1,0:T(8,128)(2,1)S(1)} %shard_map.142.refs_0_), channel_id=1, source_target_pairs={{0,24},{2,26},{4,28},{6,30},{8,16},{10,18},{12,20},{14,22},{16,8},... | collective-permute-start | bytes 172040 | tf_op jit(solution)/shard_map/ppermute | solution.py:275
  41.7 1.9 %collective-permute-start.14 = (bf16[48,256]{1,0:T(8,128)(2,1)S(1)}, bf16[48,256]{1,0:T(8,128)(2,1)S(1)}, u32[]{:S(2)}, u32[]{:S(2)}) collective-permute-start(bf16[48,256]{1,0:T(8,128)(2,1)S(1)} %get-tuple-element.35), channel_id=1, source_target_pairs={{0,2},{2,0},{4,6},{6,4},{8,10},{10,8},{12,14},{14,12},{16,18},{18,... | collective-permute-start | bytes 73736 | tf_op jit(solution)/shard_map/ppermute | solution.py:275
  41.8 4.1 %collective-permute-start.15 = (bf16[48,256]{1,0:T(8,128)(2,1)S(1)}, bf16[48,256]{1,0:T(8,128)(2,1)S(1)}, u32[]{:S(2)}, u32[]{:S(2)}) collective-permute-start(bf16[48,256]{1,0:T(8,128)(2,1)S(1)} %get-tuple-element.36), channel_id=1, source_target_pairs={{0,4},{2,6},{4,0},{6,2},{8,12},{10,14},{12,8},{14,10},{16,20},{18,... | collective-permute-start | bytes 73736 | tf_op jit(solution)/shard_map/ppermute | solution.py:275
  42.5 3.5 %collective-permute-start.16 = (bf16[48,256]{1,0:T(8,128)(2,1)S(1)}, bf16[48,256]{1,0:T(8,128)(2,1)S(1)}, u32[]{:S(2)}, u32[]{:S(2)}) collective-permute-start(bf16[48,256]{1,0:T(8,128)(2,1)S(1)} %get-tuple-element.37), channel_id=1, source_target_pairs={{0,6},{2,4},{4,2},{6,0},{8,14},{10,12},{12,10},{14,8},{16,22},{18,... | collective-permute-start | bytes 73736 | tf_op jit(solution)/shard_map/ppermute | solution.py:275

commit v5 on v4

--- a/solution.py
+++ b/solution.py
@@ -137,7 +137,7 @@
 
 def dense_body(n_col, scale_ref, listed_ref, feat_ref, self_ref, nbr_ref, bias_ref, cot_ref, *refs):
     aggs, packs, refs = refs[:n_col], refs[n_col : 2 * n_col - 1], refs[2 * n_col - 1 :]
-    act_ref, own_ref, slots, (cot_full, bias_full, full, wide) = refs[0], refs[1], refs[2 : 2 + LOW], refs[2 + LOW :]
+    act_ref, own_ref, slot_ref, cot_full, bias_full, full, wide = refs
     width, nodes = feat_ref.shape
     part_h = cot_ref.shape[0]
     hidden = part_h * n_col
@@ -192,17 +192,13 @@
         wide[q, base:, :] = jnp.zeros((wide.shape[1] - base, nodes), F32)
         wide[q, base : base + 1, :part_h] = high
         wide[q, base + 1 : base + 2, :part_h] = bias - high
-    low = lax.axis_index("dom") % LOW
-    for m in range(LOW):
-        slots[m][...] = wide[jnp.bitwise_xor(low, m)].astype(BF16)
-
-
-def group_sum_body(base, *refs):
-    got, (out_ref, wide, full) = refs[:LOW], refs[LOW:]
-    low = lax.axis_index("dom") % LOW
-    for m in range(LOW):
-        wide[jnp.bitwise_xor(low, m)] = got[m][...].astype(F32)
-    total = wide[0] + wide[1] + wide[2] + wide[3]
+    slot_ref[...] = wide[...].astype(BF16)
+
+
+def group_sum_body(base, got_ref, out_ref, full):
+    total = got_ref[0].astype(F32)
+    for q in range(1, LOW):
+        total += got_ref[q].astype(F32)
     full[...] = total
     bias = total[base : base + 1] + total[base + 1 : base + 2]
     high = bias.astype(BF16).astype(F32)
@@ -212,8 +208,7 @@
 
 
 def line_sum_body(base, width, count, stale_ref, *refs):
-    got, bias_ref, outs = refs[:count], refs[count], refs[count + 1 : count + 1 + LOW]
-    wide, kept, piece, ranks = refs[count + 1 + LOW :]
+    got, (bias_ref, out_ref, wide, kept, piece, ranks) = refs[:count], refs[count:]
     me = lax.axis_index("dom")
     place = me // LOW
     for m in range(count):
@@ -228,21 +223,19 @@
     piece[...] = jnp.zeros_like(piece)
     piece[short : short + half, :] = total[base - half : base]
     fill_ranks(stale_ref, ranks)
-    for m in range(LOW):
-        piece[:short, :] = kept[ranks[jnp.bitwise_xor(me, m)]]
-        outs[m][...] = piece[...].astype(BF16)
-
-
-def last_body(stale_ref, act_ref, bias_ref, own_ref, *refs):
-    got, (act_out, feat_ref, self_ref, nbr_ref, bias_out, wide, back) = refs[:LOW], refs[LOW:]
+    for q in range(LOW):
+        piece[:short, :] = kept[ranks[place * LOW + q]]
+        out_ref[q] = piece[...].astype(BF16)
+
+
+def last_body(stale_ref, act_ref, bias_ref, own_ref, got_ref, *refs):
+    act_out, feat_ref, self_ref, nbr_ref, bias_out, wide, back = refs
     act_out[...] = act_ref[...]
     bias_out[...] = bias_ref[:1, : bias_out.shape[1]]
     width = own_ref.shape[0]
     me = lax.axis_index("dom")
-    low = me % LOW
     half, short = width // 2, width // LOW
-    for m in range(LOW):
-        wide[jnp.bitwise_xor(low, m)] = got[m][...].astype(F32)
+    wide[...] = got_ref[...].astype(F32)
     fresh = is_fresh(stale_ref, me).astype(F32)
     for q in range(LOW):
         back[q * short : (q + 1) * short, :] = wide[q, :short]
@@ -279,6 +272,10 @@
 
     def within(slots):
         return [slots[0]] + [hop(slots[m], m) for m in range(1, LOW)]
+
+    def swap(slots):
+        groups = [[g + q for q in range(LOW)] for g in range(0, dom, LOW)]
+        return lax.all_to_all(slots, "dom", 0, 0, axis_index_groups=groups, tiled=True)
 
     def around(block):
         return [
@@ -323,9 +320,9 @@
     aggs = [agg] + around(agg)
     base = listed * (width // LOW) + width // 2
     rows = up16(base + 2)
-    act, own, *slots = call(
+    act, own, slots = call(
         functools.partial(dense_body, n_col),
-        [shape((part_h, nodes), BF16), shape((width, nodes), F32)] + [shape((rows, nodes), BF16)] * LOW,
+        [shape((part_h, nodes), BF16), shape((width, nodes), F32), shape((LOW, rows, nodes), BF16)],
         0,
         7 + 2 * n_col - 1,
         [
@@ -341,15 +338,15 @@
         functools.partial(group_sum_body, base),
         shape((rows, nodes), BF16),
         0,
-        LOW,
-        [pltpu.VMEM((LOW, rows, nodes), F32), pltpu.VMEM((rows, nodes), F32)],
+        1,
+        [pltpu.VMEM((rows, nodes), F32)],
         moved=2 * LOW * rows * nodes,
-    )(*within(slots))
+    )(swap(slots))
     lines = along(summed)
     tall = up16(width // LOW + width // 2)
-    bias, *pieces = call(
+    bias, pieces = call(
         functools.partial(line_sum_body, base, width, len(lines)),
-        [shape((8, nodes), F32)] + [shape((tall, nodes), BF16)] * LOW,
+        [shape((8, nodes), F32), shape((LOW, tall, nodes), BF16)],
         1,
         len(lines),
         [
@@ -370,10 +367,10 @@
             shape((1, part_h), F32),
         ),
         1,
-        3 + LOW,
+        4,
         [pltpu.VMEM((LOW, tall, nodes), F32), pltpu.VMEM((width, nodes), F32)],
         moved=2 * LOW * tall * nodes,
-    )(staleness, act, bias, own, *within(pieces))
+    )(staleness, act, bias, own, swap(pieces))
     return act, grad_feat, grad_self, grad_nbr, bias.reshape(-1)
 
 

time: 47.5 us -> 51.7 us (1.088)
  blocking collectives: 0 us -> 14.9 us
  waiting for transfers between devices: 15.6 us -> 8.95 us
  starting transfers between devices: 19.5 us -> 15.4 us
    all_to_all x0 -> x2, blocking collectives: none -> 14.9 us  [swap(): lax.all_to_all(slots, 'dom', 0, 0, axis_index_groups=groups, tiled=True)]
    ppermute x15 -> x9, waiting for transfers between devices: 13.2 us -> 6.52 us  [hop(): return lax.ppermute(block, 'dom', [(i, i ^ m) for i in range(dom)])]
    ppermute x15 -> x9, starting transfers between devices: 16.2 us -> 12.1 us  [hop(): return lax.ppermute(block, 'dom', [(i, i ^ m) for i in range(dom)])]
  transfers between devices with their start and end apart: 17 -> 11, of which waited for: 9 -> 5; matrix products, arithmetic and copies ran while one was open for 0% -> 0% of each run, Pallas kernels for 16% -> 15%
where the time goes in v5:
time: 51.7 us; the launch traced here: 51.4 us
  starting transfers between devices  15.4 us (30%)
  blocking collectives  14.9 us (29%)
  Pallas kernels  10.5 us (20%)
  waiting for transfers between devices  8.95 us (17%)
  local copies, waits for them, and re-layouts  0.8 us (2%)
  between operations  0.77 us (1%)
    all_to_all x2, blocking collectives, swap(): lax.all_to_all(slots, 'dom', 0, 0, axis_index_groups=groups, tiled=True)  14.9 us
    ppermute x9, starting transfers between devices, hop(): return lax.ppermute(block, 'dom', [(i, i ^ m) for i in range(dom)])  12.1 us
    ppermute x9, waiting for transfers between devices, hop(): return lax.ppermute(block, 'dom', [(i, i ^ m) for i in range(dom)])  6.52 us
    pallas_call x1, Pallas kernels, per_device(): call(count_body, (shape((listed * nodes, nodes), BF16), shape((width, nod...  4.98 us
    ppermute x2, starting transfers between devices, around(): lax.ppermute(block, 'col', [(i, (i + s) % n_col) for i in range(n_col)])  3.33 us
    ppermute x2, waiting for transfers between devices, around(): lax.ppermute(block, 'col', [(i, (i + s) % n_col) for i in range(n_col)])  2.42 us
    pallas_call x1, Pallas kernels, per_device(): call(pack_body, shape((3 * width + part_h + 16, nodes), BF16), 0, 0, [plt...  1.61 us
    pallas_call x1, Pallas kernels, per_device(): call(last_body, (shape((part_h, nodes), BF16), shape((width, nodes), BF16...  1.24 us
  transfers between devices with their start and end apart: 11, of which 5 were waited for; matrix products, arithmetic and copies ran while one was open for 0% of the time, Pallas kernels for 15%

profile of v5, /device:TPU:0, one launch (start us, length us, event | category | flops | bytes accessed | tf_op | source)
XLA Modules:
  0.0 51.4 jit_solution(11723101880056511685)
XLA Ops:
  0.6 0.0 copy-start
  0.6 3.1 %collective-permute-start = (bf16[64,256]{1,0:T(8,128)(2,1)}, bf16[64,256]{1,0:T(8,128)(2,1)S(1)}, u32[]{:S(2)}, u32[]{:S(2)}) collective-permute-start(bf16[64,256]{1,0:T(8,128)(2,1)} %feat_ref.3), channel_id=1, source_target_pairs={{0,8},{2,10},{4,12},{6,14},{8,0},{10,2},{12,4},{14,6},{16,24},{18,... | collective-permute-start | bytes 98312 | tf_op jit(solution)/shard_map/ppermute | solution.py:268
  3.7 2.6 %collective-permute-start.1 = (bf16[64,256]{1,0:T(8,128)(2,1)}, bf16[64,256]{1,0:T(8,128)(2,1)S(1)}, u32[]{:S(2)}, u32[]{:S(2)}) collective-permute-start(bf16[64,256]{1,0:T(8,128)(2,1)} %feat_ref.3), channel_id=1, source_target_pairs={{0,16},{2,18},{4,20},{6,22},{8,24},{10,26},{12,28},{14,30},{16,0},... | collective-permute-start | bytes 98312 | tf_op jit(solution)/shard_map/ppermute | solution.py:268
  6.3 0.0 collective-permute-start.2
  6.3 1.6 %shard_map.140 = bf16[336,256]{1,0:T(8,128)(2,1)} custom-call(bf16[64,256]{1,0:T(8,128)(2,1)} %feat_ref.3, bf16[64,256]{1,0:T(8,128)(2,1)} %self_ref.3, bf16[64,256]{1,0:T(8,128)(2,1)} %nbr_ref.5, bf16[128,256]{1,0:T(8,128)(2,1)} %cot_ref.3, f32[1,128]{1,0:T(1,128)} %bitcast.3), custom_call_target="tpu_custom_call" | custom-call | bytes 327680 | tf_op jit(solution)/shard_map/pallas_call | solution.py:288
  7.9 1.8 %collective-permute-start.7 = (bf16[336,256]{1,0:T(8,128)(2,1)}, bf16[336,256]{1,0:T(8,128)(2,1)S(1)}, u32[]{:S(2)}, u32[]{:S(2)}) collective-permute-start(bf16[336,256]{1,0:T(8,128)(2,1)} %shard_map.140), channel_id=1, source_target_pairs={{0,1},{1,0},{2,3},{3,2},{4,5},{5,4},{6,7},{7,6},{8,9},{9,8},{10,11... | collective-permute-start | bytes 516104 | tf_op jit(solution)/shard_map/ppermute | solution.py:282
  9.7 0.0 collective-permute-done.refs_1_
  9.7 0.0 collective-permute-done.1.refs_2_
  9.7 2.5 %collective-permute-done.2.refs_3_ = bf16[64,256]{1,0:T(8,128)(2,1)S(1)} collective-permute-done((bf16[64,256]{1,0:T(8,128)(2,1)}, bf16[64,256]{1,0:T(8,128)(2,1)S(1)}, u32[]{:S(2)}, u32[]{:S(2)}) %collective-permute-start.2) | collective-permute-done | bytes 32800 | tf_op jit(solution)/shard_map/ppermute | solution.py:268
  12.2 0.0 copy-start.1
  12.2 0.8 %copy-done.1 = bf16[64,256]{1,0:T(8,128)(2,1)S(1)} copy-done((bf16[64,256]{1,0:T(8,128)(2,1)S(1)}, bf16[64,256]{1,0:T(8,128)(2,1)}, u32[]{:S(2)}) %copy-start.1) | copy-done | bytes 32792
  13.0 0.0 copy-start.6
  13.0 0.0 copy-start.10
  13.0 0.0 copy-start.7
  13.0 0.0 copy-start.9
  13.0 0.1 collective-permute-start.3
  13.1 1.6 %collective-permute-start.4 = (bf16[256,256]{1,0:T(8,128)(2,1)S(1)}, bf16[256,256]{1,0:T(8,128)(2,1)S(1)}, u32[]{:S(2)}, u32[]{:S(2)}) collective-permute-start(bf16[256,256]{1,0:T(8,128)(2,1)S(1)} %shard_map.138.refs_0_), channel_id=1, source_target_pairs={{0,4},{2,6},{4,0},{6,2},{8,12},{10,14},{12,8},{14,10},{16,20},{18,... | collective-permute-start | bytes 393224 | tf_op jit(solution)/shard_map/ppermute | solution.py:268
  14.7 0.3 collective-permute-start.5
  15.0 0.0 copy-done
  15.0 0.0 copy-done.6
  15.0 0.0 copy-done.10
  15.0 0.0 copy-done.7
  15.0 0.0 copy-done.9
  15.0 5.0 %shard_map.137 = (bf16[1024,256]{1,0:T(8,128)(2,1)S(1)}, f32[64,256]{1,0:T(8,128)S(1)}, f32[16,256]{1,0:T(8,128)S(1)}) custom-call(s32[16]{0:T(128)S(1)} %copy-done.7, s32[16]{0:T(128)S(1)} %copy-done.10, s32[16,256]{1,0:T(8,128)S(1)} %copy-done.6, s32[1,256]{1,0:T(1,128)S(1)} %bitcast.5, bf16[64,4096]{1,0:T(8,128)(2,1)S(1)} %copy-done), custom_call_target="tpu_custom_call" | custom-call | flops 134217728 | bytes 16777216 | tf_op jit(solution)/shard_map/pallas_call | solution.py:303
  20.0 0.0 collective-permute-done.3.refs_1_
  20.0 0.0 collective-permute-done.4.refs_2_
  20.0 1.4 %collective-permute-done.5.refs_3_ = bf16[256,256]{1,0:T(8,128)(2,1)S(1)} collective-permute-done((bf16[256,256]{1,0:T(8,128)(2,1)S(1)}, bf16[256,256]{1,0:T(8,128)(2,1)S(1)}, u32[]{:S(2)}, u32[]{:S(2)}) %collective-permute-start.5) | collective-permute-done | bytes 131104 | tf_op jit(solution)/shard_map/ppermute | solution.py:268
  21.4 0.0 copy-start.2
  21.4 0.0 copy-start.3
  21.4 0.0 copy-start.4
  21.4 0.0 copy-start.5
  21.4 0.0 copy-start.8
  21.4 0.9 %shard_map.139.refs_0_ = bf16[64,256]{1,0:T(8,128)(2,1)S(1)} custom-call(s32[16]{0:T(128)S(1)} %copy-done.7, f32[16,256]{1,0:T(8,128)S(1)} %get-tuple-element.18.scale_ref, f32[64,256]{1,0:T(8,128)S(1)} %get-tuple-element.20.acc_ref, bf16[1024,256]{1,0:T(8,128)(2,1)S(1)} %get-tuple-element.19.listed_ref, bf16[256,256]{1,0:T(8,128)(2,1)S(1)} %shard_map.138.refs_0_, ...), custom_call_target="tpu_custom_call" | custom-call | bytes 524288 | tf_op jit(solution)/shard_map/pallas_call | solution.py:312
  22.4 1.6 %collective-permute-start.6 = (bf16[64,256]{1,0:T(8,128)(2,1)S(1)}, bf16[64,256]{1,0:T(8,128)(2,1)S(1)}, u32[]{:S(2)}, u32[]{:S(2)}) collective-permute-start(bf16[64,256]{1,0:T(8,128)(2,1)S(1)} %shard_map.139.refs_0_), channel_id=1, source_target_pairs={{0,1},{1,0},{2,3},{3,2},{4,5},{5,4},{6,7},{7,6},{8,9},{9,8},{10,11... | collective-permute-start | bytes 98312 | tf_op jit(solution)/shard_map/ppermute | solution.py:282
  23.9 0.0 collective-permute-done.7.refs_2_
  23.9 2.4 %collective-permute-done.6.refs_1_ = bf16[64,256]{1,0:T(8,128)(2,1)S(1)} collective-permute-done((bf16[64,256]{1,0:T(8,128)(2,1)S(1)}, bf16[64,256]{1,0:T(8,128)(2,1)S(1)}, u32[]{:S(2)}, u32[]{:S(2)}) %collective-permute-start.6) | collective-permute-done | bytes 32800 | tf_op jit(solution)/shard_map/ppermute | solution.py:282
  26.3 0.0 copy-done.2
  26.3 0.0 copy-done.3
  26.3 0.0 copy-done.4
  26.3 0.0 copy-done.5
  26.4 0.0 copy-done.8
  26.4 1.1 %shard_map.141 = (bf16[128,256]{1,0:T(8,128)(2,1)S(1)}, f32[64,256]{1,0:T(8,128)S(1)}, bf16[4,112,256]{2,1,0:T(8,128)(2,1)S(1)}) custom-call(f32[16,256]{1,0:T(8,128)S(1)} %get-tuple-element.18.scale_ref, bf16[1024,256]{1,0:T(8,128)(2,1)S(1)} %get-tuple-element.19.listed_ref, bf16[64,256]{1,0:T(8,128)(2,1)S(1)} %copy-done.2, bf16[64,256]{1,0:T(8,128)(2,1)S(1)} %copy-done.4, ...), custom_call_target="tpu_custom_call" | custom-call | flops 83886080 | bytes 458752 | tf_op jit(solution)/shard_map/pallas_call | solution.py:323
  27.4 8.3 %all_to_all.10.got_ref = bf16[4,112,256]{2,1,0:T(8,128)(2,1)S(1)} all-to-all(bf16[4,112,256]{2,1,0:T(8,128)(2,1)S(1)} %get-tuple-element.22), channel_id=1, replica_groups={{0,2,4,6},{8,10,12,14},{16,18,20,22},{24,26,28,30},{1,3,5,7},{9,11,13,1..., dimensions={0} | all-to-all | bytes 458752 | tf_op jit(solution)/shard_map/all_to_all | solution.py:278
  35.7 1.2 %collective-permute-start.10 = (bf16[112,256]{1,0:T(8,128)(2,1)S(1)}, bf16[112,256]{1,0:T(8,128)(2,1)S(1)}, u32[]{:S(2)}, u32[]{:S(2)}) collective-permute-start(bf16[112,256]{1,0:T(8,128)(2,1)S(1)} %shard_map.142.refs_0_), channel_id=1, source_target_pairs={{0,24},{2,26},{4,28},{6,30},{8,16},{10,18},{12,20},{14,22},{16,8},... | collective-permute-start | bytes 172040 | tf_op jit(solution)/shard_map/ppermute | solution.py:268
  36.9 0.0 collective-permute-start.8
  36.9 3.3 %collective-permute-start.9 = (bf16[112,256]{1,0:T(8,128)(2,1)S(1)}, bf16[112,256]{1,0:T(8,128)(2,1)S(1)}, u32[]{:S(2)}, u32[]{:S(2)}) collective-permute-start(bf16[112,256]{1,0:T(8,128)(2,1)S(1)} %shard_map.142.refs_0_), channel_id=1, source_target_pairs={{0,16},{2,18},{4,20},{6,22},{8,24},{10,26},{12,28},{14,30},{16,0},... | collective-permute-start | bytes 172040 | tf_op jit(solution)/shard_map/ppermute | solution.py:268
  40.2 2.1 %collective-permute-done.10.refs_3_ = bf16[112,256]{1,0:T(8,128)(2,1)S(1)} collective-permute-done((bf16[112,256]{1,0:T(8,128)(2,1)S(1)}, bf16[112,256]{1,0:T(8,128)(2,1)S(1)}, u32[]{:S(2)}, u32[]{:S(2)}) %collective-permute-start.10) | collective-permute-done | bytes 57376 | tf_op jit(solution)/shard_map/ppermute | solution.py:268
  42.3 0.0 collective-permute-done.8.refs_1_
  42.3 0.6 %collective-permute-done.9.refs_2_ = bf16[112,256]{1,0:T(8,128)(2,1)S(1)} collective-permute-done((bf16[112,256]{1,0:T(8,128)(2,1)S(1)}, bf16[112,256]{1,0:T(8,128)(2,1)S(1)}, u32[]{:S(2)}, u32[]{:S(2)}) %collective-permute-start.9) | collective-permute-done | bytes 57376 | tf_op jit(solution)/shard_map/ppermute | solution.py:268
  42.8 0.6 %shard_map.143 = (f32[8,256]{1,0:T(8,128)S(1)}, bf16[4,48,256]{2,1,0:T(8,128)(2,1)S(1)}) custom-call(s32[16]{0:T(128)S(1)} %copy-done.7, bf16[112,256]{1,0:T(8,128)(2,1)S(1)} %shard_map.142.refs_0_, bf16[112,256]{1,0:T(8,128)(2,1)S(1)} %collective-permute-done.8.refs_1_, bf16[112,256]{1,0:T(8,128)(2,1)S(1)} %collective-permute-done.9.refs_2_, ...), custom_call_target="tpu_custom_call" | custom-call | bytes 229376 | tf_op jit(solution)/shard_map/pallas_call | solution.py:347
  43.5 6.7 %all_to_all.11.got_ref = bf16[4,48,256]{2,1,0:T(8,128)(2,1)S(1)} all-to-all(bf16[4,48,256]{2,1,0:T(8,128)(2,1)S(1)} %get-tuple-element.25), channel_id=1, replica_groups={{0,2,4,6},{8,10,12,14},{16,18,20,22},{24,26,28,30},{1,3,5,7},{9,11,13,1..., dimensions={0} | all-to-all | bytes 196608 | tf_op jit(solution)/shard_map/all_to_all | solution.py:278
  50.1 1.2 %shard_map.144 = (bf16[128,256]{1,0:T(8,128)(2,1)}, bf16[64,256]{1,0:T(8,128)(2,1)}, f32[64,256]{1,0:T(8,128)}, f32[64,256]{1,0:T(8,128)}, f32[1,128]{1,0:T(1,128)}) custom-call(s32[16]{0:T(128)S(1)} %copy-done.7, bf16[128,256]{1,0:T(8,128)(2,1)S(1)} %get-tuple-element.21.act_ref, f32[8,256]{1,0:T(8,128)S(1)} %get-tuple-element.23.bias_ref, ...), custom_call_target="tpu_custom_call" | custom-call | bytes 98304 | tf_op jit(solution)/shard_map/pallas_call | solution.py:360
  (2 shorter events, 0.1 us)
Async XLA Ops:
  0.6 14.4 %copy-start = (bf16[64,4096]{1,0:T(8,128)(2,1)S(1)}, bf16[64,4096]{1,0:T(8,128)(2,1)}, u32[]{:S(2)}) copy-start(bf16[64,4096]{1,0:T(8,128)(2,1)} %cache_ref.1) | copy-start | bytes 1572868
  0.6 9.1 %collective-permute-start = (bf16[64,256]{1,0:T(8,128)(2,1)}, bf16[64,256]{1,0:T(8,128)(2,1)S(1)}, u32[]{:S(2)}, u32[]{:S(2)}) collective-permute-start(bf16[64,256]{1,0:T(8,128)(2,1)} %feat_ref.3), channel_id=1, source_target_pairs={{0,8},{2,10},{4,12},{6,14},{8,0},{10,2},{12,4},{14,6},{16,24},{18,... | collective-permute-start | bytes 98312 | tf_op jit(solution)/shard_map/ppermute | solution.py:268
  3.7 6.0 %collective-permute-start.1 = (bf16[64,256]{1,0:T(8,128)(2,1)}, bf16[64,256]{1,0:T(8,128)(2,1)S(1)}, u32[]{:S(2)}, u32[]{:S(2)}) collective-permute-start(bf16[64,256]{1,0:T(8,128)(2,1)} %feat_ref.3), channel_id=1, source_target_pairs={{0,16},{2,18},{4,20},{6,22},{8,24},{10,26},{12,28},{14,30},{16,0},... | collective-permute-start | bytes 98312 | tf_op jit(solution)/shard_map/ppermute | solution.py:268
  6.3 5.9 %collective-permute-start.2 = (bf16[64,256]{1,0:T(8,128)(2,1)}, bf16[64,256]{1,0:T(8,128)(2,1)S(1)}, u32[]{:S(2)}, u32[]{:S(2)}) collective-permute-start(bf16[64,256]{1,0:T(8,128)(2,1)} %feat_ref.3), channel_id=1, source_target_pairs={{0,24},{2,26},{4,28},{6,30},{8,16},{10,18},{12,20},{14,22},{16,8},... | collective-permute-start | bytes 98312 | tf_op jit(solution)/shard_map/ppermute | solution.py:268
  7.9 16.0 %collective-permute-start.7 = (bf16[336,256]{1,0:T(8,128)(2,1)}, bf16[336,256]{1,0:T(8,128)(2,1)S(1)}, u32[]{:S(2)}, u32[]{:S(2)}) collective-permute-start(bf16[336,256]{1,0:T(8,128)(2,1)} %shard_map.140), channel_id=1, source_target_pairs={{0,1},{1,0},{2,3},{3,2},{4,5},{5,4},{6,7},{7,6},{8,9},{9,8},{10,11... | collective-permute-start | bytes 516104 | tf_op jit(solution)/shard_map/ppermute | solution.py:282
  12.2 0.8 %copy-start.1 = (bf16[64,256]{1,0:T(8,128)(2,1)S(1)}, bf16[64,256]{1,0:T(8,128)(2,1)}, u32[]{:S(2)}) copy-start(bf16[64,256]{1,0:T(8,128)(2,1)} %feat_ref.3) | copy-start | bytes 98308
  13.0 2.0 %copy-start.6 = (s32[16,256]{1,0:T(8,128)S(1)}, s32[16,256]{1,0:T(8,128)}, u32[]{:S(2)}) copy-start(s32[16,256]{1,0:T(8,128)} %nbr_ref.3) | copy-start | bytes 49156
  13.0 2.0 %copy-start.10 = (s32[16]{0:T(128)S(1)}, s32[16]{0:T(128)}, u32[]{:S(2)}) copy-start(s32[16]{0:T(128)} %counts_ref.1) | copy-start | bytes 196
  13.0 2.0 %copy-start.7 = (s32[16]{0:T(128)S(1)}, s32[16]{0:T(128)}, u32[]{:S(2)}) copy-start(s32[16]{0:T(128)} %stale_ref.7) | copy-start | bytes 196
  13.0 2.0 %copy-start.9 = (s32[256]{0:T(256)S(1)}, s32[256]{0:T(256)}, u32[]{:S(2)}) copy-start(s32[256]{0:T(256)} %param.15) | copy-start | bytes 3076
  13.0 7.0 %collective-permute-start.3 = (bf16[256,256]{1,0:T(8,128)(2,1)S(1)}, bf16[256,256]{1,0:T(8,128)(2,1)S(1)}, u32[]{:S(2)}, u32[]{:S(2)}) collective-permute-start(bf16[256,256]{1,0:T(8,128)(2,1)S(1)} %shard_map.138.refs_0_), channel_id=1, source_target_pairs={{0,2},{2,0},{4,6},{6,4},{8,10},{10,8},{12,14},{14,12},{16,18},{18,... | collective-permute-start | bytes 393224 | tf_op jit(solution)/shard_map/ppermute | solution.py:268
  13.1 6.9 %collective-permute-start.4 = (bf16[256,256]{1,0:T(8,128)(2,1)S(1)}, bf16[256,256]{1,0:T(8,128)(2,1)S(1)}, u32[]{:S(2)}, u32[]{:S(2)}) collective-permute-start(bf16[256,256]{1,0:T(8,128)(2,1)S(1)} %shard_map.138.refs_0_), channel_id=1, source_target_pairs={{0,4},{2,6},{4,0},{6,2},{8,12},{10,14},{12,8},{14,10},{16,20},{18,... | collective-permute-start | bytes 393224 | tf_op jit(solution)/shard_map/ppermute | solution.py:268
  14.7 6.7 %collective-permute-start.5 = (bf16[256,256]{1,0:T(8,128)(2,1)S(1)}, bf16[256,256]{1,0:T(8,128)(2,1)S(1)}, u32[]{:S(2)}, u32[]{:S(2)}) collective-permute-start(bf16[256,256]{1,0:T(8,128)(2,1)S(1)} %shard_map.138.refs_0_), channel_id=1, source_target_pairs={{0,6},{2,4},{4,2},{6,0},{8,14},{10,12},{12,10},{14,8},{16,22},{18,... | collective-permute-start | bytes 393224 | tf_op jit(solution)/shard_map/ppermute | solution.py:268
  21.4 5.0 %copy-start.2 = (bf16[64,256]{1,0:T(8,128)(2,1)S(1)}, bf16[64,256]{1,0:T(8,128)(2,1)}, u32[]{:S(2)}) copy-start(bf16[64,256]{1,0:T(8,128)(2,1)} %feat_ref.3) | copy-start | bytes 98308
  21.4 5.0 %copy-start.3 = (bf16[128,256]{1,0:T(8,128)(2,1)S(1)}, bf16[128,256]{1,0:T(8,128)(2,1)}, u32[]{:S(2)}) copy-start(bf16[128,256]{1,0:T(8,128)(2,1)} %cot_ref.3) | copy-start | bytes 196612
  21.4 5.0 %copy-start.4 = (bf16[64,256]{1,0:T(8,128)(2,1)S(1)}, bf16[64,256]{1,0:T(8,128)(2,1)}, u32[]{:S(2)}) copy-start(bf16[64,256]{1,0:T(8,128)(2,1)} %self_ref.3) | copy-start | bytes 98308
  21.4 5.0 %copy-start.5 = (bf16[64,256]{1,0:T(8,128)(2,1)S(1)}, bf16[64,256]{1,0:T(8,128)(2,1)}, u32[]{:S(2)}) copy-start(bf16[64,256]{1,0:T(8,128)(2,1)} %nbr_ref.5) | copy-start | bytes 98308
  21.4 5.0 %copy-start.8 = (f32[128]{0:T(128)S(1)}, f32[128]{0:T(128)}, u32[]{:S(2)}) copy-start(f32[128]{0:T(128)} %param.18) | copy-start | bytes 1540
  22.4 4.0 %collective-permute-start.6 = (bf16[64,256]{1,0:T(8,128)(2,1)S(1)}, bf16[64,256]{1,0:T(8,128)(2,1)S(1)}, u32[]{:S(2)}, u32[]{:S(2)}) collective-permute-start(bf16[64,256]{1,0:T(8,128)(2,1)S(1)} %shard_map.139.refs_0_), channel_id=1, source_target_pairs={{0,1},{1,0},{2,3},{3,2},{4,5},{5,4},{6,7},{7,6},{8,9},{9,8},{10,11... | collective-permute-start | bytes 98312 | tf_op jit(solution)/shard_map/ppermute | solution.py:282
  35.7 6.5 %collective-permute-start.10 = (bf16[112,256]{1,0:T(8,128)(2,1)S(1)}, bf16[112,256]{1,0:T(8,128)(2,1)S(1)}, u32[]{:S(2)}, u32[]{:S(2)}) collective-permute-start(bf16[112,256]{1,0:T(8,128)(2,1)S(1)} %shard_map.142.refs_0_), channel_id=1, source_target_pairs={{0,24},{2,26},{4,28},{6,30},{8,16},{10,18},{12,20},{14,22},{16,8},... | collective-permute-start | bytes 172040 | tf_op jit(solution)/shard_map/ppermute | solution.py:268
  36.9 5.4 %collective-permute-start.8 = (bf16[112,256]{1,0:T(8,128)(2,1)S(1)}, bf16[112,256]{1,0:T(8,128)(2,1)S(1)}, u32[]{:S(2)}, u32[]{:S(2)}) collective-permute-start(bf16[112,256]{1,0:T(8,128)(2,1)S(1)} %shard_map.142.refs_0_), channel_id=1, source_target_pairs={{0,8},{2,10},{4,12},{6,14},{8,0},{10,2},{12,4},{14,6},{16,24},{18,... | collective-permute-start | bytes 172040 | tf_op jit(solution)/shard_map/ppermute | solution.py:268
  36.9 5.9 %collective-permute-start.9 = (bf16[112,256]{1,0:T(8,128)(2,1)S(1)}, bf16[112,256]{1,0:T(8,128)(2,1)S(1)}, u32[]{:S(2)}, u32[]{:S(2)}) collective-permute-start(bf16[112,256]{1,0:T(8,128)(2,1)S(1)} %shard_map.142.refs_0_), channel_id=1, source_target_pairs={{0,16},{2,18},{4,20},{6,22},{8,24},{10,26},{12,28},{14,30},{16,0},... | collective-permute-start | bytes 172040 | tf_op jit(solution)/shard_map/ppermute | solution.py:268

commit v6 on v4

--- a/solution.py
+++ b/solution.py
@@ -52,7 +52,9 @@
     return high, mid, x - high - mid
 
 
-def count_body(stale_ref, counts_ref, nbr_ref, deg_ref, cache_ref, listed_ref, acc_ref, scale_ref, all_ref):
+def count_body(
+    stale_ref, counts_ref, nbr_ref, deg_ref, cache_ref, listed_ref, acc_ref, scale_ref, pick_ref, all_ref, ranks
+):
     slots, nodes = nbr_ref.shape
     listed = listed_ref.shape[0] // nodes
     used = lax.broadcasted_iota(jnp.int32, (slots, nodes), 0) < deg_ref[...]
@@ -63,6 +65,13 @@
     ).astype(F32)
     scale_ref[0:8, :] = jnp.broadcast_to(live, (8, nodes))
     scale_ref[8:16, :] = jnp.broadcast_to(live / deg_ref[...].astype(F32), (8, nodes))
+    me = lax.axis_index("dom")
+    scale_ref[16:24, :] = jnp.full((8, nodes), is_fresh(stale_ref, me).astype(F32))
+    fill_ranks(stale_ref, ranks)
+    for q in range(LOW):
+        place = ranks[me // LOW * LOW + q]
+        for r in range(listed):
+            pick_ref[q * listed + r : q * listed + r + 1, :] = jnp.full((1, nodes), (place == r).astype(F32))
 
     def per_part(part, rank):
         fresh = is_fresh(stale_ref, part)
@@ -89,21 +98,22 @@
     acc_ref[...] = jnp.dot(cache_ref[...], all_ref[...], preferred_element_type=F32)
 
 
-def pack_body(feat_ref, self_ref, nbr_ref, cot_ref, bias_ref, out_ref, bias, wide, sems):
-    row = 0
+def pack_body(self_ref, nbr_ref, cot_ref, bias_ref, feat_ref, out_ref, bias, wide, sems):
+    row = feat_ref.shape[0]
     copies = []
-    for i, ref in enumerate((feat_ref, self_ref, nbr_ref, cot_ref)):
+    for i, ref in enumerate((self_ref, nbr_ref, cot_ref)):
         copies.append(pltpu.make_async_copy(ref, out_ref.at[row : row + ref.shape[0], :], sems.at[i]))
         row += ref.shape[0]
-    copies.append(pltpu.make_async_copy(bias_ref, bias, sems.at[4]))
+    copies.append(pltpu.make_async_copy(bias_ref, bias, sems.at[3]))
     for copy in copies:
         copy.start()
     wide[...] = jnp.zeros_like(wide)
-    copies[4].wait()
+    out_ref[: feat_ref.shape[0], :] = feat_ref[...]
+    copies[3].wait()
     for i, term in enumerate(split3(bias[...])):
         wide[i : i + 1, : bias.shape[1]] = term
     out_ref[row:, :] = wide[...].astype(BF16)
-    for copy in copies[:4]:
+    for copy in copies[:3]:
         copy.wait()
 
 
@@ -211,9 +221,9 @@
     out_ref[...] = full[...].astype(BF16)
 
 
-def line_sum_body(base, width, count, stale_ref, *refs):
+def line_sum_body(base, width, count, pick_ref, *refs):
     got, bias_ref, outs = refs[:count], refs[count], refs[count + 1 : count + 1 + LOW]
-    wide, kept, piece, ranks = refs[count + 1 + LOW :]
+    wide, piece, pieces = refs[count + 1 + LOW :]
     me = lax.axis_index("dom")
     place = me // LOW
     for m in range(count):
@@ -223,17 +233,21 @@
         total += wide[m]
     bias_ref[...] = jnp.broadcast_to(total[base : base + 1] + total[base + 1 : base + 2], bias_ref.shape)
     half, short = width // 2, width // LOW
-    for r in range(kept.shape[0]):
-        kept[r] = total[r * short : (r + 1) * short]
     piece[...] = jnp.zeros_like(piece)
     piece[short : short + half, :] = total[base - half : base]
-    fill_ranks(stale_ref, ranks)
+    listed = pick_ref.shape[0] // LOW
+    for q in range(LOW):
+        mine = jnp.zeros((short, total.shape[1]), F32)
+        for r in range(listed):
+            row = q * listed + r
+            mine += pick_ref[row : row + 1, :] * total[r * short : (r + 1) * short]
+        piece[:short, :] = mine
+        pieces[q] = piece[...]
     for m in range(LOW):
-        piece[:short, :] = kept[ranks[jnp.bitwise_xor(me, m)]]
-        outs[m][...] = piece[...].astype(BF16)
-
-
-def last_body(stale_ref, act_ref, bias_ref, own_ref, *refs):
+        outs[m][...] = pieces[jnp.bitwise_xor(me % LOW, m)].astype(BF16)
+
+
+def last_body(scale_ref, act_ref, bias_ref, own_ref, *refs):
     got, (act_out, feat_ref, self_ref, nbr_ref, bias_out, wide, back) = refs[:LOW], refs[LOW:]
     act_out[...] = act_ref[...]
     bias_out[...] = bias_ref[:1, : bias_out.shape[1]]
@@ -243,7 +257,7 @@
     half, short = width // 2, width // LOW
     for m in range(LOW):
         wide[jnp.bitwise_xor(low, m)] = got[m][...].astype(F32)
-    fresh = is_fresh(stale_ref, me).astype(F32)
+    fresh = scale_ref[16:17, :]
     for q in range(LOW):
         back[q * short : (q + 1) * short, :] = wide[q, :short]
         ref = nbr_ref if q // 2 else self_ref
@@ -292,23 +306,28 @@
         pack_body,
         shape((3 * width + part_h + 16, nodes), BF16),
         0,
-        0,
-        [pltpu.VMEM((1, part_h), F32), pltpu.VMEM((16, nodes), F32), pltpu.SemaphoreType.DMA((5,))],
+        1,
+        [pltpu.VMEM((1, part_h), F32), pltpu.VMEM((16, nodes), F32), pltpu.SemaphoreType.DMA((4,))],
         moved=4 * (3 * width + part_h) * nodes,
-        hbm_count=5,
-    )(features, w_self, w_nbr, cotangent, bias_row)
+        hbm_count=4,
+    )(w_self, w_nbr, cotangent, bias_row, features)
     packs = around(packed)
     deg = degrees.reshape(1, nodes)
     stacked = call(stack_body, shape((width * len(line), nodes), BF16), 0, len(line), moved=4 * dom * width * nodes // LOW)(
         *line
     )
     stacks = within([stacked] * LOW)
-    counts, acc, scale = call(
+    counts, acc, scale, picks = call(
         count_body,
-        (shape((listed * nodes, nodes), BF16), shape((width, nodes), F32), shape((16, nodes), F32)),
+        (
+            shape((listed * nodes, nodes), BF16),
+            shape((width, nodes), F32),
+            shape((24, nodes), F32),
+            shape((LOW * listed, nodes), F32),
+        ),
         2,
         3,
-        [pltpu.VMEM((dom * nodes, nodes), BF16)],
+        [pltpu.VMEM((dom * nodes, nodes), BF16), pltpu.SMEM((dom,), jnp.int32)],
         flops=2 * width * dom * nodes * nodes,
         moved=dom * nodes * nodes * 16,
     )(staleness, node_counts, neighbours, deg, cached_embed)
@@ -350,16 +369,15 @@
     bias, *pieces = call(
         functools.partial(line_sum_body, base, width, len(lines)),
         [shape((8, nodes), F32)] + [shape((tall, nodes), BF16)] * LOW,
-        1,
-        len(lines),
+        0,
+        1 + len(lines),
         [
             pltpu.VMEM((len(lines), rows, nodes), F32),
-            pltpu.VMEM((listed, width // LOW, nodes), F32),
             pltpu.VMEM((tall, nodes), F32),
-            pltpu.SMEM((dom,), jnp.int32),
+            pltpu.VMEM((LOW, tall, nodes), F32),
         ],
         moved=2 * len(lines) * rows * nodes,
-    )(staleness, *lines)
+    )(picks, *lines)
     act, grad_feat, grad_self, grad_nbr, bias = call(
         last_body,
         (
@@ -369,11 +387,11 @@
             shape((width, hidden), F32),
             shape((1, part_h), F32),
         ),
-        1,
-        3 + LOW,
+        0,
+        4 + LOW,
         [pltpu.VMEM((LOW, tall, nodes), F32), pltpu.VMEM((width, nodes), F32)],
         moved=2 * LOW * tall * nodes,
-    )(staleness, act, bias, own, *within(pieces))
+    )(scale, act, bias, own, *within(pieces))
     return act, grad_feat, grad_self, grad_nbr, bias.reshape(-1)
 
 

time: 47.5 us -> 47.2 us (level)
    pallas_call x1, Pallas kernels: 1.61 us -> 2.4 us  [per_device(): call(pack_body, shape((3 * width + part_h + 16, nodes), BF16), 0, 1, [plt...]
    pallas_call x1, Pallas kernels: 1.25 us -> 0.7 us  [per_device(): call(last_body, (shape((part_h, nodes), BF16), shape((width, nodes), BF16...]
    pallas_call x1, Pallas kernels: 0.62 us -> 0.09 us  [per_device(): call(functools.partial(line_sum_body, base, width, len(lines)), [shape((8...]
  transfers between devices with their start and end apart: 17 -> 17, of which waited for: 9 -> 8; matrix products, arithmetic and copies ran while one was open for 0% -> 0% of each run, Pallas kernels for 16% -> 18%
where the time goes in v6:
time: 47.2 us; the launch traced here: 46.9 us
  starting transfers between devices  19.5 us (41%)
  waiting for transfers between devices  15.4 us (33%)
  Pallas kernels  10.3 us (22%)
  local copies, waits for them, and re-layouts  0.8 us (2%)
  between operations  0.8 us (2%)
    ppermute x15, starting transfers between devices, hop(): return lax.ppermute(block, 'dom', [(i, i ^ m) for i in range(dom)])  16.2 us
    ppermute x15, waiting for transfers between devices, hop(): return lax.ppermute(block, 'dom', [(i, i ^ m) for i in range(dom)])  13 us
    pallas_call x1, Pallas kernels, per_device(): call(count_body, (shape((listed * nodes, nodes), BF16), shape((width, nod...  5.04 us
    ppermute x2, starting transfers between devices, around(): lax.ppermute(block, 'col', [(i, (i + s) % n_col) for i in range(n_col)])  3.3 us
    ppermute x2, waiting for transfers between devices, around(): lax.ppermute(block, 'col', [(i, (i + s) % n_col) for i in range(n_col)])  2.42 us
    pallas_call x1, Pallas kernels, per_device(): call(pack_body, shape((3 * width + part_h + 16, nodes), BF16), 0, 1, [plt...  2.4 us
    pallas_call x1, Pallas kernels, per_device(): call(functools.partial(dense_body, n_col), [shape((part_h, nodes), BF16),...  1.07 us
  transfers between devices with their start and end apart: 17, of which 8 were waited for; matrix products, arithmetic and copies ran while one was open for 0% of the time, Pallas kernels for 18%

profile of v6, /device:TPU:0, one launch (start us, length us, event | category | flops | bytes accessed | tf_op | source)
XLA Modules:
  0.0 46.9 jit_solution(5366259789777238557)
XLA Ops:
  0.6 0.0 copy-start
  0.6 3.1 %collective-permute-start = (bf16[64,256]{1,0:T(8,128)(2,1)}, bf16[64,256]{1,0:T(8,128)(2,1)S(1)}, u32[]{:S(2)}, u32[]{:S(2)}) collective-permute-start(bf16[64,256]{1,0:T(8,128)(2,1)} %feat_ref.3), channel_id=1, source_target_pairs={{0,8},{2,10},{4,12},{6,14},{8,0},{10,2},{12,4},{14,6},{16,24},{18,... | collective-permute-start | bytes 98312 | tf_op jit(solution)/shard_map/ppermute | solution.py:289
  3.7 2.6 %collective-permute-start.1 = (bf16[64,256]{1,0:T(8,128)(2,1)}, bf16[64,256]{1,0:T(8,128)(2,1)S(1)}, u32[]{:S(2)}, u32[]{:S(2)}) collective-permute-start(bf16[64,256]{1,0:T(8,128)(2,1)} %feat_ref.3), channel_id=1, source_target_pairs={{0,16},{2,18},{4,20},{6,22},{8,24},{10,26},{12,28},{14,30},{16,0},... | collective-permute-start | bytes 98312 | tf_op jit(solution)/shard_map/ppermute | solution.py:289
  6.3 0.0 collective-permute-start.2
  6.3 2.4 %shard_map.140 = bf16[336,256]{1,0:T(8,128)(2,1)} custom-call(bf16[64,256]{1,0:T(8,128)(2,1)} %self_ref.3, bf16[64,256]{1,0:T(8,128)(2,1)} %nbr_ref.5, bf16[128,256]{1,0:T(8,128)(2,1)} %cot_ref.3, f32[1,128]{1,0:T(1,128)} %bitcast.3, bf16[64,256]{1,0:T(8,128)(2,1)} %feat_ref.3), custom_call_target="tpu_custom_call" | custom-call | bytes 327680 | tf_op jit(solution)/shard_map/pallas_call | solution.py:305
  8.7 1.7 %collective-permute-start.7 = (bf16[336,256]{1,0:T(8,128)(2,1)}, bf16[336,256]{1,0:T(8,128)(2,1)S(1)}, u32[]{:S(2)}, u32[]{:S(2)}) collective-permute-start(bf16[336,256]{1,0:T(8,128)(2,1)} %shard_map.140), channel_id=1, source_target_pairs={{0,1},{1,0},{2,3},{3,2},{4,5},{5,4},{6,7},{7,6},{8,9},{9,8},{10,11... | collective-permute-start | bytes 516104 | tf_op jit(solution)/shard_map/ppermute | solution.py:299
  10.5 0.0 collective-permute-done.refs_1_
  10.5 0.0 collective-permute-done.1.refs_2_
  10.5 1.8 %collective-permute-done.2.refs_3_ = bf16[64,256]{1,0:T(8,128)(2,1)S(1)} collective-permute-done((bf16[64,256]{1,0:T(8,128)(2,1)}, bf16[64,256]{1,0:T(8,128)(2,1)S(1)}, u32[]{:S(2)}, u32[]{:S(2)}) %collective-permute-start.2) | collective-permute-done | bytes 32800 | tf_op jit(solution)/shard_map/ppermute | solution.py:289
  12.2 0.0 copy-start.1
  12.2 0.8 %copy-done.1 = bf16[64,256]{1,0:T(8,128)(2,1)S(1)} copy-done((bf16[64,256]{1,0:T(8,128)(2,1)S(1)}, bf16[64,256]{1,0:T(8,128)(2,1)}, u32[]{:S(2)}) %copy-start.1) | copy-done | bytes 32792
  13.0 0.0 copy-start.6
  13.0 0.0 copy-start.10
  13.0 0.0 copy-start.8
  13.0 0.0 copy-start.9
  13.0 0.1 collective-permute-start.3
  13.1 1.6 %collective-permute-start.4 = (bf16[256,256]{1,0:T(8,128)(2,1)S(1)}, bf16[256,256]{1,0:T(8,128)(2,1)S(1)}, u32[]{:S(2)}, u32[]{:S(2)}) collective-permute-start(bf16[256,256]{1,0:T(8,128)(2,1)S(1)} %shard_map.138.refs_0_), channel_id=1, source_target_pairs={{0,4},{2,6},{4,0},{6,2},{8,12},{10,14},{12,8},{14,10},{16,20},{18,... | collective-permute-start | bytes 393224 | tf_op jit(solution)/shard_map/ppermute | solution.py:289
  14.7 0.3 collective-permute-start.5
  15.0 0.0 copy-done
  15.0 0.0 copy-done.6
  15.0 0.0 copy-done.10
  15.0 0.0 copy-done.8
  15.0 0.0 copy-done.9
  15.0 5.0 %shard_map.137 = (bf16[1024,256]{1,0:T(8,128)(2,1)S(1)}, f32[64,256]{1,0:T(8,128)S(1)}, f32[24,256]{1,0:T(8,128)S(1)}, f32[16,256]{1,0:T(8,128)S(1)}) custom-call(s32[16]{0:T(128)S(1)} %copy-done.8, s32[16]{0:T(128)S(1)} %copy-done.10, s32[16,256]{1,0:T(8,128)S(1)} %copy-done.6, s32[1,256]{1,0:T(1,128)S(1)} %bitcast.5, bf16[64,4096]{1,0:T(8,128)(2,1)S(1)} %copy-done), custom_call_target="tpu_custom_call" | custom-call | flops 134217728 | bytes 16777216 | tf_op jit(solution)/shard_map/pallas_call | solution.py:320
  20.1 0.0 collective-permute-done.3.refs_1_
  20.1 0.0 collective-permute-done.4.refs_2_
  20.1 1.3 %collective-permute-done.5.refs_3_ = bf16[256,256]{1,0:T(8,128)(2,1)S(1)} collective-permute-done((bf16[256,256]{1,0:T(8,128)(2,1)S(1)}, bf16[256,256]{1,0:T(8,128)(2,1)S(1)}, u32[]{:S(2)}, u32[]{:S(2)}) %collective-permute-start.5) | collective-permute-done | bytes 131104 | tf_op jit(solution)/shard_map/ppermute | solution.py:289
  21.4 0.0 copy-start.2
  21.4 0.0 copy-start.3
  21.4 0.0 copy-start.4
  21.4 0.0 copy-start.5
  21.4 0.0 copy-start.7
  21.4 0.9 %shard_map.139.refs_0_ = bf16[64,256]{1,0:T(8,128)(2,1)S(1)} custom-call(s32[16]{0:T(128)S(1)} %copy-done.8, f32[24,256]{1,0:T(8,128)S(1)} %get-tuple-element.25.scale_ref, f32[64,256]{1,0:T(8,128)S(1)} %get-tuple-element.27.acc_ref, bf16[1024,256]{1,0:T(8,128)(2,1)S(1)} %get-tuple-element.26.listed_ref, bf16[256,256]{1,0:T(8,128)(2,1)S(1)} %shard_map.138.refs_0_, ...), custom_call_target="tpu_custom_call" | custom-call | bytes 524288 | tf_op jit(solution)/shard_map/pallas_call | solution.py:334
  22.4 1.6 %collective-permute-start.6 = (bf16[64,256]{1,0:T(8,128)(2,1)S(1)}, bf16[64,256]{1,0:T(8,128)(2,1)S(1)}, u32[]{:S(2)}, u32[]{:S(2)}) collective-permute-start(bf16[64,256]{1,0:T(8,128)(2,1)S(1)} %shard_map.139.refs_0_), channel_id=1, source_target_pairs={{0,1},{1,0},{2,3},{3,2},{4,5},{5,4},{6,7},{7,6},{8,9},{9,8},{10,11... | collective-permute-start | bytes 98312 | tf_op jit(solution)/shard_map/ppermute | solution.py:299
  23.9 0.0 collective-permute-done.7.refs_2_
  23.9 2.4 %collective-permute-done.6.refs_1_ = bf16[64,256]{1,0:T(8,128)(2,1)S(1)} collective-permute-done((bf16[64,256]{1,0:T(8,128)(2,1)S(1)}, bf16[64,256]{1,0:T(8,128)(2,1)S(1)}, u32[]{:S(2)}, u32[]{:S(2)}) %collective-permute-start.6) | collective-permute-done | bytes 32800 | tf_op jit(solution)/shard_map/ppermute | solution.py:299
  26.3 0.0 copy-done.2
  26.3 0.0 copy-done.3
  26.3 0.0 copy-done.4
  26.3 0.0 copy-done.5
  26.4 0.0 copy-done.7
  26.4 1.1 %shard_map.141 = (bf16[128,256]{1,0:T(8,128)(2,1)S(1)}, f32[64,256]{1,0:T(8,128)S(1)}, bf16[112,256]{1,0:T(8,128)(2,1)S(1)}, bf16[112,256]{1,0:T(8,128)(2,1)S(1)...) custom-call(f32[24,256]{1,0:T(8,128)S(1)} %get-tuple-element.25.scale_ref, ...), custom_call_target="tpu_custom_call" | custom-call | flops 83886080 | bytes 458752 | tf_op jit(solution)/shard_map/pallas_call | solution.py:345
  27.4 0.3 collective-permute-start.10
  27.8 1.4 %collective-permute-start.8 = (bf16[112,256]{1,0:T(8,128)(2,1)S(1)}, bf16[112,256]{1,0:T(8,128)(2,1)S(1)}, u32[]{:S(2)}, u32[]{:S(2)}) collective-permute-start(bf16[112,256]{1,0:T(8,128)(2,1)S(1)} %get-tuple-element.31), channel_id=1, source_target_pairs={{0,2},{2,0},{4,6},{6,4},{8,10},{10,8},{12,14},{14,12},{16,18},{18,... | collective-permute-start | bytes 172040 | tf_op jit(solution)/shard_map/ppermute | solution.py:289
  29.1 0.5 %collective-permute-start.9 = (bf16[112,256]{1,0:T(8,128)(2,1)S(1)}, bf16[112,256]{1,0:T(8,128)(2,1)S(1)}, u32[]{:S(2)}, u32[]{:S(2)}) collective-permute-start(bf16[112,256]{1,0:T(8,128)(2,1)S(1)} %get-tuple-element.32), channel_id=1, source_target_pairs={{0,4},{2,6},{4,0},{6,2},{8,12},{10,14},{12,8},{14,10},{16,20},{18,... | collective-permute-start | bytes 172040 | tf_op jit(solution)/shard_map/ppermute | solution.py:289
  29.7 2.0 %collective-permute-done.10.refs_3_ = bf16[112,256]{1,0:T(8,128)(2,1)S(1)} collective-permute-done((bf16[112,256]{1,0:T(8,128)(2,1)S(1)}, bf16[112,256]{1,0:T(8,128)(2,1)S(1)}, u32[]{:S(2)}, u32[]{:S(2)}) %collective-permute-start.10) | collective-permute-done | bytes 57376 | tf_op jit(solution)/shard_map/ppermute | solution.py:289
  31.7 0.0 collective-permute-done.8.refs_1_
  31.7 1.7 %collective-permute-done.9.refs_2_ = bf16[112,256]{1,0:T(8,128)(2,1)S(1)} collective-permute-done((bf16[112,256]{1,0:T(8,128)(2,1)S(1)}, bf16[112,256]{1,0:T(8,128)(2,1)S(1)}, u32[]{:S(2)}, u32[]{:S(2)}) %collective-permute-start.9) | collective-permute-done | bytes 57376 | tf_op jit(solution)/shard_map/ppermute | solution.py:289
  33.3 0.1 shard_map.142.refs_0_
  33.4 0.1 collective-permute-start.11
  33.5 2.4 %collective-permute-start.12 = (bf16[112,256]{1,0:T(8,128)(2,1)S(1)}, bf16[112,256]{1,0:T(8,128)(2,1)S(1)}, u32[]{:S(2)}, u32[]{:S(2)}) collective-permute-start(bf16[112,256]{1,0:T(8,128)(2,1)S(1)} %shard_map.142.refs_0_), channel_id=1, source_target_pairs={{0,16},{2,18},{4,20},{6,22},{8,24},{10,26},{12,28},{14,30},{16,0},... | collective-permute-start | bytes 172040 | tf_op jit(solution)/shard_map/ppermute | solution.py:289
  35.9 2.0 %collective-permute-start.13 = (bf16[112,256]{1,0:T(8,128)(2,1)S(1)}, bf16[112,256]{1,0:T(8,128)(2,1)S(1)}, u32[]{:S(2)}, u32[]{:S(2)}) collective-permute-start(bf16[112,256]{1,0:T(8,128)(2,1)S(1)} %shard_map.142.refs_0_), channel_id=1, source_target_pairs={{0,24},{2,26},{4,28},{6,30},{8,16},{10,18},{12,20},{14,22},{16,8},... | collective-permute-start | bytes 172040 | tf_op jit(solution)/shard_map/ppermute | solution.py:289
  37.9 0.0 collective-permute-done.11.refs_1_
  37.9 1.5 %collective-permute-done.12.refs_2_ = bf16[112,256]{1,0:T(8,128)(2,1)S(1)} collective-permute-done((bf16[112,256]{1,0:T(8,128)(2,1)S(1)}, bf16[112,256]{1,0:T(8,128)(2,1)S(1)}, u32[]{:S(2)}, u32[]{:S(2)}) %collective-permute-start.12) | collective-permute-done | bytes 57376 | tf_op jit(solution)/shard_map/ppermute | solution.py:289
  39.3 2.5 %collective-permute-done.13.refs_3_ = bf16[112,256]{1,0:T(8,128)(2,1)S(1)} collective-permute-done((bf16[112,256]{1,0:T(8,128)(2,1)S(1)}, bf16[112,256]{1,0:T(8,128)(2,1)S(1)}, u32[]{:S(2)}, u32[]{:S(2)}) %collective-permute-start.13) | collective-permute-done | bytes 57376 | tf_op jit(solution)/shard_map/ppermute | solution.py:289
  41.9 0.1 shard_map.143
  42.0 0.1 collective-permute-start.14
  42.0 0.6 %collective-permute-start.15 = (bf16[48,256]{1,0:T(8,128)(2,1)S(1)}, bf16[48,256]{1,0:T(8,128)(2,1)S(1)}, u32[]{:S(2)}, u32[]{:S(2)}) collective-permute-start(bf16[48,256]{1,0:T(8,128)(2,1)S(1)} %get-tuple-element.38), channel_id=1, source_target_pairs={{0,4},{2,6},{4,0},{6,2},{8,12},{10,14},{12,8},{14,10},{16,20},{18,... | collective-permute-start | bytes 73736 | tf_op jit(solution)/shard_map/ppermute | solution.py:289
  42.6 1.3 %collective-permute-start.16 = (bf16[48,256]{1,0:T(8,128)(2,1)S(1)}, bf16[48,256]{1,0:T(8,128)(2,1)S(1)}, u32[]{:S(2)}, u32[]{:S(2)}) collective-permute-start(bf16[48,256]{1,0:T(8,128)(2,1)S(1)} %get-tuple-element.39), channel_id=1, source_target_pairs={{0,6},{2,4},{4,2},{6,0},{8,14},{10,12},{12,10},{14,8},{16,22},{18,... | collective-permute-start | bytes 73736 | tf_op jit(solution)/shard_map/ppermute | solution.py:289
  43.9 0.0 collective-permute-done.14.refs_1_
  43.9 2.3 %collective-permute-done.15.refs_2_ = bf16[48,256]{1,0:T(8,128)(2,1)S(1)} collective-permute-done((bf16[48,256]{1,0:T(8,128)(2,1)S(1)}, bf16[48,256]{1,0:T(8,128)(2,1)S(1)}, u32[]{:S(2)}, u32[]{:S(2)}) %collective-permute-start.15) | collective-permute-done | bytes 24608 | tf_op jit(solution)/shard_map/ppermute | solution.py:289
  46.2 0.0 collective-permute-done.16.refs_3_
  46.2 0.7 %shard_map.144 = (bf16[128,256]{1,0:T(8,128)(2,1)}, bf16[64,256]{1,0:T(8,128)(2,1)}, f32[64,256]{1,0:T(8,128)}, f32[64,256]{1,0:T(8,128)}, f32[1,128]{1,0:T(1,128)}) custom-call(f32[24,256]{1,0:T(8,128)S(1)} %get-tuple-element.25.scale_ref, bf16[128,256]{1,0:T(8,128)(2,1)S(1)} %get-tuple-element.28.act_ref, f32[8,256]{1,0:T(8,128)S(1)} %get-tuple-element.34.bias_ref, ...), custom_call_target="tpu_custom_call" | custom-call | bytes 98304 | tf_op jit(solution)/shard_map/pallas_call | solution.py:381
  (1 shorter events, 0.0 us)
Async XLA Ops:
  0.6 14.4 %copy-start = (bf16[64,4096]{1,0:T(8,128)(2,1)S(1)}, bf16[64,4096]{1,0:T(8,128)(2,1)}, u32[]{:S(2)}) copy-start(bf16[64,4096]{1,0:T(8,128)(2,1)} %cache_ref.1) | copy-start | bytes 1572868
  0.6 9.8 %collective-permute-start = (bf16[64,256]{1,0:T(8,128)(2,1)}, bf16[64,256]{1,0:T(8,128)(2,1)S(1)}, u32[]{:S(2)}, u32[]{:S(2)}) collective-permute-start(bf16[64,256]{1,0:T(8,128)(2,1)} %feat_ref.3), channel_id=1, source_target_pairs={{0,8},{2,10},{4,12},{6,14},{8,0},{10,2},{12,4},{14,6},{16,24},{18,... | collective-permute-start | bytes 98312 | tf_op jit(solution)/shard_map/ppermute | solution.py:289
  3.7 6.8 %collective-permute-start.1 = (bf16[64,256]{1,0:T(8,128)(2,1)}, bf16[64,256]{1,0:T(8,128)(2,1)S(1)}, u32[]{:S(2)}, u32[]{:S(2)}) collective-permute-start(bf16[64,256]{1,0:T(8,128)(2,1)} %feat_ref.3), channel_id=1, source_target_pairs={{0,16},{2,18},{4,20},{6,22},{8,24},{10,26},{12,28},{14,30},{16,0},... | collective-permute-start | bytes 98312 | tf_op jit(solution)/shard_map/ppermute | solution.py:289
  6.3 5.9 %collective-permute-start.2 = (bf16[64,256]{1,0:T(8,128)(2,1)}, bf16[64,256]{1,0:T(8,128)(2,1)S(1)}, u32[]{:S(2)}, u32[]{:S(2)}) collective-permute-start(bf16[64,256]{1,0:T(8,128)(2,1)} %feat_ref.3), channel_id=1, source_target_pairs={{0,24},{2,26},{4,28},{6,30},{8,16},{10,18},{12,20},{14,22},{16,8},... | collective-permute-start | bytes 98312 | tf_op jit(solution)/shard_map/ppermute | solution.py:289
  8.7 15.2 %collective-permute-start.7 = (bf16[336,256]{1,0:T(8,128)(2,1)}, bf16[336,256]{1,0:T(8,128)(2,1)S(1)}, u32[]{:S(2)}, u32[]{:S(2)}) collective-permute-start(bf16[336,256]{1,0:T(8,128)(2,1)} %shard_map.140), channel_id=1, source_target_pairs={{0,1},{1,0},{2,3},{3,2},{4,5},{5,4},{6,7},{7,6},{8,9},{9,8},{10,11... | collective-permute-start | bytes 516104 | tf_op jit(solution)/shard_map/ppermute | solution.py:299
  12.2 0.8 %copy-start.1 = (bf16[64,256]{1,0:T(8,128)(2,1)S(1)}, bf16[64,256]{1,0:T(8,128)(2,1)}, u32[]{:S(2)}) copy-start(bf16[64,256]{1,0:T(8,128)(2,1)} %feat_ref.3) | copy-start | bytes 98308
  13.0 2.0 %copy-start.6 = (s32[16,256]{1,0:T(8,128)S(1)}, s32[16,256]{1,0:T(8,128)}, u32[]{:S(2)}) copy-start(s32[16,256]{1,0:T(8,128)} %nbr_ref.3) | copy-start | bytes 49156
  13.0 2.0 %copy-start.10 = (s32[16]{0:T(128)S(1)}, s32[16]{0:T(128)}, u32[]{:S(2)}) copy-start(s32[16]{0:T(128)} %counts_ref.1) | copy-start | bytes 196
  13.0 2.0 %copy-start.8 = (s32[16]{0:T(128)S(1)}, s32[16]{0:T(128)}, u32[]{:S(2)}) copy-start(s32[16]{0:T(128)} %stale_ref.3) | copy-start | bytes 196
  13.0 2.0 %copy-start.9 = (s32[256]{0:T(256)S(1)}, s32[256]{0:T(256)}, u32[]{:S(2)}) copy-start(s32[256]{0:T(256)} %param.15) | copy-start | bytes 3076
  13.0 7.0 %collective-permute-start.3 = (bf16[256,256]{1,0:T(8,128)(2,1)S(1)}, bf16[256,256]{1,0:T(8,128)(2,1)S(1)}, u32[]{:S(2)}, u32[]{:S(2)}) collective-permute-start(bf16[256,256]{1,0:T(8,128)(2,1)S(1)} %shard_map.138.refs_0_), channel_id=1, source_target_pairs={{0,2},{2,0},{4,6},{6,4},{8,10},{10,8},{12,14},{14,12},{16,18},{18,... | collective-permute-start | bytes 393224 | tf_op jit(solution)/shard_map/ppermute | solution.py:289
  13.1 6.9 %collective-permute-start.4 = (bf16[256,256]{1,0:T(8,128)(2,1)S(1)}, bf16[256,256]{1,0:T(8,128)(2,1)S(1)}, u32[]{:S(2)}, u32[]{:S(2)}) collective-permute-start(bf16[256,256]{1,0:T(8,128)(2,1)S(1)} %shard_map.138.refs_0_), channel_id=1, source_target_pairs={{0,4},{2,6},{4,0},{6,2},{8,12},{10,14},{12,8},{14,10},{16,20},{18,... | collective-permute-start | bytes 393224 | tf_op jit(solution)/shard_map/ppermute | solution.py:289
  14.7 6.7 %collective-permute-start.5 = (bf16[256,256]{1,0:T(8,128)(2,1)S(1)}, bf16[256,256]{1,0:T(8,128)(2,1)S(1)}, u32[]{:S(2)}, u32[]{:S(2)}) collective-permute-start(bf16[256,256]{1,0:T(8,128)(2,1)S(1)} %shard_map.138.refs_0_), channel_id=1, source_target_pairs={{0,6},{2,4},{4,2},{6,0},{8,14},{10,12},{12,10},{14,8},{16,22},{18,... | collective-permute-start | bytes 393224 | tf_op jit(solution)/shard_map/ppermute | solution.py:289
  21.4 5.0 %copy-start.2 = (bf16[64,256]{1,0:T(8,128)(2,1)S(1)}, bf16[64,256]{1,0:T(8,128)(2,1)}, u32[]{:S(2)}) copy-start(bf16[64,256]{1,0:T(8,128)(2,1)} %feat_ref.3) | copy-start | bytes 98308
  21.4 5.0 %copy-start.3 = (bf16[128,256]{1,0:T(8,128)(2,1)S(1)}, bf16[128,256]{1,0:T(8,128)(2,1)}, u32[]{:S(2)}) copy-start(bf16[128,256]{1,0:T(8,128)(2,1)} %cot_ref.3) | copy-start | bytes 196612
  21.4 5.0 %copy-start.4 = (bf16[64,256]{1,0:T(8,128)(2,1)S(1)}, bf16[64,256]{1,0:T(8,128)(2,1)}, u32[]{:S(2)}) copy-start(bf16[64,256]{1,0:T(8,128)(2,1)} %self_ref.3) | copy-start | bytes 98308
  21.4 5.0 %copy-start.5 = (bf16[64,256]{1,0:T(8,128)(2,1)S(1)}, bf16[64,256]{1,0:T(8,128)(2,1)}, u32[]{:S(2)}) copy-start(bf16[64,256]{1,0:T(8,128)(2,1)} %nbr_ref.5) | copy-start | bytes 98308
  21.4 5.0 %copy-start.7 = (f32[128]{0:T(128)S(1)}, f32[128]{0:T(128)}, u32[]{:S(2)}) copy-start(f32[128]{0:T(128)} %param.18) | copy-start | bytes 1540
  22.4 4.0 %collective-permute-start.6 = (bf16[64,256]{1,0:T(8,128)(2,1)S(1)}, bf16[64,256]{1,0:T(8,128)(2,1)S(1)}, u32[]{:S(2)}, u32[]{:S(2)}) collective-permute-start(bf16[64,256]{1,0:T(8,128)(2,1)S(1)} %shard_map.139.refs_0_), channel_id=1, source_target_pairs={{0,1},{1,0},{2,3},{3,2},{4,5},{5,4},{6,7},{7,6},{8,9},{9,8},{10,11... | collective-permute-start | bytes 98312 | tf_op jit(solution)/shard_map/ppermute | solution.py:299
  27.4 4.2 %collective-permute-start.10 = (bf16[112,256]{1,0:T(8,128)(2,1)S(1)}, bf16[112,256]{1,0:T(8,128)(2,1)S(1)}, u32[]{:S(2)}, u32[]{:S(2)}) collective-permute-start(bf16[112,256]{1,0:T(8,128)(2,1)S(1)} %get-tuple-element.33), channel_id=1, source_target_pairs={{0,6},{2,4},{4,2},{6,0},{8,14},{10,12},{12,10},{14,8},{16,22},{18,... | collective-permute-start | bytes 172040 | tf_op jit(solution)/shard_map/ppermute | solution.py:289
  27.8 3.9 %collective-permute-start.8 = (bf16[112,256]{1,0:T(8,128)(2,1)S(1)}, bf16[112,256]{1,0:T(8,128)(2,1)S(1)}, u32[]{:S(2)}, u32[]{:S(2)}) collective-permute-start(bf16[112,256]{1,0:T(8,128)(2,1)S(1)} %get-tuple-element.31), channel_id=1, source_target_pairs={{0,2},{2,0},{4,6},{6,4},{8,10},{10,8},{12,14},{14,12},{16,18},{18,... | collective-permute-start | bytes 172040 | tf_op jit(solution)/shard_map/ppermute | solution.py:289
  29.1 4.2 %collective-permute-start.9 = (bf16[112,256]{1,0:T(8,128)(2,1)S(1)}, bf16[112,256]{1,0:T(8,128)(2,1)S(1)}, u32[]{:S(2)}, u32[]{:S(2)}) collective-permute-start(bf16[112,256]{1,0:T(8,128)(2,1)S(1)} %get-tuple-element.32), channel_id=1, source_target_pairs={{0,4},{2,6},{4,0},{6,2},{8,12},{10,14},{12,8},{14,10},{16,20},{18,... | collective-permute-start | bytes 172040 | tf_op jit(solution)/shard_map/ppermute | solution.py:289
  33.4 4.5 %collective-permute-start.11 = (bf16[112,256]{1,0:T(8,128)(2,1)S(1)}, bf16[112,256]{1,0:T(8,128)(2,1)S(1)}, u32[]{:S(2)}, u32[]{:S(2)}) collective-permute-start(bf16[112,256]{1,0:T(8,128)(2,1)S(1)} %shard_map.142.refs_0_), channel_id=1, source_target_pairs={{0,8},{2,10},{4,12},{6,14},{8,0},{10,2},{12,4},{14,6},{16,24},{18,... | collective-permute-start | bytes 172040 | tf_op jit(solution)/shard_map/ppermute | solution.py:289
  33.5 5.8 %collective-permute-start.12 = (bf16[112,256]{1,0:T(8,128)(2,1)S(1)}, bf16[112,256]{1,0:T(8,128)(2,1)S(1)}, u32[]{:S(2)}, u32[]{:S(2)}) collective-permute-start(bf16[112,256]{1,0:T(8,128)(2,1)S(1)} %shard_map.142.refs_0_), channel_id=1, source_target_pairs={{0,16},{2,18},{4,20},{6,22},{8,24},{10,26},{12,28},{14,30},{16,0},... | collective-permute-start | bytes 172040 | tf_op jit(solution)/shard_map/ppermute | solution.py:289
  35.9 6.0 %collective-permute-start.13 = (bf16[112,256]{1,0:T(8,128)(2,1)S(1)}, bf16[112,256]{1,0:T(8,128)(2,1)S(1)}, u32[]{:S(2)}, u32[]{:S(2)}) collective-permute-start(bf16[112,256]{1,0:T(8,128)(2,1)S(1)} %shard_map.142.refs_0_), channel_id=1, source_target_pairs={{0,24},{2,26},{4,28},{6,30},{8,16},{10,18},{12,20},{14,22},{16,8},... | collective-permute-start | bytes 172040 | tf_op jit(solution)/shard_map/ppermute | solution.py:289
  42.0 1.9 %collective-permute-start.14 = (bf16[48,256]{1,0:T(8,128)(2,1)S(1)}, bf16[48,256]{1,0:T(8,128)(2,1)S(1)}, u32[]{:S(2)}, u32[]{:S(2)}) collective-permute-start(bf16[48,256]{1,0:T(8,128)(2,1)S(1)} %get-tuple-element.37), channel_id=1, source_target_pairs={{0,2},{2,0},{4,6},{6,4},{8,10},{10,8},{12,14},{14,12},{16,18},{18,... | collective-permute-start | bytes 73736 | tf_op jit(solution)/shard_map/ppermute | solution.py:289
  42.0 4.1 %collective-permute-start.15 = (bf16[48,256]{1,0:T(8,128)(2,1)S(1)}, bf16[48,256]{1,0:T(8,128)(2,1)S(1)}, u32[]{:S(2)}, u32[]{:S(2)}) collective-permute-start(bf16[48,256]{1,0:T(8,128)(2,1)S(1)} %get-tuple-element.38), channel_id=1, source_target_pairs={{0,4},{2,6},{4,0},{6,2},{8,12},{10,14},{12,8},{14,10},{16,20},{18,... | collective-permute-start | bytes 73736 | tf_op jit(solution)/shard_map/ppermute | solution.py:289
  42.6 3.5 %collective-permute-start.16 = (bf16[48,256]{1,0:T(8,128)(2,1)S(1)}, bf16[48,256]{1,0:T(8,128)(2,1)S(1)}, u32[]{:S(2)}, u32[]{:S(2)}) collective-permute-start(bf16[48,256]{1,0:T(8,128)(2,1)S(1)} %get-tuple-element.39), channel_id=1, source_target_pairs={{0,6},{2,4},{4,2},{6,0},{8,14},{10,12},{12,10},{14,8},{16,22},{18,... | collective-permute-start | bytes 73736 | tf_op jit(solution)/shard_map/ppermute | solution.py:289

commit v7 on v6

--- a/solution.py
+++ b/solution.py
@@ -53,7 +53,7 @@
 
 
 def count_body(
-    stale_ref, counts_ref, nbr_ref, deg_ref, cache_ref, listed_ref, acc_ref, scale_ref, pick_ref, all_ref, ranks
+    stale_ref, counts_ref, nbr_ref, deg_ref, cache_ref, listed_ref, acc_ref, scale_ref, pick_ref, find_ref, all_ref, ranks
 ):
     slots, nodes = nbr_ref.shape
     listed = listed_ref.shape[0] // nodes
@@ -68,6 +68,12 @@
     me = lax.axis_index("dom")
     scale_ref[16:24, :] = jnp.full((8, nodes), is_fresh(stale_ref, me).astype(F32))
     fill_ranks(stale_ref, ranks)
+    for m in range(stale_ref.shape[0]):
+        part = jnp.bitwise_xor(me, m)
+        place = jnp.where(is_fresh(stale_ref, part), ranks[part], -1)
+        for r in range(listed):
+            row = r * stale_ref.shape[0] + m
+            find_ref[row : row + 1, :] = jnp.full((1, nodes), (place == r).astype(F32))
     for q in range(LOW):
         place = ranks[me // LOW * LOW + q]
         for r in range(listed):
@@ -98,22 +104,21 @@
     acc_ref[...] = jnp.dot(cache_ref[...], all_ref[...], preferred_element_type=F32)
 
 
-def pack_body(self_ref, nbr_ref, cot_ref, bias_ref, feat_ref, out_ref, bias, wide, sems):
-    row = feat_ref.shape[0]
+def pack_body(feat_ref, self_ref, nbr_ref, cot_ref, bias_ref, out_ref, bias, wide, sems):
+    row = 0
     copies = []
-    for i, ref in enumerate((self_ref, nbr_ref, cot_ref)):
+    for i, ref in enumerate((feat_ref, self_ref, nbr_ref, cot_ref)):
         copies.append(pltpu.make_async_copy(ref, out_ref.at[row : row + ref.shape[0], :], sems.at[i]))
         row += ref.shape[0]
-    copies.append(pltpu.make_async_copy(bias_ref, bias, sems.at[3]))
+    copies.append(pltpu.make_async_copy(bias_ref, bias, sems.at[4]))
     for copy in copies:
         copy.start()
     wide[...] = jnp.zeros_like(wide)
-    out_ref[: feat_ref.shape[0], :] = feat_ref[...]
-    copies[3].wait()
+    copies[4].wait()
     for i, term in enumerate(split3(bias[...])):
         wide[i : i + 1, : bias.shape[1]] = term
     out_ref[row:, :] = wide[...].astype(BF16)
-    for copy in copies[:3]:
+    for copy in copies[:4]:
         copy.wait()
 
 
@@ -124,23 +129,24 @@
         out_ref[i * rows : (i + 1) * rows, :] = ref[...]
 
 
-def mean_body(stale_ref, scale_ref, acc_ref, listed_ref, *refs):
-    stacks, (out_ref, blocks, ranks) = refs[:LOW], refs[LOW:]
+def mean_body(find_ref, scale_ref, acc_ref, listed_ref, *refs):
+    stacks, out_ref = refs[:LOW], refs[LOW]
     width, nodes = acc_ref.shape
-    me = lax.axis_index("dom")
-    fill_ranks(stale_ref, ranks)
-    for low in range(LOW):
-        for high in range(stacks[0].shape[0] // width):
-            part = jnp.bitwise_xor(me, low + LOW * high)
-
-            @pl.when(is_fresh(stale_ref, part))
-            def _(low=low, high=high, part=part):
-                blocks[ranks[part]] = stacks[low][high * width : (high + 1) * width, :]
-
+    listed = listed_ref.shape[0] // nodes
+    dom = find_ref.shape[0] // listed
     total = acc_ref[...]
-    for r in range(blocks.shape[0]):
+    for r in range(listed):
+        block = jnp.zeros((width // 16, 16, nodes), BF16)
+        for m in range(dom):
+            row = r * dom + m
+            one = jnp.broadcast_to(find_ref[row : row + 1, :], (16, nodes)).astype(BF16)
+            low, high = m % LOW, m // LOW
+            part = stacks[low][high * width : (high + 1) * width, :].reshape(width // 16, 16, nodes)
+            block = block + part * one[None]
         total += jnp.dot(
-            blocks[r], listed_ref[r * nodes : (r + 1) * nodes, :], preferred_element_type=F32
+            block.reshape(width, nodes),
+            listed_ref[r * nodes : (r + 1) * nodes, :],
+            preferred_element_type=F32,
         )
     out_ref[...] = (total * scale_ref[8:9, :]).astype(BF16)
 
@@ -306,24 +312,25 @@
         pack_body,
         shape((3 * width + part_h + 16, nodes), BF16),
         0,
-        1,
-        [pltpu.VMEM((1, part_h), F32), pltpu.VMEM((16, nodes), F32), pltpu.SemaphoreType.DMA((4,))],
+        0,
+        [pltpu.VMEM((1, part_h), F32), pltpu.VMEM((16, nodes), F32), pltpu.SemaphoreType.DMA((5,))],
         moved=4 * (3 * width + part_h) * nodes,
-        hbm_count=4,
-    )(w_self, w_nbr, cotangent, bias_row, features)
+        hbm_count=5,
+    )(features, w_self, w_nbr, cotangent, bias_row)
     packs = around(packed)
     deg = degrees.reshape(1, nodes)
     stacked = call(stack_body, shape((width * len(line), nodes), BF16), 0, len(line), moved=4 * dom * width * nodes // LOW)(
         *line
     )
     stacks = within([stacked] * LOW)
-    counts, acc, scale, picks = call(
+    counts, acc, scale, picks, finds = call(
         count_body,
         (
             shape((listed * nodes, nodes), BF16),
             shape((width, nodes), F32),
             shape((24, nodes), F32),
             shape((LOW * listed, nodes), F32),
+            shape((dom * listed, nodes), F32),
         ),
         2,
         3,
@@ -334,11 +341,10 @@
     agg = call(
         mean_body,
         shape((width, nodes), BF16),
-        1,
-        3 + LOW,
-        [pltpu.VMEM((listed, width, nodes), BF16), pltpu.SMEM((dom,), jnp.int32)],
+        0,
+        4 + LOW,
         moved=2 * dom * width * nodes,
-    )(staleness, scale, acc, counts, *stacks)
+    )(finds, scale, acc, counts, *stacks)
     aggs = [agg] + around(agg)
     base = listed * (width // LOW) + width // 2
     rows = up16(base + 2)

time: 47.2 us -> 45.8 us (0.970)
  Pallas kernels: 10.3 us -> 9.03 us
    pallas_call x2, Pallas kernels: 3.34 us -> 1.93 us  [the longest x1 1.61 us: per_device(): call(pack_body, shape((3 * width + part_h + 16, nodes), BF16), 0, 0, [plt...]
  transfers between devices with their start and end apart: 17 -> 17, of which waited for: 8 -> 8; matrix products, arithmetic and copies ran while one was open for 0% -> 0% of each run, Pallas kernels for 18% -> 16%
where the time goes in v7:
time: 45.8 us; the launch traced here: 45.5 us
  starting transfers between devices  19.5 us (43%)
  waiting for transfers between devices  15.4 us (34%)
  Pallas kernels  9.03 us (20%)
  local copies, waits for them, and re-layouts  0.8 us (2%)
  between operations  0.79 us (2%)
    ppermute x15, starting transfers between devices, hop(): return lax.ppermute(block, 'dom', [(i, i ^ m) for i in range(dom)])  16.2 us
    ppermute x15, waiting for transfers between devices, hop(): return lax.ppermute(block, 'dom', [(i, i ^ m) for i in range(dom)])  13 us
    pallas_call x1, Pallas kernels, per_device(): call(count_body, (shape((listed * nodes, nodes), BF16), shape((width, nod...  5.14 us
    ppermute x2, starting transfers between devices, around(): lax.ppermute(block, 'col', [(i, (i + s) % n_col) for i in range(n_col)])  3.33 us
    ppermute x2, waiting for transfers between devices, around(): lax.ppermute(block, 'col', [(i, (i + s) % n_col) for i in range(n_col)])  2.42 us
    pallas_call x1, Pallas kernels, per_device(): call(pack_body, shape((3 * width + part_h + 16, nodes), BF16), 0, 0, [plt...  1.61 us
    pallas_call x1, Pallas kernels, per_device(): call(functools.partial(dense_body, n_col), [shape((part_h, nodes), BF16),...  1.07 us
  transfers between devices with their start and end apart: 17, of which 8 were waited for; matrix products, arithmetic and copies ran while one was open for 0% of the time, Pallas kernels for 16%

profile of v7, /device:TPU:0, one launch (start us, length us, event | category | flops | bytes accessed | tf_op | source)
XLA Modules:
  0.0 45.5 jit_solution(11959741322940824966)
XLA Ops:
  0.6 0.0 copy-start
  0.6 3.1 %collective-permute-start = (bf16[64,256]{1,0:T(8,128)(2,1)}, bf16[64,256]{1,0:T(8,128)(2,1)S(1)}, u32[]{:S(2)}, u32[]{:S(2)}) collective-permute-start(bf16[64,256]{1,0:T(8,128)(2,1)} %feat_ref.3), channel_id=1, source_target_pairs={{0,8},{2,10},{4,12},{6,14},{8,0},{10,2},{12,4},{14,6},{16,24},{18,... | collective-permute-start | bytes 98312 | tf_op jit(solution)/shard_map/ppermute | solution.py:295
  3.7 2.6 %collective-permute-start.1 = (bf16[64,256]{1,0:T(8,128)(2,1)}, bf16[64,256]{1,0:T(8,128)(2,1)S(1)}, u32[]{:S(2)}, u32[]{:S(2)}) collective-permute-start(bf16[64,256]{1,0:T(8,128)(2,1)} %feat_ref.3), channel_id=1, source_target_pairs={{0,16},{2,18},{4,20},{6,22},{8,24},{10,26},{12,28},{14,30},{16,0},... | collective-permute-start | bytes 98312 | tf_op jit(solution)/shard_map/ppermute | solution.py:295
  6.3 0.0 collective-permute-start.2
  6.3 1.6 %shard_map.140 = bf16[336,256]{1,0:T(8,128)(2,1)} custom-call(bf16[64,256]{1,0:T(8,128)(2,1)} %feat_ref.3, bf16[64,256]{1,0:T(8,128)(2,1)} %self_ref.3, bf16[64,256]{1,0:T(8,128)(2,1)} %nbr_ref.5, bf16[128,256]{1,0:T(8,128)(2,1)} %cot_ref.3, f32[1,128]{1,0:T(1,128)} %bitcast.3), custom_call_target="tpu_custom_call" | custom-call | bytes 327680 | tf_op jit(solution)/shard_map/pallas_call | solution.py:311
  7.9 1.8 %collective-permute-start.7 = (bf16[336,256]{1,0:T(8,128)(2,1)}, bf16[336,256]{1,0:T(8,128)(2,1)S(1)}, u32[]{:S(2)}, u32[]{:S(2)}) collective-permute-start(bf16[336,256]{1,0:T(8,128)(2,1)} %shard_map.140), channel_id=1, source_target_pairs={{0,1},{1,0},{2,3},{3,2},{4,5},{5,4},{6,7},{7,6},{8,9},{9,8},{10,11... | collective-permute-start | bytes 516104 | tf_op jit(solution)/shard_map/ppermute | solution.py:305
  9.7 0.0 collective-permute-done.refs_1_
  9.7 0.0 collective-permute-done.1.refs_2_
  9.7 2.5 %collective-permute-done.2.refs_3_ = bf16[64,256]{1,0:T(8,128)(2,1)S(1)} collective-permute-done((bf16[64,256]{1,0:T(8,128)(2,1)}, bf16[64,256]{1,0:T(8,128)(2,1)S(1)}, u32[]{:S(2)}, u32[]{:S(2)}) %collective-permute-start.2) | collective-permute-done | bytes 32800 | tf_op jit(solution)/shard_map/ppermute | solution.py:295
  12.2 0.0 copy-start.1
  12.2 0.8 %copy-done.1 = bf16[64,256]{1,0:T(8,128)(2,1)S(1)} copy-done((bf16[64,256]{1,0:T(8,128)(2,1)S(1)}, bf16[64,256]{1,0:T(8,128)(2,1)}, u32[]{:S(2)}) %copy-start.1) | copy-done | bytes 32792
  13.0 0.0 copy-start.6
  13.0 0.0 copy-start.10
  13.0 0.0 copy-start.8
  13.0 0.0 copy-start.9
  13.0 0.1 collective-permute-start.3
  13.1 1.6 %collective-permute-start.4 = (bf16[256,256]{1,0:T(8,128)(2,1)S(1)}, bf16[256,256]{1,0:T(8,128)(2,1)S(1)}, u32[]{:S(2)}, u32[]{:S(2)}) collective-permute-start(bf16[256,256]{1,0:T(8,128)(2,1)S(1)} %shard_map.138.refs_0_), channel_id=1, source_target_pairs={{0,4},{2,6},{4,0},{6,2},{8,12},{10,14},{12,8},{14,10},{16,20},{18,... | collective-permute-start | bytes 393224 | tf_op jit(solution)/shard_map/ppermute | solution.py:295
  14.7 0.3 collective-permute-start.5
  15.0 0.0 copy-done
  15.0 0.0 copy-done.6
  15.0 0.0 copy-done.10
  15.0 0.0 copy-done.8
  15.0 0.0 copy-done.9
  15.0 5.1 %shard_map.137 = (bf16[1024,256]{1,0:T(8,128)(2,1)S(1)}, f32[64,256]{1,0:T(8,128)S(1)}, f32[24,256]{1,0:T(8,128)S(1)}, f32[16,256]{1,0:T(8,128)S(1)}, f32[64,256]{1,0:T(8,128)S(1)}) custom-call(s32[16]{0:T(128)S(1)} %copy-done.9, s32[16]{0:T(128)S(1)} %copy-done.10, s32[16,256]{1,0:T(8,128)S(1)} %copy-done.6, s32[1,256]{1,0:T(1,128)S(1)} %bitcast.5, ...), custom_call_target="tpu_custom_call" | custom-call | flops 134217728 | bytes 16777216 | tf_op jit(solution)/shard_map/pallas_call | solution.py:326
  20.2 0.0 collective-permute-done.3.refs_1_
  20.2 0.0 collective-permute-done.4.refs_2_
  20.2 1.2 %collective-permute-done.5.refs_3_ = bf16[256,256]{1,0:T(8,128)(2,1)S(1)} collective-permute-done((bf16[256,256]{1,0:T(8,128)(2,1)S(1)}, bf16[256,256]{1,0:T(8,128)(2,1)S(1)}, u32[]{:S(2)}, u32[]{:S(2)}) %collective-permute-start.5) | collective-permute-done | bytes 131104 | tf_op jit(solution)/shard_map/ppermute | solution.py:295
  21.4 0.0 copy-start.2
  21.4 0.0 copy-start.3
  21.4 0.0 copy-start.4
  21.4 0.0 copy-start.5
  21.4 0.0 copy-start.7
  21.4 0.3 shard_map.139.refs_0_
  21.7 1.6 %collective-permute-start.6 = (bf16[64,256]{1,0:T(8,128)(2,1)S(1)}, bf16[64,256]{1,0:T(8,128)(2,1)S(1)}, u32[]{:S(2)}, u32[]{:S(2)}) collective-permute-start(bf16[64,256]{1,0:T(8,128)(2,1)S(1)} %shard_map.139.refs_0_), channel_id=1, source_target_pairs={{0,1},{1,0},{2,3},{3,2},{4,5},{5,4},{6,7},{7,6},{8,9},{9,8},{10,11... | collective-permute-start | bytes 98312 | tf_op jit(solution)/shard_map/ppermute | solution.py:305
  23.3 0.0 collective-permute-done.7.refs_2_
  23.3 2.4 %collective-permute-done.6.refs_1_ = bf16[64,256]{1,0:T(8,128)(2,1)S(1)} collective-permute-done((bf16[64,256]{1,0:T(8,128)(2,1)S(1)}, bf16[64,256]{1,0:T(8,128)(2,1)S(1)}, u32[]{:S(2)}, u32[]{:S(2)}) %collective-permute-start.6) | collective-permute-done | bytes 32800 | tf_op jit(solution)/shard_map/ppermute | solution.py:305
  25.7 0.0 copy-done.2
  25.7 0.0 copy-done.3
  25.7 0.0 copy-done.4
  25.7 0.0 copy-done.5
  25.7 0.0 copy-done.7
  25.7 1.1 %shard_map.141 = (bf16[128,256]{1,0:T(8,128)(2,1)S(1)}, f32[64,256]{1,0:T(8,128)S(1)}, bf16[112,256]{1,0:T(8,128)(2,1)S(1)}, bf16[112,256]{1,0:T(8,128)(2,1)S(1)...) custom-call(f32[24,256]{1,0:T(8,128)S(1)} %get-tuple-element.26.scale_ref, ...), custom_call_target="tpu_custom_call" | custom-call | flops 83886080 | bytes 458752 | tf_op jit(solution)/shard_map/pallas_call | solution.py:351
  26.8 0.3 collective-permute-start.10
  27.1 1.4 %collective-permute-start.8 = (bf16[112,256]{1,0:T(8,128)(2,1)S(1)}, bf16[112,256]{1,0:T(8,128)(2,1)S(1)}, u32[]{:S(2)}, u32[]{:S(2)}) collective-permute-start(bf16[112,256]{1,0:T(8,128)(2,1)S(1)} %get-tuple-element.33), channel_id=1, source_target_pairs={{0,2},{2,0},{4,6},{6,4},{8,10},{10,8},{12,14},{14,12},{16,18},{18,... | collective-permute-start | bytes 172040 | tf_op jit(solution)/shard_map/ppermute | solution.py:295
  28.5 0.5 %collective-permute-start.9 = (bf16[112,256]{1,0:T(8,128)(2,1)S(1)}, bf16[112,256]{1,0:T(8,128)(2,1)S(1)}, u32[]{:S(2)}, u32[]{:S(2)}) collective-permute-start(bf16[112,256]{1,0:T(8,128)(2,1)S(1)} %get-tuple-element.34), channel_id=1, source_target_pairs={{0,4},{2,6},{4,0},{6,2},{8,12},{10,14},{12,8},{14,10},{16,20},{18,... | collective-permute-start | bytes 172040 | tf_op jit(solution)/shard_map/ppermute | solution.py:295
  29.0 2.0 %collective-permute-done.10.refs_3_ = bf16[112,256]{1,0:T(8,128)(2,1)S(1)} collective-permute-done((bf16[112,256]{1,0:T(8,128)(2,1)S(1)}, bf16[112,256]{1,0:T(8,128)(2,1)S(1)}, u32[]{:S(2)}, u32[]{:S(2)}) %collective-permute-start.10) | collective-permute-done | bytes 57376 | tf_op jit(solution)/shard_map/ppermute | solution.py:295
  31.0 0.0 collective-permute-done.8.refs_1_
  31.0 1.7 %collective-permute-done.9.refs_2_ = bf16[112,256]{1,0:T(8,128)(2,1)S(1)} collective-permute-done((bf16[112,256]{1,0:T(8,128)(2,1)S(1)}, bf16[112,256]{1,0:T(8,128)(2,1)S(1)}, u32[]{:S(2)}, u32[]{:S(2)}) %collective-permute-start.9) | collective-permute-done | bytes 57376 | tf_op jit(solution)/shard_map/ppermute | solution.py:295
  32.7 0.1 shard_map.142.refs_0_
  32.8 0.1 collective-permute-start.11
  32.9 1.6 %collective-permute-start.12 = (bf16[112,256]{1,0:T(8,128)(2,1)S(1)}, bf16[112,256]{1,0:T(8,128)(2,1)S(1)}, u32[]{:S(2)}, u32[]{:S(2)}) collective-permute-start(bf16[112,256]{1,0:T(8,128)(2,1)S(1)} %shard_map.142.refs_0_), channel_id=1, source_target_pairs={{0,16},{2,18},{4,20},{6,22},{8,24},{10,26},{12,28},{14,30},{16,0},... | collective-permute-start | bytes 172040 | tf_op jit(solution)/shard_map/ppermute | solution.py:295
  34.5 2.7 %collective-permute-start.13 = (bf16[112,256]{1,0:T(8,128)(2,1)S(1)}, bf16[112,256]{1,0:T(8,128)(2,1)S(1)}, u32[]{:S(2)}, u32[]{:S(2)}) collective-permute-start(bf16[112,256]{1,0:T(8,128)(2,1)S(1)} %shard_map.142.refs_0_), channel_id=1, source_target_pairs={{0,24},{2,26},{4,28},{6,30},{8,16},{10,18},{12,20},{14,22},{16,8},... | collective-permute-start | bytes 172040 | tf_op jit(solution)/shard_map/ppermute | solution.py:295
  37.2 0.0 collective-permute-done.11.refs_1_
  37.2 1.2 %collective-permute-done.12.refs_2_ = bf16[112,256]{1,0:T(8,128)(2,1)S(1)} collective-permute-done((bf16[112,256]{1,0:T(8,128)(2,1)S(1)}, bf16[112,256]{1,0:T(8,128)(2,1)S(1)}, u32[]{:S(2)}, u32[]{:S(2)}) %collective-permute-start.12) | collective-permute-done | bytes 57376 | tf_op jit(solution)/shard_map/ppermute | solution.py:295
  38.4 2.1 %collective-permute-done.13.refs_3_ = bf16[112,256]{1,0:T(8,128)(2,1)S(1)} collective-permute-done((bf16[112,256]{1,0:T(8,128)(2,1)S(1)}, bf16[112,256]{1,0:T(8,128)(2,1)S(1)}, u32[]{:S(2)}, u32[]{:S(2)}) %collective-permute-start.13) | collective-permute-done | bytes 57376 | tf_op jit(solution)/shard_map/ppermute | solution.py:295
  40.5 0.1 shard_map.143
  40.6 0.1 collective-permute-start.14
  40.7 0.7 %collective-permute-start.15 = (bf16[48,256]{1,0:T(8,128)(2,1)S(1)}, bf16[48,256]{1,0:T(8,128)(2,1)S(1)}, u32[]{:S(2)}, u32[]{:S(2)}) collective-permute-start(bf16[48,256]{1,0:T(8,128)(2,1)S(1)} %get-tuple-element.40), channel_id=1, source_target_pairs={{0,4},{2,6},{4,0},{6,2},{8,12},{10,14},{12,8},{14,10},{16,20},{18,... | collective-permute-start | bytes 73736 | tf_op jit(solution)/shard_map/ppermute | solution.py:295
  41.3 1.2 %collective-permute-start.16 = (bf16[48,256]{1,0:T(8,128)(2,1)S(1)}, bf16[48,256]{1,0:T(8,128)(2,1)S(1)}, u32[]{:S(2)}, u32[]{:S(2)}) collective-permute-start(bf16[48,256]{1,0:T(8,128)(2,1)S(1)} %get-tuple-element.41), channel_id=1, source_target_pairs={{0,6},{2,4},{4,2},{6,0},{8,14},{10,12},{12,10},{14,8},{16,22},{18,... | collective-permute-start | bytes 73736 | tf_op jit(solution)/shard_map/ppermute | solution.py:295
  42.5 0.0 collective-permute-done.14.refs_1_
  42.5 2.3 %collective-permute-done.15.refs_2_ = bf16[48,256]{1,0:T(8,128)(2,1)S(1)} collective-permute-done((bf16[48,256]{1,0:T(8,128)(2,1)S(1)}, bf16[48,256]{1,0:T(8,128)(2,1)S(1)}, u32[]{:S(2)}, u32[]{:S(2)}) %collective-permute-start.15) | collective-permute-done | bytes 24608 | tf_op jit(solution)/shard_map/ppermute | solution.py:295
  44.8 0.0 collective-permute-done.16.refs_3_
  44.8 0.7 %shard_map.144 = (bf16[128,256]{1,0:T(8,128)(2,1)}, bf16[64,256]{1,0:T(8,128)(2,1)}, f32[64,256]{1,0:T(8,128)}, f32[64,256]{1,0:T(8,128)}, f32[1,128]{1,0:T(1,128)}) custom-call(f32[24,256]{1,0:T(8,128)S(1)} %get-tuple-element.26.scale_ref, bf16[128,256]{1,0:T(8,128)(2,1)S(1)} %get-tuple-element.30.act_ref, f32[8,256]{1,0:T(8,128)S(1)} %get-tuple-element.36.bias_ref, ...), custom_call_target="tpu_custom_call" | custom-call | bytes 98304 | tf_op jit(solution)/shard_map/pallas_call | solution.py:387
  (1 shorter events, 0.0 us)
Async XLA Ops:
  0.6 14.4 %copy-start = (bf16[64,4096]{1,0:T(8,128)(2,1)S(1)}, bf16[64,4096]{1,0:T(8,128)(2,1)}, u32[]{:S(2)}) copy-start(bf16[64,4096]{1,0:T(8,128)(2,1)} %cache_ref.1) | copy-start | bytes 1572868
  0.6 9.1 %collective-permute-start = (bf16[64,256]{1,0:T(8,128)(2,1)}, bf16[64,256]{1,0:T(8,128)(2,1)S(1)}, u32[]{:S(2)}, u32[]{:S(2)}) collective-permute-start(bf16[64,256]{1,0:T(8,128)(2,1)} %feat_ref.3), channel_id=1, source_target_pairs={{0,8},{2,10},{4,12},{6,14},{8,0},{10,2},{12,4},{14,6},{16,24},{18,... | collective-permute-start | bytes 98312 | tf_op jit(solution)/shard_map/ppermute | solution.py:295
  3.7 6.0 %collective-permute-start.1 = (bf16[64,256]{1,0:T(8,128)(2,1)}, bf16[64,256]{1,0:T(8,128)(2,1)S(1)}, u32[]{:S(2)}, u32[]{:S(2)}) collective-permute-start(bf16[64,256]{1,0:T(8,128)(2,1)} %feat_ref.3), channel_id=1, source_target_pairs={{0,16},{2,18},{4,20},{6,22},{8,24},{10,26},{12,28},{14,30},{16,0},... | collective-permute-start | bytes 98312 | tf_op jit(solution)/shard_map/ppermute | solution.py:295
  6.3 5.9 %collective-permute-start.2 = (bf16[64,256]{1,0:T(8,128)(2,1)}, bf16[64,256]{1,0:T(8,128)(2,1)S(1)}, u32[]{:S(2)}, u32[]{:S(2)}) collective-permute-start(bf16[64,256]{1,0:T(8,128)(2,1)} %feat_ref.3), channel_id=1, source_target_pairs={{0,24},{2,26},{4,28},{6,30},{8,16},{10,18},{12,20},{14,22},{16,8},... | collective-permute-start | bytes 98312 | tf_op jit(solution)/shard_map/ppermute | solution.py:295
  7.9 15.4 %collective-permute-start.7 = (bf16[336,256]{1,0:T(8,128)(2,1)}, bf16[336,256]{1,0:T(8,128)(2,1)S(1)}, u32[]{:S(2)}, u32[]{:S(2)}) collective-permute-start(bf16[336,256]{1,0:T(8,128)(2,1)} %shard_map.140), channel_id=1, source_target_pairs={{0,1},{1,0},{2,3},{3,2},{4,5},{5,4},{6,7},{7,6},{8,9},{9,8},{10,11... | collective-permute-start | bytes 516104 | tf_op jit(solution)/shard_map/ppermute | solution.py:305
  12.2 0.8 %copy-start.1 = (bf16[64,256]{1,0:T(8,128)(2,1)S(1)}, bf16[64,256]{1,0:T(8,128)(2,1)}, u32[]{:S(2)}) copy-start(bf16[64,256]{1,0:T(8,128)(2,1)} %feat_ref.3) | copy-start | bytes 98308
  13.0 2.0 %copy-start.6 = (s32[16,256]{1,0:T(8,128)S(1)}, s32[16,256]{1,0:T(8,128)}, u32[]{:S(2)}) copy-start(s32[16,256]{1,0:T(8,128)} %nbr_ref.3) | copy-start | bytes 49156
  13.0 2.0 %copy-start.10 = (s32[16]{0:T(128)S(1)}, s32[16]{0:T(128)}, u32[]{:S(2)}) copy-start(s32[16]{0:T(128)} %counts_ref.1) | copy-start | bytes 196
  13.0 2.0 %copy-start.8 = (s32[256]{0:T(256)S(1)}, s32[256]{0:T(256)}, u32[]{:S(2)}) copy-start(s32[256]{0:T(256)} %param.15) | copy-start | bytes 3076
  13.0 2.0 %copy-start.9 = (s32[16]{0:T(128)S(1)}, s32[16]{0:T(128)}, u32[]{:S(2)}) copy-start(s32[16]{0:T(128)} %stale_ref.1) | copy-start | bytes 196
  13.0 7.1 %collective-permute-start.3 = (bf16[256,256]{1,0:T(8,128)(2,1)S(1)}, bf16[256,256]{1,0:T(8,128)(2,1)S(1)}, u32[]{:S(2)}, u32[]{:S(2)}) collective-permute-start(bf16[256,256]{1,0:T(8,128)(2,1)S(1)} %shard_map.138.refs_0_), channel_id=1, source_target_pairs={{0,2},{2,0},{4,6},{6,4},{8,10},{10,8},{12,14},{14,12},{16,18},{18,... | collective-permute-start | bytes 393224 | tf_op jit(solution)/shard_map/ppermute | solution.py:295
  13.1 7.1 %collective-permute-start.4 = (bf16[256,256]{1,0:T(8,128)(2,1)S(1)}, bf16[256,256]{1,0:T(8,128)(2,1)S(1)}, u32[]{:S(2)}, u32[]{:S(2)}) collective-permute-start(bf16[256,256]{1,0:T(8,128)(2,1)S(1)} %shard_map.138.refs_0_), channel_id=1, source_target_pairs={{0,4},{2,6},{4,0},{6,2},{8,12},{10,14},{12,8},{14,10},{16,20},{18,... | collective-permute-start | bytes 393224 | tf_op jit(solution)/shard_map/ppermute | solution.py:295
  14.7 6.7 %collective-permute-start.5 = (bf16[256,256]{1,0:T(8,128)(2,1)S(1)}, bf16[256,256]{1,0:T(8,128)(2,1)S(1)}, u32[]{:S(2)}, u32[]{:S(2)}) collective-permute-start(bf16[256,256]{1,0:T(8,128)(2,1)S(1)} %shard_map.138.refs_0_), channel_id=1, source_target_pairs={{0,6},{2,4},{4,2},{6,0},{8,14},{10,12},{12,10},{14,8},{16,22},{18,... | collective-permute-start | bytes 393224 | tf_op jit(solution)/shard_map/ppermute | solution.py:295
  21.4 4.3 %copy-start.2 = (bf16[64,256]{1,0:T(8,128)(2,1)S(1)}, bf16[64,256]{1,0:T(8,128)(2,1)}, u32[]{:S(2)}) copy-start(bf16[64,256]{1,0:T(8,128)(2,1)} %feat_ref.3) | copy-start | bytes 98308
  21.4 4.3 %copy-start.3 = (bf16[128,256]{1,0:T(8,128)(2,1)S(1)}, bf16[128,256]{1,0:T(8,128)(2,1)}, u32[]{:S(2)}) copy-start(bf16[128,256]{1,0:T(8,128)(2,1)} %cot_ref.3) | copy-start | bytes 196612
  21.4 4.3 %copy-start.4 = (bf16[64,256]{1,0:T(8,128)(2,1)S(1)}, bf16[64,256]{1,0:T(8,128)(2,1)}, u32[]{:S(2)}) copy-start(bf16[64,256]{1,0:T(8,128)(2,1)} %self_ref.3) | copy-start | bytes 98308
  21.4 4.3 %copy-start.5 = (bf16[64,256]{1,0:T(8,128)(2,1)S(1)}, bf16[64,256]{1,0:T(8,128)(2,1)}, u32[]{:S(2)}) copy-start(bf16[64,256]{1,0:T(8,128)(2,1)} %nbr_ref.5) | copy-start | bytes 98308
  21.4 4.3 %copy-start.7 = (f32[128]{0:T(128)S(1)}, f32[128]{0:T(128)}, u32[]{:S(2)}) copy-start(f32[128]{0:T(128)} %param.18) | copy-start | bytes 1540
  21.7 4.0 %collective-permute-start.6 = (bf16[64,256]{1,0:T(8,128)(2,1)S(1)}, bf16[64,256]{1,0:T(8,128)(2,1)S(1)}, u32[]{:S(2)}, u32[]{:S(2)}) collective-permute-start(bf16[64,256]{1,0:T(8,128)(2,1)S(1)} %shard_map.139.refs_0_), channel_id=1, source_target_pairs={{0,1},{1,0},{2,3},{3,2},{4,5},{5,4},{6,7},{7,6},{8,9},{9,8},{10,11... | collective-permute-start | bytes 98312 | tf_op jit(solution)/shard_map/ppermute | solution.py:305
  26.8 4.2 %collective-permute-start.10 = (bf16[112,256]{1,0:T(8,128)(2,1)S(1)}, bf16[112,256]{1,0:T(8,128)(2,1)S(1)}, u32[]{:S(2)}, u32[]{:S(2)}) collective-permute-start(bf16[112,256]{1,0:T(8,128)(2,1)S(1)} %get-tuple-element.35), channel_id=1, source_target_pairs={{0,6},{2,4},{4,2},{6,0},{8,14},{10,12},{12,10},{14,8},{16,22},{18,... | collective-permute-start | bytes 172040 | tf_op jit(solution)/shard_map/ppermute | solution.py:295
  27.1 3.9 %collective-permute-start.8 = (bf16[112,256]{1,0:T(8,128)(2,1)S(1)}, bf16[112,256]{1,0:T(8,128)(2,1)S(1)}, u32[]{:S(2)}, u32[]{:S(2)}) collective-permute-start(bf16[112,256]{1,0:T(8,128)(2,1)S(1)} %get-tuple-element.33), channel_id=1, source_target_pairs={{0,2},{2,0},{4,6},{6,4},{8,10},{10,8},{12,14},{14,12},{16,18},{18,... | collective-permute-start | bytes 172040 | tf_op jit(solution)/shard_map/ppermute | solution.py:295
  28.5 4.2 %collective-permute-start.9 = (bf16[112,256]{1,0:T(8,128)(2,1)S(1)}, bf16[112,256]{1,0:T(8,128)(2,1)S(1)}, u32[]{:S(2)}, u32[]{:S(2)}) collective-permute-start(bf16[112,256]{1,0:T(8,128)(2,1)S(1)} %get-tuple-element.34), channel_id=1, source_target_pairs={{0,4},{2,6},{4,0},{6,2},{8,12},{10,14},{12,8},{14,10},{16,20},{18,... | collective-permute-start | bytes 172040 | tf_op jit(solution)/shard_map/ppermute | solution.py:295
  32.8 4.5 %collective-permute-start.11 = (bf16[112,256]{1,0:T(8,128)(2,1)S(1)}, bf16[112,256]{1,0:T(8,128)(2,1)S(1)}, u32[]{:S(2)}, u32[]{:S(2)}) collective-permute-start(bf16[112,256]{1,0:T(8,128)(2,1)S(1)} %shard_map.142.refs_0_), channel_id=1, source_target_pairs={{0,8},{2,10},{4,12},{6,14},{8,0},{10,2},{12,4},{14,6},{16,24},{18,... | collective-permute-start | bytes 172040 | tf_op jit(solution)/shard_map/ppermute | solution.py:295
  32.9 5.6 %collective-permute-start.12 = (bf16[112,256]{1,0:T(8,128)(2,1)S(1)}, bf16[112,256]{1,0:T(8,128)(2,1)S(1)}, u32[]{:S(2)}, u32[]{:S(2)}) collective-permute-start(bf16[112,256]{1,0:T(8,128)(2,1)S(1)} %shard_map.142.refs_0_), channel_id=1, source_target_pairs={{0,16},{2,18},{4,20},{6,22},{8,24},{10,26},{12,28},{14,30},{16,0},... | collective-permute-start | bytes 172040 | tf_op jit(solution)/shard_map/ppermute | solution.py:295
  34.5 6.0 %collective-permute-start.13 = (bf16[112,256]{1,0:T(8,128)(2,1)S(1)}, bf16[112,256]{1,0:T(8,128)(2,1)S(1)}, u32[]{:S(2)}, u32[]{:S(2)}) collective-permute-start(bf16[112,256]{1,0:T(8,128)(2,1)S(1)} %shard_map.142.refs_0_), channel_id=1, source_target_pairs={{0,24},{2,26},{4,28},{6,30},{8,16},{10,18},{12,20},{14,22},{16,8},... | collective-permute-start | bytes 172040 | tf_op jit(solution)/shard_map/ppermute | solution.py:295
  40.6 1.9 %collective-permute-start.14 = (bf16[48,256]{1,0:T(8,128)(2,1)S(1)}, bf16[48,256]{1,0:T(8,128)(2,1)S(1)}, u32[]{:S(2)}, u32[]{:S(2)}) collective-permute-start(bf16[48,256]{1,0:T(8,128)(2,1)S(1)} %get-tuple-element.39), channel_id=1, source_target_pairs={{0,2},{2,0},{4,6},{6,4},{8,10},{10,8},{12,14},{14,12},{16,18},{18,... | collective-permute-start | bytes 73736 | tf_op jit(solution)/shard_map/ppermute | solution.py:295
  40.7 4.1 %collective-permute-start.15 = (bf16[48,256]{1,0:T(8,128)(2,1)S(1)}, bf16[48,256]{1,0:T(8,128)(2,1)S(1)}, u32[]{:S(2)}, u32[]{:S(2)}) collective-permute-start(bf16[48,256]{1,0:T(8,128)(2,1)S(1)} %get-tuple-element.40), channel_id=1, source_target_pairs={{0,4},{2,6},{4,0},{6,2},{8,12},{10,14},{12,8},{14,10},{16,20},{18,... | collective-permute-start | bytes 73736 | tf_op jit(solution)/shard_map/ppermute | solution.py:295
  41.3 3.5 %collective-permute-start.16 = (bf16[48,256]{1,0:T(8,128)(2,1)S(1)}, bf16[48,256]{1,0:T(8,128)(2,1)S(1)}, u32[]{:S(2)}, u32[]{:S(2)}) collective-permute-start(bf16[48,256]{1,0:T(8,128)(2,1)S(1)} %get-tuple-element.41), channel_id=1, source_target_pairs={{0,6},{2,4},{4,2},{6,0},{8,14},{10,12},{12,10},{14,8},{16,22},{18,... | collective-permute-start | bytes 73736 | tf_op jit(solution)/shard_map/ppermute | solution.py:295

commit v8 on v7

--- a/solution.py
+++ b/solution.py
@@ -295,7 +295,8 @@
         return lax.ppermute(block, "dom", [(i, i ^ m) for i in range(dom)])
 
     def along(block):
-        return [block] + [hop(block, m) for m in range(LOW, dom, LOW)]
+        far_first = [hop(block, m) for m in range(dom - LOW, 0, -LOW)]
+        return [block] + far_first[::-1]
 
     def within(slots):
         return [slots[0]] + [hop(slots[m], m) for m in range(1, LOW)]

time: 45.8 us -> 45.8 us (level)
  no operation moved by 1% of the time
where the time goes in v8:
time: 45.8 us; the launch traced here: 45.5 us
  starting transfers between devices  19.5 us (43%)
  waiting for transfers between devices  15.4 us (34%)
  Pallas kernels  9.03 us (20%)
  local copies, waits for them, and re-layouts  0.8 us (2%)
  between operations  0.79 us (2%)
    ppermute x15, starting transfers between devices, hop(): return lax.ppermute(block, 'dom', [(i, i ^ m) for i in range(dom)])  16.2 us
    ppermute x15, waiting for transfers between devices, hop(): return lax.ppermute(block, 'dom', [(i, i ^ m) for i in range(dom)])  13 us
    pallas_call x1, Pallas kernels, per_device(): call(count_body, (shape((listed * nodes, nodes), BF16), shape((width, nod...  5.14 us
    ppermute x2, starting transfers between devices, around(): lax.ppermute(block, 'col', [(i, (i + s) % n_col) for i in range(n_col)])  3.33 us
    ppermute x2, waiting for transfers between devices, around(): lax.ppermute(block, 'col', [(i, (i + s) % n_col) for i in range(n_col)])  2.42 us
    pallas_call x1, Pallas kernels, per_device(): call(pack_body, shape((3 * width + part_h + 16, nodes), BF16), 0, 0, [plt...  1.61 us
    pallas_call x1, Pallas kernels, per_device(): call(functools.partial(dense_body, n_col), [shape((part_h, nodes), BF16),...  1.07 us
  transfers between devices with their start and end apart: 17, of which 8 were waited for; matrix products, arithmetic and copies ran while one was open for 0% of the time, Pallas kernels for 16%

profile of v8, /device:TPU:0, one launch (start us, length us, event | category | flops | bytes accessed | tf_op | source)
XLA Modules:
  0.0 45.5 jit_solution(11959741322940824966)
XLA Ops:
  0.6 0.0 copy-start
  0.6 3.1 %collective-permute-start = (bf16[64,256]{1,0:T(8,128)(2,1)}, bf16[64,256]{1,0:T(8,128)(2,1)S(1)}, u32[]{:S(2)}, u32[]{:S(2)}) collective-permute-start(bf16[64,256]{1,0:T(8,128)(2,1)} %feat_ref.3), channel_id=1, source_target_pairs={{0,8},{2,10},{4,12},{6,14},{8,0},{10,2},{12,4},{14,6},{16,24},{18,... | collective-permute-start | bytes 98312 | tf_op jit(solution)/shard_map/ppermute | solution.py:295
  3.7 2.6 %collective-permute-start.1 = (bf16[64,256]{1,0:T(8,128)(2,1)}, bf16[64,256]{1,0:T(8,128)(2,1)S(1)}, u32[]{:S(2)}, u32[]{:S(2)}) collective-permute-start(bf16[64,256]{1,0:T(8,128)(2,1)} %feat_ref.3), channel_id=1, source_target_pairs={{0,16},{2,18},{4,20},{6,22},{8,24},{10,26},{12,28},{14,30},{16,0},... | collective-permute-start | bytes 98312 | tf_op jit(solution)/shard_map/ppermute | solution.py:295
  6.3 0.0 collective-permute-start.2
  6.3 1.6 %shard_map.140 = bf16[336,256]{1,0:T(8,128)(2,1)} custom-call(bf16[64,256]{1,0:T(8,128)(2,1)} %feat_ref.3, bf16[64,256]{1,0:T(8,128)(2,1)} %self_ref.3, bf16[64,256]{1,0:T(8,128)(2,1)} %nbr_ref.5, bf16[128,256]{1,0:T(8,128)(2,1)} %cot_ref.3, f32[1,128]{1,0:T(1,128)} %bitcast.3), custom_call_target="tpu_custom_call" | custom-call | bytes 327680 | tf_op jit(solution)/shard_map/pallas_call | solution.py:312
  7.9 1.8 %collective-permute-start.7 = (bf16[336,256]{1,0:T(8,128)(2,1)}, bf16[336,256]{1,0:T(8,128)(2,1)S(1)}, u32[]{:S(2)}, u32[]{:S(2)}) collective-permute-start(bf16[336,256]{1,0:T(8,128)(2,1)} %shard_map.140), channel_id=1, source_target_pairs={{0,1},{1,0},{2,3},{3,2},{4,5},{5,4},{6,7},{7,6},{8,9},{9,8},{10,11... | collective-permute-start | bytes 516104 | tf_op jit(solution)/shard_map/ppermute | solution.py:306
  9.7 0.0 collective-permute-done.refs_1_
  9.7 0.0 collective-permute-done.1.refs_2_
  9.7 2.5 %collective-permute-done.2.refs_3_ = bf16[64,256]{1,0:T(8,128)(2,1)S(1)} collective-permute-done((bf16[64,256]{1,0:T(8,128)(2,1)}, bf16[64,256]{1,0:T(8,128)(2,1)S(1)}, u32[]{:S(2)}, u32[]{:S(2)}) %collective-permute-start.2) | collective-permute-done | bytes 32800 | tf_op jit(solution)/shard_map/ppermute | solution.py:295
  12.2 0.0 copy-start.1
  12.2 0.8 %copy-done.1 = bf16[64,256]{1,0:T(8,128)(2,1)S(1)} copy-done((bf16[64,256]{1,0:T(8,128)(2,1)S(1)}, bf16[64,256]{1,0:T(8,128)(2,1)}, u32[]{:S(2)}) %copy-start.1) | copy-done | bytes 32792
  13.0 0.0 copy-start.6
  13.0 0.0 copy-start.10
  13.0 0.0 copy-start.8
  13.0 0.0 copy-start.9
  13.0 0.1 collective-permute-start.3
  13.1 1.6 %collective-permute-start.4 = (bf16[256,256]{1,0:T(8,128)(2,1)S(1)}, bf16[256,256]{1,0:T(8,128)(2,1)S(1)}, u32[]{:S(2)}, u32[]{:S(2)}) collective-permute-start(bf16[256,256]{1,0:T(8,128)(2,1)S(1)} %shard_map.138.refs_0_), channel_id=1, source_target_pairs={{0,4},{2,6},{4,0},{6,2},{8,12},{10,14},{12,8},{14,10},{16,20},{18,... | collective-permute-start | bytes 393224 | tf_op jit(solution)/shard_map/ppermute | solution.py:295
  14.7 0.3 collective-permute-start.5
  15.0 0.0 copy-done
  15.0 0.0 copy-done.6
  15.0 0.0 copy-done.10
  15.0 0.0 copy-done.8
  15.0 0.0 copy-done.9
  15.0 5.1 %shard_map.137 = (bf16[1024,256]{1,0:T(8,128)(2,1)S(1)}, f32[64,256]{1,0:T(8,128)S(1)}, f32[24,256]{1,0:T(8,128)S(1)}, f32[16,256]{1,0:T(8,128)S(1)}, f32[64,256]{1,0:T(8,128)S(1)}) custom-call(s32[16]{0:T(128)S(1)} %copy-done.9, s32[16]{0:T(128)S(1)} %copy-done.10, s32[16,256]{1,0:T(8,128)S(1)} %copy-done.6, s32[1,256]{1,0:T(1,128)S(1)} %bitcast.5, ...), custom_call_target="tpu_custom_call" | custom-call | flops 134217728 | bytes 16777216 | tf_op jit(solution)/shard_map/pallas_call | solution.py:327
  20.2 0.0 collective-permute-done.3.refs_1_
  20.2 0.0 collective-permute-done.4.refs_2_
  20.2 1.2 %collective-permute-done.5.refs_3_ = bf16[256,256]{1,0:T(8,128)(2,1)S(1)} collective-permute-done((bf16[256,256]{1,0:T(8,128)(2,1)S(1)}, bf16[256,256]{1,0:T(8,128)(2,1)S(1)}, u32[]{:S(2)}, u32[]{:S(2)}) %collective-permute-start.5) | collective-permute-done | bytes 131104 | tf_op jit(solution)/shard_map/ppermute | solution.py:295
  21.4 0.0 copy-start.2
  21.4 0.0 copy-start.3
  21.4 0.0 copy-start.4
  21.4 0.0 copy-start.5
  21.4 0.0 copy-start.7
  21.4 0.3 shard_map.139.refs_0_
  21.7 1.6 %collective-permute-start.6 = (bf16[64,256]{1,0:T(8,128)(2,1)S(1)}, bf16[64,256]{1,0:T(8,128)(2,1)S(1)}, u32[]{:S(2)}, u32[]{:S(2)}) collective-permute-start(bf16[64,256]{1,0:T(8,128)(2,1)S(1)} %shard_map.139.refs_0_), channel_id=1, source_target_pairs={{0,1},{1,0},{2,3},{3,2},{4,5},{5,4},{6,7},{7,6},{8,9},{9,8},{10,11... | collective-permute-start | bytes 98312 | tf_op jit(solution)/shard_map/ppermute | solution.py:306
  23.3 0.0 collective-permute-done.7.refs_2_
  23.3 2.4 %collective-permute-done.6.refs_1_ = bf16[64,256]{1,0:T(8,128)(2,1)S(1)} collective-permute-done((bf16[64,256]{1,0:T(8,128)(2,1)S(1)}, bf16[64,256]{1,0:T(8,128)(2,1)S(1)}, u32[]{:S(2)}, u32[]{:S(2)}) %collective-permute-start.6) | collective-permute-done | bytes 32800 | tf_op jit(solution)/shard_map/ppermute | solution.py:306
  25.7 0.0 copy-done.2
  25.7 0.0 copy-done.3
  25.7 0.0 copy-done.4
  25.7 0.0 copy-done.5
  25.7 0.0 copy-done.7
  25.7 1.1 %shard_map.141 = (bf16[128,256]{1,0:T(8,128)(2,1)S(1)}, f32[64,256]{1,0:T(8,128)S(1)}, bf16[112,256]{1,0:T(8,128)(2,1)S(1)}, bf16[112,256]{1,0:T(8,128)(2,1)S(1)...) custom-call(f32[24,256]{1,0:T(8,128)S(1)} %get-tuple-element.26.scale_ref, ...), custom_call_target="tpu_custom_call" | custom-call | flops 83886080 | bytes 458752 | tf_op jit(solution)/shard_map/pallas_call | solution.py:352
  26.8 0.3 collective-permute-start.10
  27.1 1.4 %collective-permute-start.8 = (bf16[112,256]{1,0:T(8,128)(2,1)S(1)}, bf16[112,256]{1,0:T(8,128)(2,1)S(1)}, u32[]{:S(2)}, u32[]{:S(2)}) collective-permute-start(bf16[112,256]{1,0:T(8,128)(2,1)S(1)} %get-tuple-element.33), channel_id=1, source_target_pairs={{0,2},{2,0},{4,6},{6,4},{8,10},{10,8},{12,14},{14,12},{16,18},{18,... | collective-permute-start | bytes 172040 | tf_op jit(solution)/shard_map/ppermute | solution.py:295
  28.5 0.5 %collective-permute-start.9 = (bf16[112,256]{1,0:T(8,128)(2,1)S(1)}, bf16[112,256]{1,0:T(8,128)(2,1)S(1)}, u32[]{:S(2)}, u32[]{:S(2)}) collective-permute-start(bf16[112,256]{1,0:T(8,128)(2,1)S(1)} %get-tuple-element.34), channel_id=1, source_target_pairs={{0,4},{2,6},{4,0},{6,2},{8,12},{10,14},{12,8},{14,10},{16,20},{18,... | collective-permute-start | bytes 172040 | tf_op jit(solution)/shard_map/ppermute | solution.py:295
  29.0 2.0 %collective-permute-done.10.refs_3_ = bf16[112,256]{1,0:T(8,128)(2,1)S(1)} collective-permute-done((bf16[112,256]{1,0:T(8,128)(2,1)S(1)}, bf16[112,256]{1,0:T(8,128)(2,1)S(1)}, u32[]{:S(2)}, u32[]{:S(2)}) %collective-permute-start.10) | collective-permute-done | bytes 57376 | tf_op jit(solution)/shard_map/ppermute | solution.py:295
  31.0 0.0 collective-permute-done.8.refs_1_
  31.0 1.7 %collective-permute-done.9.refs_2_ = bf16[112,256]{1,0:T(8,128)(2,1)S(1)} collective-permute-done((bf16[112,256]{1,0:T(8,128)(2,1)S(1)}, bf16[112,256]{1,0:T(8,128)(2,1)S(1)}, u32[]{:S(2)}, u32[]{:S(2)}) %collective-permute-start.9) | collective-permute-done | bytes 57376 | tf_op jit(solution)/shard_map/ppermute | solution.py:295
  32.7 0.1 shard_map.142.refs_0_
  32.8 0.1 collective-permute-start.11
  32.9 1.6 %collective-permute-start.12 = (bf16[112,256]{1,0:T(8,128)(2,1)S(1)}, bf16[112,256]{1,0:T(8,128)(2,1)S(1)}, u32[]{:S(2)}, u32[]{:S(2)}) collective-permute-start(bf16[112,256]{1,0:T(8,128)(2,1)S(1)} %shard_map.142.refs_0_), channel_id=1, source_target_pairs={{0,16},{2,18},{4,20},{6,22},{8,24},{10,26},{12,28},{14,30},{16,0},... | collective-permute-start | bytes 172040 | tf_op jit(solution)/shard_map/ppermute | solution.py:295
  34.5 2.7 %collective-permute-start.13 = (bf16[112,256]{1,0:T(8,128)(2,1)S(1)}, bf16[112,256]{1,0:T(8,128)(2,1)S(1)}, u32[]{:S(2)}, u32[]{:S(2)}) collective-permute-start(bf16[112,256]{1,0:T(8,128)(2,1)S(1)} %shard_map.142.refs_0_), channel_id=1, source_target_pairs={{0,24},{2,26},{4,28},{6,30},{8,16},{10,18},{12,20},{14,22},{16,8},... | collective-permute-start | bytes 172040 | tf_op jit(solution)/shard_map/ppermute | solution.py:295
  37.2 0.0 collective-permute-done.11.refs_1_
  37.2 1.2 %collective-permute-done.12.refs_2_ = bf16[112,256]{1,0:T(8,128)(2,1)S(1)} collective-permute-done((bf16[112,256]{1,0:T(8,128)(2,1)S(1)}, bf16[112,256]{1,0:T(8,128)(2,1)S(1)}, u32[]{:S(2)}, u32[]{:S(2)}) %collective-permute-start.12) | collective-permute-done | bytes 57376 | tf_op jit(solution)/shard_map/ppermute | solution.py:295
  38.4 2.1 %collective-permute-done.13.refs_3_ = bf16[112,256]{1,0:T(8,128)(2,1)S(1)} collective-permute-done((bf16[112,256]{1,0:T(8,128)(2,1)S(1)}, bf16[112,256]{1,0:T(8,128)(2,1)S(1)}, u32[]{:S(2)}, u32[]{:S(2)}) %collective-permute-start.13) | collective-permute-done | bytes 57376 | tf_op jit(solution)/shard_map/ppermute | solution.py:295
  40.5 0.1 shard_map.143
  40.6 0.1 collective-permute-start.14
  40.7 0.7 %collective-permute-start.15 = (bf16[48,256]{1,0:T(8,128)(2,1)S(1)}, bf16[48,256]{1,0:T(8,128)(2,1)S(1)}, u32[]{:S(2)}, u32[]{:S(2)}) collective-permute-start(bf16[48,256]{1,0:T(8,128)(2,1)S(1)} %get-tuple-element.40), channel_id=1, source_target_pairs={{0,4},{2,6},{4,0},{6,2},{8,12},{10,14},{12,8},{14,10},{16,20},{18,... | collective-permute-start | bytes 73736 | tf_op jit(solution)/shard_map/ppermute | solution.py:295
  41.3 1.2 %collective-permute-start.16 = (bf16[48,256]{1,0:T(8,128)(2,1)S(1)}, bf16[48,256]{1,0:T(8,128)(2,1)S(1)}, u32[]{:S(2)}, u32[]{:S(2)}) collective-permute-start(bf16[48,256]{1,0:T(8,128)(2,1)S(1)} %get-tuple-element.41), channel_id=1, source_target_pairs={{0,6},{2,4},{4,2},{6,0},{8,14},{10,12},{12,10},{14,8},{16,22},{18,... | collective-permute-start | bytes 73736 | tf_op jit(solution)/shard_map/ppermute | solution.py:295
  42.5 0.0 collective-permute-done.14.refs_1_
  42.5 2.3 %collective-permute-done.15.refs_2_ = bf16[48,256]{1,0:T(8,128)(2,1)S(1)} collective-permute-done((bf16[48,256]{1,0:T(8,128)(2,1)S(1)}, bf16[48,256]{1,0:T(8,128)(2,1)S(1)}, u32[]{:S(2)}, u32[]{:S(2)}) %collective-permute-start.15) | collective-permute-done | bytes 24608 | tf_op jit(solution)/shard_map/ppermute | solution.py:295
  44.8 0.0 collective-permute-done.16.refs_3_
  44.8 0.7 %shard_map.144 = (bf16[128,256]{1,0:T(8,128)(2,1)}, bf16[64,256]{1,0:T(8,128)(2,1)}, f32[64,256]{1,0:T(8,128)}, f32[64,256]{1,0:T(8,128)}, f32[1,128]{1,0:T(1,128)}) custom-call(f32[24,256]{1,0:T(8,128)S(1)} %get-tuple-element.26.scale_ref, bf16[128,256]{1,0:T(8,128)(2,1)S(1)} %get-tuple-element.30.act_ref, f32[8,256]{1,0:T(8,128)S(1)} %get-tuple-element.36.bias_ref, ...), custom_call_target="tpu_custom_call" | custom-call | bytes 98304 | tf_op jit(solution)/shard_map/pallas_call | solution.py:388
  (1 shorter events, 0.0 us)
Async XLA Ops:
  0.6 14.4 %copy-start = (bf16[64,4096]{1,0:T(8,128)(2,1)S(1)}, bf16[64,4096]{1,0:T(8,128)(2,1)}, u32[]{:S(2)}) copy-start(bf16[64,4096]{1,0:T(8,128)(2,1)} %cache_ref.1) | copy-start | bytes 1572868
  0.6 9.1 %collective-permute-start = (bf16[64,256]{1,0:T(8,128)(2,1)}, bf16[64,256]{1,0:T(8,128)(2,1)S(1)}, u32[]{:S(2)}, u32[]{:S(2)}) collective-permute-start(bf16[64,256]{1,0:T(8,128)(2,1)} %feat_ref.3), channel_id=1, source_target_pairs={{0,8},{2,10},{4,12},{6,14},{8,0},{10,2},{12,4},{14,6},{16,24},{18,... | collective-permute-start | bytes 98312 | tf_op jit(solution)/shard_map/ppermute | solution.py:295
  3.7 6.0 %collective-permute-start.1 = (bf16[64,256]{1,0:T(8,128)(2,1)}, bf16[64,256]{1,0:T(8,128)(2,1)S(1)}, u32[]{:S(2)}, u32[]{:S(2)}) collective-permute-start(bf16[64,256]{1,0:T(8,128)(2,1)} %feat_ref.3), channel_id=1, source_target_pairs={{0,16},{2,18},{4,20},{6,22},{8,24},{10,26},{12,28},{14,30},{16,0},... | collective-permute-start | bytes 98312 | tf_op jit(solution)/shard_map/ppermute | solution.py:295
  6.3 5.9 %collective-permute-start.2 = (bf16[64,256]{1,0:T(8,128)(2,1)}, bf16[64,256]{1,0:T(8,128)(2,1)S(1)}, u32[]{:S(2)}, u32[]{:S(2)}) collective-permute-start(bf16[64,256]{1,0:T(8,128)(2,1)} %feat_ref.3), channel_id=1, source_target_pairs={{0,24},{2,26},{4,28},{6,30},{8,16},{10,18},{12,20},{14,22},{16,8},... | collective-permute-start | bytes 98312 | tf_op jit(solution)/shard_map/ppermute | solution.py:295
  7.9 15.4 %collective-permute-start.7 = (bf16[336,256]{1,0:T(8,128)(2,1)}, bf16[336,256]{1,0:T(8,128)(2,1)S(1)}, u32[]{:S(2)}, u32[]{:S(2)}) collective-permute-start(bf16[336,256]{1,0:T(8,128)(2,1)} %shard_map.140), channel_id=1, source_target_pairs={{0,1},{1,0},{2,3},{3,2},{4,5},{5,4},{6,7},{7,6},{8,9},{9,8},{10,11... | collective-permute-start | bytes 516104 | tf_op jit(solution)/shard_map/ppermute | solution.py:306
  12.2 0.8 %copy-start.1 = (bf16[64,256]{1,0:T(8,128)(2,1)S(1)}, bf16[64,256]{1,0:T(8,128)(2,1)}, u32[]{:S(2)}) copy-start(bf16[64,256]{1,0:T(8,128)(2,1)} %feat_ref.3) | copy-start | bytes 98308
  13.0 2.0 %copy-start.6 = (s32[16,256]{1,0:T(8,128)S(1)}, s32[16,256]{1,0:T(8,128)}, u32[]{:S(2)}) copy-start(s32[16,256]{1,0:T(8,128)} %nbr_ref.3) | copy-start | bytes 49156
  13.0 2.0 %copy-start.10 = (s32[16]{0:T(128)S(1)}, s32[16]{0:T(128)}, u32[]{:S(2)}) copy-start(s32[16]{0:T(128)} %counts_ref.1) | copy-start | bytes 196
  13.0 2.0 %copy-start.8 = (s32[256]{0:T(256)S(1)}, s32[256]{0:T(256)}, u32[]{:S(2)}) copy-start(s32[256]{0:T(256)} %param.15) | copy-start | bytes 3076
  13.0 2.0 %copy-start.9 = (s32[16]{0:T(128)S(1)}, s32[16]{0:T(128)}, u32[]{:S(2)}) copy-start(s32[16]{0:T(128)} %stale_ref.1) | copy-start | bytes 196
  13.0 7.1 %collective-permute-start.3 = (bf16[256,256]{1,0:T(8,128)(2,1)S(1)}, bf16[256,256]{1,0:T(8,128)(2,1)S(1)}, u32[]{:S(2)}, u32[]{:S(2)}) collective-permute-start(bf16[256,256]{1,0:T(8,128)(2,1)S(1)} %shard_map.138.refs_0_), channel_id=1, source_target_pairs={{0,2},{2,0},{4,6},{6,4},{8,10},{10,8},{12,14},{14,12},{16,18},{18,... | collective-permute-start | bytes 393224 | tf_op jit(solution)/shard_map/ppermute | solution.py:295
  13.1 7.1 %collective-permute-start.4 = (bf16[256,256]{1,0:T(8,128)(2,1)S(1)}, bf16[256,256]{1,0:T(8,128)(2,1)S(1)}, u32[]{:S(2)}, u32[]{:S(2)}) collective-permute-start(bf16[256,256]{1,0:T(8,128)(2,1)S(1)} %shard_map.138.refs_0_), channel_id=1, source_target_pairs={{0,4},{2,6},{4,0},{6,2},{8,12},{10,14},{12,8},{14,10},{16,20},{18,... | collective-permute-start | bytes 393224 | tf_op jit(solution)/shard_map/ppermute | solution.py:295
  14.7 6.7 %collective-permute-start.5 = (bf16[256,256]{1,0:T(8,128)(2,1)S(1)}, bf16[256,256]{1,0:T(8,128)(2,1)S(1)}, u32[]{:S(2)}, u32[]{:S(2)}) collective-permute-start(bf16[256,256]{1,0:T(8,128)(2,1)S(1)} %shard_map.138.refs_0_), channel_id=1, source_target_pairs={{0,6},{2,4},{4,2},{6,0},{8,14},{10,12},{12,10},{14,8},{16,22},{18,... | collective-permute-start | bytes 393224 | tf_op jit(solution)/shard_map/ppermute | solution.py:295
  21.4 4.3 %copy-start.2 = (bf16[64,256]{1,0:T(8,128)(2,1)S(1)}, bf16[64,256]{1,0:T(8,128)(2,1)}, u32[]{:S(2)}) copy-start(bf16[64,256]{1,0:T(8,128)(2,1)} %feat_ref.3) | copy-start | bytes 98308
  21.4 4.3 %copy-start.3 = (bf16[128,256]{1,0:T(8,128)(2,1)S(1)}, bf16[128,256]{1,0:T(8,128)(2,1)}, u32[]{:S(2)}) copy-start(bf16[128,256]{1,0:T(8,128)(2,1)} %cot_ref.3) | copy-start | bytes 196612
  21.4 4.3 %copy-start.4 = (bf16[64,256]{1,0:T(8,128)(2,1)S(1)}, bf16[64,256]{1,0:T(8,128)(2,1)}, u32[]{:S(2)}) copy-start(bf16[64,256]{1,0:T(8,128)(2,1)} %self_ref.3) | copy-start | bytes 98308
  21.4 4.3 %copy-start.5 = (bf16[64,256]{1,0:T(8,128)(2,1)S(1)}, bf16[64,256]{1,0:T(8,128)(2,1)}, u32[]{:S(2)}) copy-start(bf16[64,256]{1,0:T(8,128)(2,1)} %nbr_ref.5) | copy-start | bytes 98308
  21.4 4.3 %copy-start.7 = (f32[128]{0:T(128)S(1)}, f32[128]{0:T(128)}, u32[]{:S(2)}) copy-start(f32[128]{0:T(128)} %param.18) | copy-start | bytes 1540
  21.7 4.0 %collective-permute-start.6 = (bf16[64,256]{1,0:T(8,128)(2,1)S(1)}, bf16[64,256]{1,0:T(8,128)(2,1)S(1)}, u32[]{:S(2)}, u32[]{:S(2)}) collective-permute-start(bf16[64,256]{1,0:T(8,128)(2,1)S(1)} %shard_map.139.refs_0_), channel_id=1, source_target_pairs={{0,1},{1,0},{2,3},{3,2},{4,5},{5,4},{6,7},{7,6},{8,9},{9,8},{10,11... | collective-permute-start | bytes 98312 | tf_op jit(solution)/shard_map/ppermute | solution.py:306
  26.8 4.2 %collective-permute-start.10 = (bf16[112,256]{1,0:T(8,128)(2,1)S(1)}, bf16[112,256]{1,0:T(8,128)(2,1)S(1)}, u32[]{:S(2)}, u32[]{:S(2)}) collective-permute-start(bf16[112,256]{1,0:T(8,128)(2,1)S(1)} %get-tuple-element.35), channel_id=1, source_target_pairs={{0,6},{2,4},{4,2},{6,0},{8,14},{10,12},{12,10},{14,8},{16,22},{18,... | collective-permute-start | bytes 172040 | tf_op jit(solution)/shard_map/ppermute | solution.py:295
  27.1 3.9 %collective-permute-start.8 = (bf16[112,256]{1,0:T(8,128)(2,1)S(1)}, bf16[112,256]{1,0:T(8,128)(2,1)S(1)}, u32[]{:S(2)}, u32[]{:S(2)}) collective-permute-start(bf16[112,256]{1,0:T(8,128)(2,1)S(1)} %get-tuple-element.33), channel_id=1, source_target_pairs={{0,2},{2,0},{4,6},{6,4},{8,10},{10,8},{12,14},{14,12},{16,18},{18,... | collective-permute-start | bytes 172040 | tf_op jit(solution)/shard_map/ppermute | solution.py:295
  28.5 4.2 %collective-permute-start.9 = (bf16[112,256]{1,0:T(8,128)(2,1)S(1)}, bf16[112,256]{1,0:T(8,128)(2,1)S(1)}, u32[]{:S(2)}, u32[]{:S(2)}) collective-permute-start(bf16[112,256]{1,0:T(8,128)(2,1)S(1)} %get-tuple-element.34), channel_id=1, source_target_pairs={{0,4},{2,6},{4,0},{6,2},{8,12},{10,14},{12,8},{14,10},{16,20},{18,... | collective-permute-start | bytes 172040 | tf_op jit(solution)/shard_map/ppermute | solution.py:295
  32.8 4.5 %collective-permute-start.11 = (bf16[112,256]{1,0:T(8,128)(2,1)S(1)}, bf16[112,256]{1,0:T(8,128)(2,1)S(1)}, u32[]{:S(2)}, u32[]{:S(2)}) collective-permute-start(bf16[112,256]{1,0:T(8,128)(2,1)S(1)} %shard_map.142.refs_0_), channel_id=1, source_target_pairs={{0,8},{2,10},{4,12},{6,14},{8,0},{10,2},{12,4},{14,6},{16,24},{18,... | collective-permute-start | bytes 172040 | tf_op jit(solution)/shard_map/ppermute | solution.py:295
  32.9 5.6 %collective-permute-start.12 = (bf16[112,256]{1,0:T(8,128)(2,1)S(1)}, bf16[112,256]{1,0:T(8,128)(2,1)S(1)}, u32[]{:S(2)}, u32[]{:S(2)}) collective-permute-start(bf16[112,256]{1,0:T(8,128)(2,1)S(1)} %shard_map.142.refs_0_), channel_id=1, source_target_pairs={{0,16},{2,18},{4,20},{6,22},{8,24},{10,26},{12,28},{14,30},{16,0},... | collective-permute-start | bytes 172040 | tf_op jit(solution)/shard_map/ppermute | solution.py:295
  34.5 6.0 %collective-permute-start.13 = (bf16[112,256]{1,0:T(8,128)(2,1)S(1)}, bf16[112,256]{1,0:T(8,128)(2,1)S(1)}, u32[]{:S(2)}, u32[]{:S(2)}) collective-permute-start(bf16[112,256]{1,0:T(8,128)(2,1)S(1)} %shard_map.142.refs_0_), channel_id=1, source_target_pairs={{0,24},{2,26},{4,28},{6,30},{8,16},{10,18},{12,20},{14,22},{16,8},... | collective-permute-start | bytes 172040 | tf_op jit(solution)/shard_map/ppermute | solution.py:295
  40.6 1.9 %collective-permute-start.14 = (bf16[48,256]{1,0:T(8,128)(2,1)S(1)}, bf16[48,256]{1,0:T(8,128)(2,1)S(1)}, u32[]{:S(2)}, u32[]{:S(2)}) collective-permute-start(bf16[48,256]{1,0:T(8,128)(2,1)S(1)} %get-tuple-element.39), channel_id=1, source_target_pairs={{0,2},{2,0},{4,6},{6,4},{8,10},{10,8},{12,14},{14,12},{16,18},{18,... | collective-permute-start | bytes 73736 | tf_op jit(solution)/shard_map/ppermute | solution.py:295
  40.7 4.1 %collective-permute-start.15 = (bf16[48,256]{1,0:T(8,128)(2,1)S(1)}, bf16[48,256]{1,0:T(8,128)(2,1)S(1)}, u32[]{:S(2)}, u32[]{:S(2)}) collective-permute-start(bf16[48,256]{1,0:T(8,128)(2,1)S(1)} %get-tuple-element.40), channel_id=1, source_target_pairs={{0,4},{2,6},{4,0},{6,2},{8,12},{10,14},{12,8},{14,10},{16,20},{18,... | collective-permute-start | bytes 73736 | tf_op jit(solution)/shard_map/ppermute | solution.py:295
  41.3 3.5 %collective-permute-start.16 = (bf16[48,256]{1,0:T(8,128)(2,1)S(1)}, bf16[48,256]{1,0:T(8,128)(2,1)S(1)}, u32[]{:S(2)}, u32[]{:S(2)}) collective-permute-start(bf16[48,256]{1,0:T(8,128)(2,1)S(1)} %get-tuple-element.41), channel_id=1, source_target_pairs={{0,6},{2,4},{4,2},{6,0},{8,14},{10,12},{12,10},{14,8},{16,22},{18,... | collective-permute-start | bytes 73736 | tf_op jit(solution)/shard_map/ppermute | solution.py:295
